TPU v7x, 768 devices: a whole 4x8x12 slice. The times are simulated.
768 devices in a mesh: gx: 12 (over z), gy: 16 (over y, core), gz: 4 (over x).
Axes of the slice: x: 4, y: 8, z: 12, core: 2. Of those that a mesh axis runs over, the one named last changes fastest.
Arguments:
- solution: float32 [3, 96, 256, 512], P(None, 'gx', 'gy', 'gz'), may hold values from -6 to 6
- residual: float32 [3, 96, 256, 512], P(None, 'gx', 'gy', 'gz'), may hold values from -15 to 15
- density_bins: int32 [96, 256, 512], P('gx', 'gy', 'gz'), may hold values from 0 to 15
- fixed_dofs: int32 [3, 96, 256, 512], P(None, 'gx', 'gy', 'gz'), may hold values from 0 to 1
Outputs:
- solution_next: float32 [3, 96, 256, 512], P(None, 'gx', 'gy', 'gz')
- residual_next: float32 [3, 96, 256, 512], P(None, 'gx', 'gy', 'gz')
- direction: float32 [3, 96, 256, 512], P(None, 'gx', 'gy', 'gz')
All inputs are finite; a program needn't handle non-finite values.
Results may differ from a plain program's by a relative error of at most 0.0003.
Values sent between devices are 32-bit elements; how exact they have to be, the bound alone decides.
No kernel may reach another device: no remote copies, remote signals or barrier semaphores. Data moves between devices by JAX's collectives and lax.ppermute only.
A program may use at most 64 MiB of HBM per device.

v0:
```python
import jax
import jax.numpy as jnp
from jax import lax
from jax.sharding import PartitionSpec as P

SWEEPS = 3
BINS = 16


damping = 0.6
eig_center = 1.05
eig_halfwidth = 0.95


def padded_2(cells, sides, width):
    for axis, dim in sides:
        count = lax.axis_size(axis)
        ends = count - 1
        head = lax.slice_in_dim(cells, 0, width, axis=dim)
        tail = lax.slice_in_dim(cells, cells.shape[dim] - width, cells.shape[dim], axis=dim)
        cells = jnp.concatenate(
            [
                lax.ppermute(tail, axis, [(i, (i + 1) % count) for i in range(ends)]),
                cells,
                lax.ppermute(head, axis, [((i + 1) % count, i) for i in range(ends)]),
            ],
            axis=dim,
        )
    return cells


def stiffness(density_bins):
    fraction = (density_bins.astype(jnp.float32) + 1.0) / BINS
    return 0.05 + 0.95 * fraction * fraction * fraction


def couplings(padded):
    center = padded[1:-1, 1:-1, 1:-1]

    def shared(other):
        return jnp.where(other > 0.0, 0.5 * (center + other), 0.0)

    upper = jnp.stack(
        [
            shared(padded[2:, 1:-1, 1:-1]),
            shared(padded[1:-1, 2:, 1:-1]),
            shared(padded[1:-1, 1:-1, 2:]),
        ]
    )
    lower = jnp.stack(
        [
            shared(padded[:-2, 1:-1, 1:-1]),
            shared(padded[1:-1, :-2, 1:-1]),
            shared(padded[1:-1, 1:-1, :-2]),
        ]
    )
    return (upper, lower)


def level_apply(field, padded, upper, lower, spring):
    total = spring * field
    total = (
        total
        + upper[0] * (field - padded[:, 2:, 1:-1, 1:-1])
        + lower[0] * (field - padded[:, :-2, 1:-1, 1:-1])
    )
    total = (
        total
        + upper[1] * (field - padded[:, 1:-1, 2:, 1:-1])
        + lower[1] * (field - padded[:, 1:-1, :-2, 1:-1])
    )
    total = (
        total
        + upper[2] * (field - padded[:, 1:-1, 1:-1, 2:])
        + lower[2] * (field - padded[:, 1:-1, 1:-1, :-2])
    )
    return total


def level_diagonal(upper, lower, spring):
    return jnp.sum(upper, axis=0) + jnp.sum(lower, axis=0) + spring


def restrict(field):
    channels, size_x, size_y, size_z = field.shape
    return field.reshape(channels, size_x // 2, 2, size_y // 2, 2, size_z // 2, 2).sum(
        axis=(2, 4, 6)
    )


def prolong(field):
    return jnp.repeat(jnp.repeat(jnp.repeat(field, 2, axis=1), 2, axis=2), 2, axis=3)


def coarse_links(links, offset):
    size_x, size_y, size_z = links.shape[1:]
    along_x = (
        links[0][offset::2].reshape(size_x // 2, size_y // 2, 2, size_z // 2, 2).sum(axis=(2, 4))
    )
    along_y = (
        links[1][:, offset::2].reshape(size_x // 2, 2, size_y // 2, size_z // 2, 2).sum(axis=(1, 4))
    )
    along_z = (
        links[2][:, :, offset::2]
        .reshape(size_x // 2, 2, size_y // 2, 2, size_z // 2)
        .sum(axis=(1, 3))
    )
    return jnp.stack([along_x, along_y, along_z])


def with_rim(field):
    return padded_2(field, (("gx", 1), ("gy", 2), ("gz", 3)), 1)


def chebyshev(rhs, upper, lower, spring, diagonal, padder):
    ratio = eig_center / eig_halfwidth
    factor = 1.0 / ratio
    update = rhs / (eig_center * diagonal)
    iterate = update
    for step_index in range(SWEEPS - 1):
        remainder = rhs - level_apply(iterate, padder(iterate), upper, lower, spring)
        next_factor = 1.0 / (2.0 * ratio - factor)
        update = (
            next_factor * factor * update + 2.0 * next_factor / eig_halfwidth * remainder / diagonal
        )
        iterate = iterate + update
        factor = next_factor
    return iterate


def shards(solution, residual, density_bins, fixed_dofs):
    fixed = fixed_dofs.astype(jnp.float32)
    free = 1.0 - fixed
    modulus = stiffness(density_bins)
    widened = padded_2(modulus[None], (("gx", 1), ("gy", 2), ("gz", 3)), 1)[0]
    fine_upper, fine_lower = couplings(widened)
    fine_spring = 0.1 * modulus
    fine_diag = free * level_diagonal(fine_upper, fine_lower, fine_spring) + fixed

    def fine_apply(field):
        masked = free * field
        return (
            free * level_apply(masked, with_rim(masked), fine_upper, fine_lower, fine_spring)
            + fixed * field
        )

    mid_upper = coarse_links(fine_upper, 1)
    mid_lower = coarse_links(fine_lower, 0)
    mid_spring = restrict(fine_spring[None])[0]
    mid_diag = level_diagonal(mid_upper, mid_lower, mid_spring)
    low_upper = coarse_links(mid_upper, 1)
    low_lower = coarse_links(mid_lower, 0)
    low_spring = restrict(mid_spring[None])[0]
    fine_corr = damping * residual / fine_diag
    mid_rhs = restrict(residual - fine_apply(fine_corr))
    mid_corr = damping * mid_rhs / mid_diag
    coarse_rhs = restrict(
        mid_rhs - level_apply(mid_corr, with_rim(mid_corr), mid_upper, mid_lower, mid_spring)
    )
    low_diag = level_diagonal(low_upper, low_lower, low_spring)
    coarse_corr = chebyshev(coarse_rhs, low_upper, low_lower, low_spring, low_diag, with_rim)
    mid_corr = mid_corr + prolong(coarse_corr)
    mid_corr = (
        mid_corr
        + damping
        * (mid_rhs - level_apply(mid_corr, with_rim(mid_corr), mid_upper, mid_lower, mid_spring))
        / mid_diag
    )
    fine_corr = fine_corr + prolong(mid_corr)
    direction = fine_corr + damping * (residual - fine_apply(fine_corr)) / fine_diag
    precond_inner = lax.psum(jnp.sum(residual * direction), ("gx", "gy", "gz"))
    image = fine_apply(direction)
    curve_inner = lax.psum(jnp.sum(direction * image), ("gx", "gy", "gz"))
    alpha = precond_inner / curve_inner
    return (solution + alpha * direction, residual - alpha * image, direction)


def solution(mesh):
    return jax.shard_map(
        shards,
        mesh=mesh,
        in_specs=(
            P(None, "gx", "gy", "gz"),
            P(None, "gx", "gy", "gz"),
            P("gx", "gy", "gz"),
            P(None, "gx", "gy", "gz"),
        ),
        out_specs=(P(None, "gx", "gy", "gz"), P(None, "gx", "gy", "gz"), P(None, "gx", "gy", "gz")),
        check_vma=False,
    )
```

profile of v0, /device:TPU:1, one launch (start us, length us, event | category | flops | bytes accessed | tf_op | source)
XLA Modules:
  0.0 383.3 jit_solution(2636584339562638979)
XLA Ops:
  2.8 5.5 %collective-permute-start = (f32[1,1,16,128]{3,2,1,0:T(8,128)S(1)}, f32[1,1,16,128]{3,2,1,0:T(8,128)S(1)}, u32[]{:S(2)}, u32[]{:S(2)}) collective-permute-start(f32[1,1,16,128]{3,2,1,0:T(8,128)S(1)} %get-tuple-element.74), channel_id=1, source_target_pairs={{0,64},{64,128},{128,192},{192,256},{256,320},{320,384},{384,448},... | collective-permute-start | bytes 24584 | tf_op jit(solution)/shard_map/ppermute | solution.py:23
  9.1 12.1 %collective-permute-start.3 = (f32[1,10,1,128]{3,2,1,0:T(1,128)S(1)}, f32[1,10,1,128]{3,2,1,0:T(1,128)S(1)}, u32[]{:S(2)}, u32[]{:S(2)}) collective-permute-start(f32[1,10,1,128]{3,2,1,0:T(1,128)S(1)} %get-tuple-element.68), channel_id=1, source_target_pairs={{4,0},{8,4},{12,8},{16,12},{20,16},{24,20},{28,24},{32,28},{36,32}... | collective-permute-start | bytes 15368 | tf_op jit(solution)/shard_map/ppermute | solution.py:25
  21.2 1.9 collective-permute-start.2
  25.6 4.0 %collective-permute-start.4 = (f32[1,10,18,1]{3,2,1,0:T(8,128)S(1)}, f32[1,10,18,1]{3,2,1,0:T(8,128)S(1)}, u32[]{:S(2)}, u32[]{:S(2)}) collective-permute-start(f32[1,10,18,1]{3,2,1,0:T(8,128)S(1)} %get-tuple-element.65), channel_id=1, source_target_pairs={{0,1},{1,2},{2,3},{4,5},{5,6},{6,7},{8,9},{9,10},{10,11},{12,13},{... | collective-permute-start | bytes 2168 | tf_op jit(solution)/shard_map/ppermute | solution.py:23
  35.5 4.5 %collective-permute-start.7 = (f32[3,1,16,128]{3,2,1,0:T(8,128)S(1)}, f32[3,1,16,128]{3,2,1,0:T(8,128)S(1)}, u32[]{:S(2)}, u32[]{:S(2)}) collective-permute-start(f32[3,1,16,128]{3,2,1,0:T(8,128)S(1)} %get-tuple-element.55), channel_id=1, source_target_pairs={{0,64},{64,128},{128,192},{192,256},{256,320},{320,384},{384,448},... | collective-permute-start | bytes 73736 | tf_op jit(solution)/shard_map/ppermute | solution.py:23
  41.0 4.0 %collective-permute-start.8 = (f32[3,10,1,128]{3,2,1,0:T(1,128)S(1)}, f32[3,10,1,128]{3,2,1,0:T(1,128)S(1)}, u32[]{:S(2)}, u32[]{:S(2)}) collective-permute-start(f32[3,10,1,128]{3,2,1,0:T(1,128)S(1)} %get-tuple-element.50), channel_id=1, source_target_pairs={{4,0},{8,4},{12,8},{16,12},{20,16},{24,20},{28,24},{32,28},{36,32}... | collective-permute-start | bytes 46088 | tf_op jit(solution)/shard_map/ppermute | solution.py:25
  45.1 3.3 collective-permute-start.9
  48.3 5.5 %reshape_broadcast_in_dim.3 = f32[4,2,8,2,64,2]{5,4,3,2,1,0:T(8,128)} reshape(f32[8,16,128]{2,1,0:T(8,128)S(1)} %get-tuple-element.73) | data formatting | bytes 131072 | tf_op jit(solution)/shard_map/reshape;broadcast_in_dim | solution.py:86
  55.0 2.5 reduce_sum.273
  63.3 4.1 %collective-permute-start.11 = (f32[3,10,18,1]{3,2,1,0:T(8,128)S(1)}, f32[3,10,18,1]{3,2,1,0:T(8,128)S(1)}, u32[]{:S(2)}, u32[]{:S(2)}) collective-permute-start(f32[3,10,18,1]{3,2,1,0:T(8,128)S(1)} %get-tuple-element.44), channel_id=1, source_target_pairs={{0,1},{1,2},{2,3},{4,5},{5,6},{6,7},{8,9},{9,10},{10,11},{12,13},{... | collective-permute-start | bytes 6488 | tf_op jit(solution)/shard_map/ppermute | solution.py:23
  68.7 6.7 %collective-permute-done.11 = f32[3,10,18,1]{3,2,1,0:T(8,128)S(1)} collective-permute-done((f32[3,10,18,1]{3,2,1,0:T(8,128)S(1)}, f32[3,10,18,1]{3,2,1,0:T(8,128)S(1)}, u32[]{:S(2)}, u32[]{:S(2)}) %collective-permute-start.11) | collective-permute-done | bytes 2192 | tf_op jit(solution)/shard_map/ppermute | solution.py:23
  75.4 4.3 %collective-permute-done.10 = f32[3,10,18,1]{3,2,1,0:T(8,128)S(1)} collective-permute-done((f32[3,10,18,1]{3,2,1,0:T(8,128)S(1)}, f32[3,10,18,1]{3,2,1,0:T(8,128)S(1)}, u32[]{:S(2)}, u32[]{:S(2)}) %collective-permute-start.10) | collective-permute-done | bytes 2192 | tf_op jit(solution)/shard_map/ppermute | solution.py:25
  80.1 13.9 %reshape.191 = f32[3,4,2,8,2,64,2]{6,5,4,3,2,1,0:T(8,128)} reshape(f32[3,8,16,128]{3,2,1,0:T(8,128)S(1)} %fusion.49) | data formatting | bytes 393216 | tf_op jit(solution)/shard_map/reshape | solution.py:86
  94.1 5.5 %reduce_sum.262 = f32[3,4,8,64]{3,2,1,0:T(8,128)S(1)} reduce(f32[3,4,2,8,2,64,2]{6,5,4,3,2,1,0:T(8,128)} %reshape.191, f32[]{:T(128)} %constant.4.clone.1), dimensions={2,4,6}, to_apply=%region_0.1 | reduce | flops 43008 | bytes 221188 | tf_op jit(solution)/shard_map/reduce_sum | solution.py:86
  100.9 4.6 %collective-permute-start.13 = (f32[3,1,8,64]{3,2,1,0:T(8,128)S(1)}, f32[3,1,8,64]{3,2,1,0:T(8,128)S(1)}, u32[]{:S(2)}, u32[]{:S(2)}) collective-permute-start(f32[3,1,8,64]{3,2,1,0:T(8,128)S(1)} %get-tuple-element.82), channel_id=1, source_target_pairs={{0,64},{64,128},{128,192},{192,256},{256,320},{320,384},{384,448},... | collective-permute-start | bytes 18440 | tf_op jit(solution)/shard_map/ppermute | solution.py:23
  106.3 3.5 collective-permute-start.15
  113.0 1.9 collective-permute-start.14
  115.0 3.0 collective-permute-done.14
  119.4 4.0 %collective-permute-start.17 = (f32[3,6,10,1]{3,1,2,0:T(8,128)S(1)}, f32[3,6,10,1]{3,1,2,0:T(8,128)S(1)}, u32[]{:S(2)}, u32[]{:S(2)}) collective-permute-start(f32[3,6,10,1]{3,1,2,0:T(8,128)S(1)} %get-tuple-element.64), channel_id=1, source_target_pairs={{0,1},{1,2},{2,3},{4,5},{5,6},{6,7},{8,9},{9,10},{10,11},{12,13},{... | collective-permute-start | bytes 2168 | tf_op jit(solution)/shard_map/ppermute | solution.py:23
  123.7 1.6 collective-permute-done.17
  128.7 4.5 %collective-permute-start.19 = (f32[3,1,4,32]{3,2,1,0:T(4,128)S(1)}, f32[3,1,4,32]{3,2,1,0:T(4,128)S(1)}, u32[]{:S(2)}, u32[]{:S(2)}) collective-permute-start(f32[3,1,4,32]{3,2,1,0:T(4,128)S(1)} %get-tuple-element.90), channel_id=1, source_target_pairs={{0,64},{64,128},{128,192},{192,256},{256,320},{320,384},{384,448},... | collective-permute-start | bytes 4616 | tf_op jit(solution)/shard_map/ppermute | solution.py:23
  134.1 2.0 collective-permute-start.20
  136.0 3.8 collective-permute-start.21
  140.7 4.1 %collective-permute-start.23 = (f32[3,4,6,1]{3,2,1,0:T(8,128)S(1)}, f32[3,4,6,1]{3,2,1,0:T(8,128)S(1)}, u32[]{:S(2)}, u32[]{:S(2)}) collective-permute-start(f32[3,4,6,1]{3,2,1,0:T(8,128)S(1)} %get-tuple-element.81), channel_id=1, source_target_pairs={{0,1},{1,2},{2,3},{4,5},{5,6},{6,7},{8,9},{9,10},{10,11},{12,13},{... | collective-permute-start | bytes 872 | tf_op jit(solution)/shard_map/ppermute | solution.py:23
  146.0 3.5 collective-permute-done.22
  151.0 4.6 %collective-permute-start.25 = (f32[3,1,4,32]{3,2,1,0:T(4,128)S(1)}, f32[3,1,4,32]{3,2,1,0:T(4,128)S(1)}, u32[]{:S(2)}, u32[]{:S(2)}) collective-permute-start(f32[3,1,4,32]{3,2,1,0:T(4,128)S(1)} %get-tuple-element.88), channel_id=1, source_target_pairs={{0,64},{64,128},{128,192},{192,256},{256,320},{320,384},{384,448},... | collective-permute-start | bytes 4616 | tf_op jit(solution)/shard_map/ppermute | solution.py:23
  156.4 3.0 collective-permute-start.26
  159.4 5.3 %collective-permute-start.27 = (f32[3,4,1,32]{3,2,1,0:T(1,128)S(1)}, f32[3,4,1,32]{3,2,1,0:T(1,128)S(1)}, u32[]{:S(2)}, u32[]{:S(2)}) collective-permute-start(f32[3,4,1,32]{3,2,1,0:T(1,128)S(1)} %get-tuple-element.84), channel_id=1, source_target_pairs={{0,4},{4,8},{8,12},{12,16},{16,20},{20,24},{24,28},{28,32},{32,36}... | collective-permute-start | bytes 4616 | tf_op jit(solution)/shard_map/ppermute | solution.py:23
  165.6 1.9 collective-permute-start.29
  168.8 3.5 collective-permute-done.28
  174.2 4.5 %collective-permute-start.31 = (f32[3,1,8,64]{3,2,1,0:T(8,128)S(1)}, f32[3,1,8,64]{3,2,1,0:T(8,128)S(1)}, u32[]{:S(2)}, u32[]{:S(2)}) collective-permute-start(f32[3,1,8,64]{3,2,1,0:T(8,128)S(1)} %get-tuple-element.76), channel_id=1, source_target_pairs={{0,64},{64,128},{128,192},{192,256},{256,320},{320,384},{384,448},... | collective-permute-start | bytes 18440 | tf_op jit(solution)/shard_map/ppermute | solution.py:23
  179.6 6.5 %collective-permute-start.33 = (f32[3,6,1,64]{3,2,1,0:T(1,128)S(1)}, f32[3,6,1,64]{3,2,1,0:T(1,128)S(1)}, u32[]{:S(2)}, u32[]{:S(2)}) collective-permute-start(f32[3,6,1,64]{3,2,1,0:T(1,128)S(1)} %get-tuple-element.70), channel_id=1, source_target_pairs={{0,4},{4,8},{8,12},{12,16},{16,20},{20,24},{24,28},{28,32},{32,36}... | collective-permute-start | bytes 13832 | tf_op jit(solution)/shard_map/ppermute | solution.py:23
  186.1 1.9 collective-permute-start.32
  188.1 3.0 collective-permute-done.32
  192.5 4.0 %collective-permute-start.35 = (f32[3,6,10,1]{3,1,2,0:T(8,128)S(1)}, f32[3,6,10,1]{3,1,2,0:T(8,128)S(1)}, u32[]{:S(2)}, u32[]{:S(2)}) collective-permute-start(f32[3,6,10,1]{3,1,2,0:T(8,128)S(1)} %get-tuple-element.60), channel_id=1, source_target_pairs={{0,1},{1,2},{2,3},{4,5},{5,6},{6,7},{8,9},{9,10},{10,11},{12,13},{... | collective-permute-start | bytes 2168 | tf_op jit(solution)/shard_map/ppermute | solution.py:23
  201.1 5.8 %collective-permute-start.37 = (f32[3,1,16,128]{3,2,1,0:T(8,128)S(1)}, f32[3,1,16,128]{3,2,1,0:T(8,128)S(1)}, u32[]{:S(2)}, u32[]{:S(2)}) collective-permute-start(f32[3,1,16,128]{3,2,1,0:T(8,128)S(1)} %get-tuple-element.53), channel_id=1, source_target_pairs={{0,64},{64,128},{128,192},{192,256},{256,320},{320,384},{384,448},... | collective-permute-start | bytes 73736 | tf_op jit(solution)/shard_map/ppermute | solution.py:23
  207.8 2.0 collective-permute-start.38
  209.8 5.0 %collective-permute-start.39 = (f32[3,10,1,128]{3,2,1,0:T(1,128)S(1)}, f32[3,10,1,128]{3,2,1,0:T(1,128)S(1)}, u32[]{:S(2)}, u32[]{:S(2)}) collective-permute-start(f32[3,10,1,128]{3,2,1,0:T(1,128)S(1)} %get-tuple-element.47), channel_id=1, source_target_pairs={{0,4},{4,8},{8,12},{12,16},{16,20},{20,24},{24,28},{28,32},{32,36}... | collective-permute-start | bytes 46088 | tf_op jit(solution)/shard_map/ppermute | solution.py:23
  215.8 4.1 %collective-permute-start.41 = (f32[3,10,18,1]{3,2,1,0:T(8,128)S(1)}, f32[3,10,18,1]{3,2,1,0:T(8,128)S(1)}, u32[]{:S(2)}, u32[]{:S(2)}) collective-permute-start(f32[3,10,18,1]{3,2,1,0:T(8,128)S(1)} %get-tuple-element.42), channel_id=1, source_target_pairs={{0,1},{1,2},{2,3},{4,5},{5,6},{6,7},{8,9},{9,10},{10,11},{12,13},{... | collective-permute-start | bytes 6488 | tf_op jit(solution)/shard_map/ppermute | solution.py:23
  221.3 5.0 %collective-permute-done.41 = f32[3,10,18,1]{3,2,1,0:T(8,128)S(1)} collective-permute-done((f32[3,10,18,1]{3,2,1,0:T(8,128)S(1)}, f32[3,10,18,1]{3,2,1,0:T(8,128)S(1)}, u32[]{:S(2)}, u32[]{:S(2)}) %collective-permute-start.41) | collective-permute-done | bytes 2192 | tf_op jit(solution)/shard_map/ppermute | solution.py:23
  226.3 4.1 %collective-permute-done.40 = f32[3,10,18,1]{3,2,1,0:T(8,128)S(1)} collective-permute-done((f32[3,10,18,1]{3,2,1,0:T(8,128)S(1)}, f32[3,10,18,1]{3,2,1,0:T(8,128)S(1)}, u32[]{:S(2)}, u32[]{:S(2)}) %collective-permute-start.40) | collective-permute-done | bytes 2192 | tf_op jit(solution)/shard_map/ppermute | solution.py:25
  232.1 5.7 %collective-permute-start.43 = (f32[3,1,16,128]{3,2,1,0:T(8,128)S(1)}, f32[3,1,16,128]{3,2,1,0:T(8,128)S(1)}, u32[]{:S(2)}, u32[]{:S(2)}) collective-permute-start(f32[3,1,16,128]{3,2,1,0:T(8,128)S(1)} %get-tuple-element.51), channel_id=1, source_target_pairs={{0,64},{64,128},{128,192},{192,256},{256,320},{320,384},{384,448},... | collective-permute-start | bytes 73736 | tf_op jit(solution)/shard_map/ppermute | solution.py:23
  238.8 1.9 collective-permute-start.44
  240.8 5.7 %collective-permute-start.45 = (f32[3,10,1,128]{3,2,1,0:T(1,128)S(1)}, f32[3,10,1,128]{3,2,1,0:T(1,128)S(1)}, u32[]{:S(2)}, u32[]{:S(2)}) collective-permute-start(f32[3,10,1,128]{3,2,1,0:T(1,128)S(1)} %get-tuple-element.45), channel_id=1, source_target_pairs={{0,4},{4,8},{8,12},{12,16},{16,20},{20,24},{24,28},{28,32},{32,36}... | collective-permute-start | bytes 46088 | tf_op jit(solution)/shard_map/ppermute | solution.py:23
  247.5 3.1 collective-permute-start.47
  252.0 4.2 %collective-permute-done.47 = f32[3,10,18,1]{3,2,1,0:T(8,128)S(1)} collective-permute-done((f32[3,10,18,1]{3,2,1,0:T(8,128)S(1)}, f32[3,10,18,1]{3,2,1,0:T(8,128)S(1)}, u32[]{:S(2)}, u32[]{:S(2)}) %collective-permute-start.47) | collective-permute-done | bytes 2192 | tf_op jit(solution)/shard_map/ppermute | solution.py:23
  256.2 4.1 %collective-permute-done.46 = f32[3,10,18,1]{3,2,1,0:T(8,128)S(1)} collective-permute-done((f32[3,10,18,1]{3,2,1,0:T(8,128)S(1)}, f32[3,10,18,1]{3,2,1,0:T(8,128)S(1)}, u32[]{:S(2)}, u32[]{:S(2)}) %collective-permute-start.46) | collective-permute-done | bytes 2192 | tf_op jit(solution)/shard_map/ppermute | solution.py:25
  261.3 119.9 %all-reduce = (f32[]{:T(128)}, f32[]{:T(128)}) all-reduce(f32[]{:T(128)} %get-tuple-element.22, f32[]{:T(128)} %get-tuple-element.21), channel_id=1, replica_groups=mesh['gx'=12,'gy'=16,'gz'=4] {'gx','gy','gz'}, use_global_device_ids=true, to_apply=%region_17.18 | all-reduce | flops 2 | bytes 16 | tf_op jit(solution)/shard_map/psum | solution.py:171
  (170 shorter events, 56.9 us)
Async XLA Ops:
  1.5 6.8 %collective-permute-start.1 = (f32[1,1,16,128]{3,2,1,0:T(8,128)S(1)}, f32[1,1,16,128]{3,2,1,0:T(8,128)S(1)}, u32[]{:S(2)}, u32[]{:S(2)}) collective-permute-start(f32[1,1,16,128]{3,2,1,0:T(8,128)S(1)} %get-tuple-element.75), channel_id=1, source_target_pairs={{64,0},{128,64},{192,128},{256,192},{320,256},{384,320},{448,384},... | collective-permute-start | bytes 24584 | tf_op jit(solution)/shard_map/ppermute | solution.py:25
  2.8 6.2 %collective-permute-start = (f32[1,1,16,128]{3,2,1,0:T(8,128)S(1)}, f32[1,1,16,128]{3,2,1,0:T(8,128)S(1)}, u32[]{:S(2)}, u32[]{:S(2)}) collective-permute-start(f32[1,1,16,128]{3,2,1,0:T(8,128)S(1)} %get-tuple-element.74), channel_id=1, source_target_pairs={{0,64},{64,128},{128,192},{192,256},{256,320},{320,384},{384,448},... | collective-permute-start | bytes 24584 | tf_op jit(solution)/shard_map/ppermute | solution.py:23
  9.1 14.0 %collective-permute-start.3 = (f32[1,10,1,128]{3,2,1,0:T(1,128)S(1)}, f32[1,10,1,128]{3,2,1,0:T(1,128)S(1)}, u32[]{:S(2)}, u32[]{:S(2)}) collective-permute-start(f32[1,10,1,128]{3,2,1,0:T(1,128)S(1)} %get-tuple-element.68), channel_id=1, source_target_pairs={{4,0},{8,4},{12,8},{16,12},{20,16},{24,20},{28,24},{32,28},{36,32}... | collective-permute-start | bytes 15368 | tf_op jit(solution)/shard_map/ppermute | solution.py:25
  21.2 3.1 collective-permute-start.2
  24.3 6.7 %collective-permute-start.5 = (f32[1,10,18,1]{3,2,1,0:T(8,128)S(1)}, f32[1,10,18,1]{3,2,1,0:T(8,128)S(1)}, u32[]{:S(2)}, u32[]{:S(2)}) collective-permute-start(f32[1,10,18,1]{3,2,1,0:T(8,128)S(1)} %get-tuple-element.66), channel_id=1, source_target_pairs={{1,0},{2,1},{3,2},{5,4},{6,5},{7,6},{9,8},{10,9},{11,10},{13,12},{... | collective-permute-start | bytes 2168 | tf_op jit(solution)/shard_map/ppermute | solution.py:25
  25.6 6.2 %collective-permute-start.4 = (f32[1,10,18,1]{3,2,1,0:T(8,128)S(1)}, f32[1,10,18,1]{3,2,1,0:T(8,128)S(1)}, u32[]{:S(2)}, u32[]{:S(2)}) collective-permute-start(f32[1,10,18,1]{3,2,1,0:T(8,128)S(1)} %get-tuple-element.65), channel_id=1, source_target_pairs={{0,1},{1,2},{2,3},{4,5},{5,6},{6,7},{8,9},{9,10},{10,11},{12,13},{... | collective-permute-start | bytes 2168 | tf_op jit(solution)/shard_map/ppermute | solution.py:23
  34.2 5.8 %collective-permute-start.6 = (f32[3,1,16,128]{3,2,1,0:T(8,128)S(1)}, f32[3,1,16,128]{3,2,1,0:T(8,128)S(1)}, u32[]{:S(2)}, u32[]{:S(2)}) collective-permute-start(f32[3,1,16,128]{3,2,1,0:T(8,128)S(1)} %get-tuple-element.56), channel_id=1, source_target_pairs={{64,0},{128,64},{192,128},{256,192},{320,256},{384,320},{448,384},... | collective-permute-start | bytes 73736 | tf_op jit(solution)/shard_map/ppermute | solution.py:25
  35.5 5.5 %collective-permute-start.7 = (f32[3,1,16,128]{3,2,1,0:T(8,128)S(1)}, f32[3,1,16,128]{3,2,1,0:T(8,128)S(1)}, u32[]{:S(2)}, u32[]{:S(2)}) collective-permute-start(f32[3,1,16,128]{3,2,1,0:T(8,128)S(1)} %get-tuple-element.55), channel_id=1, source_target_pairs={{0,64},{64,128},{128,192},{192,256},{256,320},{320,384},{384,448},... | collective-permute-start | bytes 73736 | tf_op jit(solution)/shard_map/ppermute | solution.py:23
  41.0 22.1 %collective-permute-start.8 = (f32[3,10,1,128]{3,2,1,0:T(1,128)S(1)}, f32[3,10,1,128]{3,2,1,0:T(1,128)S(1)}, u32[]{:S(2)}, u32[]{:S(2)}) collective-permute-start(f32[3,10,1,128]{3,2,1,0:T(1,128)S(1)} %get-tuple-element.50), channel_id=1, source_target_pairs={{4,0},{8,4},{12,8},{16,12},{20,16},{24,20},{28,24},{32,28},{36,32}... | collective-permute-start | bytes 46088 | tf_op jit(solution)/shard_map/ppermute | solution.py:25
  45.1 18.0 %collective-permute-start.9 = (f32[3,10,1,128]{3,2,1,0:T(1,128)S(1)}, f32[3,10,1,128]{3,2,1,0:T(1,128)S(1)}, u32[]{:S(2)}, u32[]{:S(2)}) collective-permute-start(f32[3,10,1,128]{3,2,1,0:T(1,128)S(1)} %get-tuple-element.49), channel_id=1, source_target_pairs={{0,4},{4,8},{8,12},{12,16},{16,20},{20,24},{24,28},{28,32},{32,36}... | collective-permute-start | bytes 46088 | tf_op jit(solution)/shard_map/ppermute | solution.py:23
  63.3 12.1 %collective-permute-start.11 = (f32[3,10,18,1]{3,2,1,0:T(8,128)S(1)}, f32[3,10,18,1]{3,2,1,0:T(8,128)S(1)}, u32[]{:S(2)}, u32[]{:S(2)}) collective-permute-start(f32[3,10,18,1]{3,2,1,0:T(8,128)S(1)} %get-tuple-element.44), channel_id=1, source_target_pairs={{0,1},{1,2},{2,3},{4,5},{5,6},{6,7},{8,9},{9,10},{10,11},{12,13},{... | collective-permute-start | bytes 6488 | tf_op jit(solution)/shard_map/ppermute | solution.py:23
  67.4 12.3 %collective-permute-start.10 = (f32[3,10,18,1]{3,2,1,0:T(8,128)S(1)}, f32[3,10,18,1]{3,2,1,0:T(8,128)S(1)}, u32[]{:S(2)}, u32[]{:S(2)}) collective-permute-start(f32[3,10,18,1]{3,2,1,0:T(8,128)S(1)} %get-tuple-element.43), channel_id=1, source_target_pairs={{1,0},{2,1},{3,2},{5,4},{6,5},{7,6},{9,8},{10,9},{11,10},{13,12},{... | collective-permute-start | bytes 6488 | tf_op jit(solution)/shard_map/ppermute | solution.py:25
  99.6 5.9 %collective-permute-start.12 = (f32[3,1,8,64]{3,2,1,0:T(8,128)S(1)}, f32[3,1,8,64]{3,2,1,0:T(8,128)S(1)}, u32[]{:S(2)}, u32[]{:S(2)}) collective-permute-start(f32[3,1,8,64]{3,2,1,0:T(8,128)S(1)} %get-tuple-element.83), channel_id=1, source_target_pairs={{64,0},{128,64},{192,128},{256,192},{320,256},{384,320},{448,384},... | collective-permute-start | bytes 18440 | tf_op jit(solution)/shard_map/ppermute | solution.py:25
  100.9 5.4 %collective-permute-start.13 = (f32[3,1,8,64]{3,2,1,0:T(8,128)S(1)}, f32[3,1,8,64]{3,2,1,0:T(8,128)S(1)}, u32[]{:S(2)}, u32[]{:S(2)}) collective-permute-start(f32[3,1,8,64]{3,2,1,0:T(8,128)S(1)} %get-tuple-element.82), channel_id=1, source_target_pairs={{0,64},{64,128},{128,192},{192,256},{256,320},{320,384},{384,448},... | collective-permute-start | bytes 18440 | tf_op jit(solution)/shard_map/ppermute | solution.py:23
  106.3 8.7 %collective-permute-start.15 = (f32[3,6,1,64]{3,2,1,0:T(1,128)S(1)}, f32[3,6,1,64]{3,2,1,0:T(1,128)S(1)}, u32[]{:S(2)}, u32[]{:S(2)}) collective-permute-start(f32[3,6,1,64]{3,2,1,0:T(1,128)S(1)} %get-tuple-element.72), channel_id=1, source_target_pairs={{0,4},{4,8},{8,12},{12,16},{16,20},{20,24},{24,28},{28,32},{32,36}... | collective-permute-start | bytes 13832 | tf_op jit(solution)/shard_map/ppermute | solution.py:23
  113.0 5.0 %collective-permute-start.14 = (f32[3,6,1,64]{3,2,1,0:T(1,128)S(1)}, f32[3,6,1,64]{3,2,1,0:T(1,128)S(1)}, u32[]{:S(2)}, u32[]{:S(2)}) collective-permute-start(f32[3,6,1,64]{3,2,1,0:T(1,128)S(1)} %get-tuple-element.71), channel_id=1, source_target_pairs={{4,0},{8,4},{12,8},{16,12},{20,16},{24,20},{28,24},{32,28},{36,32}... | collective-permute-start | bytes 13832 | tf_op jit(solution)/shard_map/ppermute | solution.py:25
  118.1 5.6 %collective-permute-start.16 = (f32[3,6,10,1]{3,1,2,0:T(8,128)S(1)}, f32[3,6,10,1]{3,1,2,0:T(8,128)S(1)}, u32[]{:S(2)}, u32[]{:S(2)}) collective-permute-start(f32[3,6,10,1]{3,1,2,0:T(8,128)S(1)} %get-tuple-element.63), channel_id=1, source_target_pairs={{1,0},{2,1},{3,2},{5,4},{6,5},{7,6},{9,8},{10,9},{11,10},{13,12},{... | collective-permute-start | bytes 2168 | tf_op jit(solution)/shard_map/ppermute | solution.py:25
  119.4 6.0 %collective-permute-start.17 = (f32[3,6,10,1]{3,1,2,0:T(8,128)S(1)}, f32[3,6,10,1]{3,1,2,0:T(8,128)S(1)}, u32[]{:S(2)}, u32[]{:S(2)}) collective-permute-start(f32[3,6,10,1]{3,1,2,0:T(8,128)S(1)} %get-tuple-element.64), channel_id=1, source_target_pairs={{0,1},{1,2},{2,3},{4,5},{5,6},{6,7},{8,9},{9,10},{10,11},{12,13},{... | collective-permute-start | bytes 2168 | tf_op jit(solution)/shard_map/ppermute | solution.py:23
  127.4 5.9 %collective-permute-start.18 = (f32[3,1,4,32]{3,2,1,0:T(4,128)S(1)}, f32[3,1,4,32]{3,2,1,0:T(4,128)S(1)}, u32[]{:S(2)}, u32[]{:S(2)}) collective-permute-start(f32[3,1,4,32]{3,2,1,0:T(4,128)S(1)} %get-tuple-element.91), channel_id=1, source_target_pairs={{64,0},{128,64},{192,128},{256,192},{320,256},{384,320},{448,384},... | collective-permute-start | bytes 4616 | tf_op jit(solution)/shard_map/ppermute | solution.py:25
  128.7 5.3 %collective-permute-start.19 = (f32[3,1,4,32]{3,2,1,0:T(4,128)S(1)}, f32[3,1,4,32]{3,2,1,0:T(4,128)S(1)}, u32[]{:S(2)}, u32[]{:S(2)}) collective-permute-start(f32[3,1,4,32]{3,2,1,0:T(4,128)S(1)} %get-tuple-element.90), channel_id=1, source_target_pairs={{0,64},{64,128},{128,192},{192,256},{256,320},{320,384},{384,448},... | collective-permute-start | bytes 4616 | tf_op jit(solution)/shard_map/ppermute | solution.py:23
  134.1 5.8 %collective-permute-start.20 = (f32[3,4,1,32]{3,2,1,0:T(1,128)S(1)}, f32[3,4,1,32]{3,2,1,0:T(1,128)S(1)}, u32[]{:S(2)}, u32[]{:S(2)}) collective-permute-start(f32[3,4,1,32]{3,2,1,0:T(1,128)S(1)} %get-tuple-element.87), channel_id=1, source_target_pairs={{4,0},{8,4},{12,8},{16,12},{20,16},{24,20},{28,24},{32,28},{36,32}... | collective-permute-start | bytes 4616 | tf_op jit(solution)/shard_map/ppermute | solution.py:25
  136.0 4.5 %collective-permute-start.21 = (f32[3,4,1,32]{3,2,1,0:T(1,128)S(1)}, f32[3,4,1,32]{3,2,1,0:T(1,128)S(1)}, u32[]{:S(2)}, u32[]{:S(2)}) collective-permute-start(f32[3,4,1,32]{3,2,1,0:T(1,128)S(1)} %get-tuple-element.86), channel_id=1, source_target_pairs={{0,4},{4,8},{8,12},{12,16},{16,20},{20,24},{24,28},{28,32},{32,36}... | collective-permute-start | bytes 4616 | tf_op jit(solution)/shard_map/ppermute | solution.py:23
  140.7 5.4 %collective-permute-start.23 = (f32[3,4,6,1]{3,2,1,0:T(8,128)S(1)}, f32[3,4,6,1]{3,2,1,0:T(8,128)S(1)}, u32[]{:S(2)}, u32[]{:S(2)}) collective-permute-start(f32[3,4,6,1]{3,2,1,0:T(8,128)S(1)} %get-tuple-element.81), channel_id=1, source_target_pairs={{0,1},{1,2},{2,3},{4,5},{5,6},{6,7},{8,9},{9,10},{10,11},{12,13},{... | collective-permute-start | bytes 872 | tf_op jit(solution)/shard_map/ppermute | solution.py:23
  144.7 4.8 %collective-permute-start.22 = (f32[3,4,6,1]{3,2,1,0:T(8,128)S(1)}, f32[3,4,6,1]{3,2,1,0:T(8,128)S(1)}, u32[]{:S(2)}, u32[]{:S(2)}) collective-permute-start(f32[3,4,6,1]{3,2,1,0:T(8,128)S(1)} %get-tuple-element.80), channel_id=1, source_target_pairs={{1,0},{2,1},{3,2},{5,4},{6,5},{7,6},{9,8},{10,9},{11,10},{13,12},{... | collective-permute-start | bytes 872 | tf_op jit(solution)/shard_map/ppermute | solution.py:25
  149.7 5.9 %collective-permute-start.24 = (f32[3,1,4,32]{3,2,1,0:T(4,128)S(1)}, f32[3,1,4,32]{3,2,1,0:T(4,128)S(1)}, u32[]{:S(2)}, u32[]{:S(2)}) collective-permute-start(f32[3,1,4,32]{3,2,1,0:T(4,128)S(1)} %get-tuple-element.89), channel_id=1, source_target_pairs={{64,0},{128,64},{192,128},{256,192},{320,256},{384,320},{448,384},... | collective-permute-start | bytes 4616 | tf_op jit(solution)/shard_map/ppermute | solution.py:25
  151.0 5.3 %collective-permute-start.25 = (f32[3,1,4,32]{3,2,1,0:T(4,128)S(1)}, f32[3,1,4,32]{3,2,1,0:T(4,128)S(1)}, u32[]{:S(2)}, u32[]{:S(2)}) collective-permute-start(f32[3,1,4,32]{3,2,1,0:T(4,128)S(1)} %get-tuple-element.88), channel_id=1, source_target_pairs={{0,64},{64,128},{128,192},{192,256},{256,320},{320,384},{384,448},... | collective-permute-start | bytes 4616 | tf_op jit(solution)/shard_map/ppermute | solution.py:23
  156.4 8.4 %collective-permute-start.26 = (f32[3,4,1,32]{3,2,1,0:T(1,128)S(1)}, f32[3,4,1,32]{3,2,1,0:T(1,128)S(1)}, u32[]{:S(2)}, u32[]{:S(2)}) collective-permute-start(f32[3,4,1,32]{3,2,1,0:T(1,128)S(1)} %get-tuple-element.85), channel_id=1, source_target_pairs={{4,0},{8,4},{12,8},{16,12},{20,16},{24,20},{28,24},{32,28},{36,32}... | collective-permute-start | bytes 4616 | tf_op jit(solution)/shard_map/ppermute | solution.py:25
  159.4 6.1 %collective-permute-start.27 = (f32[3,4,1,32]{3,2,1,0:T(1,128)S(1)}, f32[3,4,1,32]{3,2,1,0:T(1,128)S(1)}, u32[]{:S(2)}, u32[]{:S(2)}) collective-permute-start(f32[3,4,1,32]{3,2,1,0:T(1,128)S(1)} %get-tuple-element.84), channel_id=1, source_target_pairs={{0,4},{4,8},{8,12},{12,16},{16,20},{20,24},{24,28},{28,32},{32,36}... | collective-permute-start | bytes 4616 | tf_op jit(solution)/shard_map/ppermute | solution.py:23
  165.6 3.2 collective-permute-start.29
  167.5 4.8 %collective-permute-start.28 = (f32[3,4,6,1]{3,2,1,0:T(8,128)S(1)}, f32[3,4,6,1]{3,2,1,0:T(8,128)S(1)}, u32[]{:S(2)}, u32[]{:S(2)}) collective-permute-start(f32[3,4,6,1]{3,2,1,0:T(8,128)S(1)} %get-tuple-element.78), channel_id=1, source_target_pairs={{1,0},{2,1},{3,2},{5,4},{6,5},{7,6},{9,8},{10,9},{11,10},{13,12},{... | collective-permute-start | bytes 872 | tf_op jit(solution)/shard_map/ppermute | solution.py:25
  172.9 5.8 %collective-permute-start.30 = (f32[3,1,8,64]{3,2,1,0:T(8,128)S(1)}, f32[3,1,8,64]{3,2,1,0:T(8,128)S(1)}, u32[]{:S(2)}, u32[]{:S(2)}) collective-permute-start(f32[3,1,8,64]{3,2,1,0:T(8,128)S(1)} %get-tuple-element.77), channel_id=1, source_target_pairs={{64,0},{128,64},{192,128},{256,192},{320,256},{384,320},{448,384},... | collective-permute-start | bytes 18440 | tf_op jit(solution)/shard_map/ppermute | solution.py:25
  174.2 5.4 %collective-permute-start.31 = (f32[3,1,8,64]{3,2,1,0:T(8,128)S(1)}, f32[3,1,8,64]{3,2,1,0:T(8,128)S(1)}, u32[]{:S(2)}, u32[]{:S(2)}) collective-permute-start(f32[3,1,8,64]{3,2,1,0:T(8,128)S(1)} %get-tuple-element.76), channel_id=1, source_target_pairs={{0,64},{64,128},{128,192},{192,256},{256,320},{320,384},{384,448},... | collective-permute-start | bytes 18440 | tf_op jit(solution)/shard_map/ppermute | solution.py:23
  179.6 8.4 %collective-permute-start.33 = (f32[3,6,1,64]{3,2,1,0:T(1,128)S(1)}, f32[3,6,1,64]{3,2,1,0:T(1,128)S(1)}, u32[]{:S(2)}, u32[]{:S(2)}) collective-permute-start(f32[3,6,1,64]{3,2,1,0:T(1,128)S(1)} %get-tuple-element.70), channel_id=1, source_target_pairs={{0,4},{4,8},{8,12},{12,16},{16,20},{20,24},{24,28},{28,32},{32,36}... | collective-permute-start | bytes 13832 | tf_op jit(solution)/shard_map/ppermute | solution.py:23
  186.1 5.0 %collective-permute-start.32 = (f32[3,6,1,64]{3,2,1,0:T(1,128)S(1)}, f32[3,6,1,64]{3,2,1,0:T(1,128)S(1)}, u32[]{:S(2)}, u32[]{:S(2)}) collective-permute-start(f32[3,6,1,64]{3,2,1,0:T(1,128)S(1)} %get-tuple-element.69), channel_id=1, source_target_pairs={{4,0},{8,4},{12,8},{16,12},{20,16},{24,20},{28,24},{32,28},{36,32}... | collective-permute-start | bytes 13832 | tf_op jit(solution)/shard_map/ppermute | solution.py:25
  191.2 5.6 %collective-permute-start.34 = (f32[3,6,10,1]{3,1,2,0:T(8,128)S(1)}, f32[3,6,10,1]{3,1,2,0:T(8,128)S(1)}, u32[]{:S(2)}, u32[]{:S(2)}) collective-permute-start(f32[3,6,10,1]{3,1,2,0:T(8,128)S(1)} %get-tuple-element.59), channel_id=1, source_target_pairs={{1,0},{2,1},{3,2},{5,4},{6,5},{7,6},{9,8},{10,9},{11,10},{13,12},{... | collective-permute-start | bytes 2168 | tf_op jit(solution)/shard_map/ppermute | solution.py:25
  192.5 6.0 %collective-permute-start.35 = (f32[3,6,10,1]{3,1,2,0:T(8,128)S(1)}, f32[3,6,10,1]{3,1,2,0:T(8,128)S(1)}, u32[]{:S(2)}, u32[]{:S(2)}) collective-permute-start(f32[3,6,10,1]{3,1,2,0:T(8,128)S(1)} %get-tuple-element.60), channel_id=1, source_target_pairs={{0,1},{1,2},{2,3},{4,5},{5,6},{6,7},{8,9},{9,10},{10,11},{12,13},{... | collective-permute-start | bytes 2168 | tf_op jit(solution)/shard_map/ppermute | solution.py:23
  199.8 7.1 %collective-permute-start.36 = (f32[3,1,16,128]{3,2,1,0:T(8,128)S(1)}, f32[3,1,16,128]{3,2,1,0:T(8,128)S(1)}, u32[]{:S(2)}, u32[]{:S(2)}) collective-permute-start(f32[3,1,16,128]{3,2,1,0:T(8,128)S(1)} %get-tuple-element.54), channel_id=1, source_target_pairs={{64,0},{128,64},{192,128},{256,192},{320,256},{384,320},{448,384},... | collective-permute-start | bytes 73736 | tf_op jit(solution)/shard_map/ppermute | solution.py:25
  201.1 6.7 %collective-permute-start.37 = (f32[3,1,16,128]{3,2,1,0:T(8,128)S(1)}, f32[3,1,16,128]{3,2,1,0:T(8,128)S(1)}, u32[]{:S(2)}, u32[]{:S(2)}) collective-permute-start(f32[3,1,16,128]{3,2,1,0:T(8,128)S(1)} %get-tuple-element.53), channel_id=1, source_target_pairs={{0,64},{64,128},{128,192},{192,256},{256,320},{320,384},{384,448},... | collective-permute-start | bytes 73736 | tf_op jit(solution)/shard_map/ppermute | solution.py:23
  207.8 7.0 %collective-permute-start.38 = (f32[3,10,1,128]{3,2,1,0:T(1,128)S(1)}, f32[3,10,1,128]{3,2,1,0:T(1,128)S(1)}, u32[]{:S(2)}, u32[]{:S(2)}) collective-permute-start(f32[3,10,1,128]{3,2,1,0:T(1,128)S(1)} %get-tuple-element.48), channel_id=1, source_target_pairs={{4,0},{8,4},{12,8},{16,12},{20,16},{24,20},{28,24},{32,28},{36,32}... | collective-permute-start | bytes 46088 | tf_op jit(solution)/shard_map/ppermute | solution.py:25
  209.8 5.8 %collective-permute-start.39 = (f32[3,10,1,128]{3,2,1,0:T(1,128)S(1)}, f32[3,10,1,128]{3,2,1,0:T(1,128)S(1)}, u32[]{:S(2)}, u32[]{:S(2)}) collective-permute-start(f32[3,10,1,128]{3,2,1,0:T(1,128)S(1)} %get-tuple-element.47), channel_id=1, source_target_pairs={{0,4},{4,8},{8,12},{12,16},{16,20},{20,24},{24,28},{28,32},{32,36}... | collective-permute-start | bytes 46088 | tf_op jit(solution)/shard_map/ppermute | solution.py:23
  215.8 10.4 %collective-permute-start.41 = (f32[3,10,18,1]{3,2,1,0:T(8,128)S(1)}, f32[3,10,18,1]{3,2,1,0:T(8,128)S(1)}, u32[]{:S(2)}, u32[]{:S(2)}) collective-permute-start(f32[3,10,18,1]{3,2,1,0:T(8,128)S(1)} %get-tuple-element.42), channel_id=1, source_target_pairs={{0,1},{1,2},{2,3},{4,5},{5,6},{6,7},{8,9},{9,10},{10,11},{12,13},{... | collective-permute-start | bytes 6488 | tf_op jit(solution)/shard_map/ppermute | solution.py:23
  220.0 10.4 %collective-permute-start.40 = (f32[3,10,18,1]{3,2,1,0:T(8,128)S(1)}, f32[3,10,18,1]{3,2,1,0:T(8,128)S(1)}, u32[]{:S(2)}, u32[]{:S(2)}) collective-permute-start(f32[3,10,18,1]{3,2,1,0:T(8,128)S(1)} %get-tuple-element.41), channel_id=1, source_target_pairs={{1,0},{2,1},{3,2},{5,4},{6,5},{7,6},{9,8},{10,9},{11,10},{13,12},{... | collective-permute-start | bytes 6488 | tf_op jit(solution)/shard_map/ppermute | solution.py:25
  230.8 7.1 %collective-permute-start.42 = (f32[3,1,16,128]{3,2,1,0:T(8,128)S(1)}, f32[3,1,16,128]{3,2,1,0:T(8,128)S(1)}, u32[]{:S(2)}, u32[]{:S(2)}) collective-permute-start(f32[3,1,16,128]{3,2,1,0:T(8,128)S(1)} %get-tuple-element.52), channel_id=1, source_target_pairs={{64,0},{128,64},{192,128},{256,192},{320,256},{384,320},{448,384},... | collective-permute-start | bytes 73736 | tf_op jit(solution)/shard_map/ppermute | solution.py:25
  232.1 6.7 %collective-permute-start.43 = (f32[3,1,16,128]{3,2,1,0:T(8,128)S(1)}, f32[3,1,16,128]{3,2,1,0:T(8,128)S(1)}, u32[]{:S(2)}, u32[]{:S(2)}) collective-permute-start(f32[3,1,16,128]{3,2,1,0:T(8,128)S(1)} %get-tuple-element.51), channel_id=1, source_target_pairs={{0,64},{64,128},{128,192},{192,256},{256,320},{320,384},{384,448},... | collective-permute-start | bytes 73736 | tf_op jit(solution)/shard_map/ppermute | solution.py:23
  238.8 7.6 %collective-permute-start.44 = (f32[3,10,1,128]{3,2,1,0:T(1,128)S(1)}, f32[3,10,1,128]{3,2,1,0:T(1,128)S(1)}, u32[]{:S(2)}, u32[]{:S(2)}) collective-permute-start(f32[3,10,1,128]{3,2,1,0:T(1,128)S(1)} %get-tuple-element.46), channel_id=1, source_target_pairs={{4,0},{8,4},{12,8},{16,12},{20,16},{24,20},{28,24},{32,28},{36,32}... | collective-permute-start | bytes 46088 | tf_op jit(solution)/shard_map/ppermute | solution.py:25
  240.8 6.5 %collective-permute-start.45 = (f32[3,10,1,128]{3,2,1,0:T(1,128)S(1)}, f32[3,10,1,128]{3,2,1,0:T(1,128)S(1)}, u32[]{:S(2)}, u32[]{:S(2)}) collective-permute-start(f32[3,10,1,128]{3,2,1,0:T(1,128)S(1)} %get-tuple-element.45), channel_id=1, source_target_pairs={{0,4},{4,8},{8,12},{12,16},{16,20},{20,24},{24,28},{28,32},{32,36}... | collective-permute-start | bytes 46088 | tf_op jit(solution)/shard_map/ppermute | solution.py:23
  247.5 8.7 %collective-permute-start.47 = (f32[3,10,18,1]{3,2,1,0:T(8,128)S(1)}, f32[3,10,18,1]{3,2,1,0:T(8,128)S(1)}, u32[]{:S(2)}, u32[]{:S(2)}) collective-permute-start(f32[3,10,18,1]{3,2,1,0:T(8,128)S(1)} %get-tuple-element.40), channel_id=1, source_target_pairs={{0,1},{1,2},{2,3},{4,5},{5,6},{6,7},{8,9},{9,10},{10,11},{12,13},{... | collective-permute-start | bytes 6488 | tf_op jit(solution)/shard_map/ppermute | solution.py:23
  250.7 9.6 %collective-permute-start.46 = (f32[3,10,18,1]{3,2,1,0:T(8,128)S(1)}, f32[3,10,18,1]{3,2,1,0:T(8,128)S(1)}, u32[]{:S(2)}, u32[]{:S(2)}) collective-permute-start(f32[3,10,18,1]{3,2,1,0:T(8,128)S(1)} %get-tuple-element.39), channel_id=1, source_target_pairs={{1,0},{2,1},{3,2},{5,4},{6,5},{7,6},{9,8},{10,9},{11,10},{13,12},{... | collective-permute-start | bytes 6488 | tf_op jit(solution)/shard_map/ppermute | solution.py:25
  (4 other events, 361.2 us)
where the time goes:
time: 389 us; the launch traced here: 383 us
  starting transfers between devices  153 us (39%)
  blocking collectives  120 us (31%)
  waiting for transfers between devices  58.6 us (15%)
  local copies, waits for them, and re-layouts  29.7 us (8%)
  other arithmetic  18.6 us (5%)
    psum x1, blocking collectives, shards(): precond_inner = lax.psum(jnp.sum(residual * direction), ('gx', 'gy', 'gz'))  120 us
    ppermute x24, starting transfers between devices, padded_2(): lax.ppermute(tail, axis, [(i, (i + 1) % count) for i in range(ends)])  104 us
    ppermute x24, starting transfers between devices, padded_2(): lax.ppermute(head, axis, [((i + 1) % count, i) for i in range(ends)])  49.5 us
    ppermute x24, waiting for transfers between devices, padded_2(): lax.ppermute(tail, axis, [(i, (i + 1) % count) for i in range(ends)])  30.9 us
    ppermute x24, waiting for transfers between devices, padded_2(): lax.ppermute(head, axis, [((i + 1) % count, i) for i in range(ends)])  27.7 us
    reshape x2, local copies, waits for them, and re-layouts, restrict(): field.reshape(channels, size_x // 2, 2, size_y // 2, 2, size_z // 2, 2)  15.5 us
    reduce_sum x4, other arithmetic, restrict(): field.reshape(channels, size_x // 2, 2, size_y // 2, 2, size_z // 2, 2)  8.36 us
  transfers between devices with their start and end apart: 48, of which 29 were waited for; matrix products, arithmetic and copies ran while one was open for 5% of the time, Pallas kernels for 0%

commit v1 on v0

v1 whole, which is shorter than its diff:
```python
import functools

import jax
import jax.numpy as jnp
from jax import lax
from jax.experimental import pallas as pl
from jax.experimental.pallas import tpu as pltpu
from jax.sharding import Mesh
from jax.sharding import PartitionSpec as P

BINS = 16
damping = 0.6
keep = 1.0 - damping
eig_center = 1.05
eig_halfwidth = 0.95

F32 = jnp.float32
CX, CY, CZ = 8, 16, 128
LANES = 2 * CZ
ROWS = CY + 16
PLANES = CX + 16
ZH = 16
FIELDS = 7
GYX = CX + 2

VMEM = pl.BlockSpec(memory_space=pltpu.VMEM)
SMEM = pl.BlockSpec(memory_space=pltpu.SMEM)


def call(kernel, outs, scratch=()):
    return pl.pallas_call(
        kernel,
        out_shape=[jax.ShapeDtypeStruct(s, F32) for s in outs],
        out_specs=[VMEM] * len(outs),
        scratch_shapes=[pltpu.VMEM(s, F32) for s in scratch],
        compiler_params=pltpu.CompilerParams(vmem_limit_bytes=48 * 1024 * 1024),
    )


def before(v, k, axis):
    return pltpu.roll(v, k, axis)


def after(v, k, axis):
    return pltpu.roll(v, v.shape[axis] - k, axis)


def lane_of(shape):
    return lax.broadcasted_iota(jnp.int32, shape, len(shape) - 1)


def pair_sum(v, k):
    low = lane_of(v.shape) % (2 * k) < k
    return v + jnp.where(low, after(v, k, 1), before(v, k, 1))


def odd_group(v, k):
    low = lane_of(v.shape) % (2 * k) < k
    return jnp.where(low, after(v, k, 1), v)


def neighbours(ux, ux_prev, uy, uz, here, prev, nxt, k):
    return (
        ux * nxt
        + ux_prev * prev
        + uy * after(here, 1, 0)
        + before(uy * here, 1, 0)
        + uz * after(here, k, 1)
        + before(uz * here, k, 1)
    )


def gather_kernel(density, residual, fixed, main, to_right, to_left):
    lane = lane_of((CY, CZ))

    def stage(field, values):
        right = jnp.zeros((CY, CZ), F32)
        left = jnp.zeros((CY, CZ), F32)
        for x, v in enumerate(values):
            main[field, x] = v
            mine = (lane >= ZH * x) & (lane < ZH * (x + 1))
            right = jnp.where(mine, pltpu.roll(v, (ZH * x + ZH) % CZ, 1), right)
            left = jnp.where(mine, pltpu.roll(v, ZH * x, 1) if x else v, left)
        to_right[field] = right
        to_left[field] = left

    def modulus(bins):
        f = (bins.astype(F32) + 1.0) / BINS
        return 0.05 + 0.95 * f * f * f

    stage(0, [modulus(density[x]) for x in range(CX)])
    for c in range(3):
        stage(1 + c, [residual[c, x] for x in range(CX)])
        stage(4 + c, [1.0 - fixed[c, x].astype(F32) for x in range(CX)])


def restrict_rows(tmp, v):
    n = v.shape[0] // 2
    for h in range(2):
        tmp[h] = v[:, CZ * h : CZ * (h + 1)]
    return [jnp.concatenate([tmp[h, pl.ds(i, n, stride=2), :] for h in range(2)], axis=1) for i in range(2)]


def repeat_rows(tmp, v):
    n = v.shape[0]
    for h in range(2):
        for i in range(2):
            tmp[h, pl.ds(i, n, stride=2), :] = v[:, CZ * h : CZ * (h + 1)]
    return jnp.concatenate([tmp[0], tmp[1]], axis=1)


def fine_kernel(
    ends, x0, xl, xr, yl, yr,
    o_r, o_free, o_ux, o_uy, o_uz, o_ig, o_mc, o_mux, o_muy, o_muz, o_mig, o_right, o_left, o_own,
    ext, ux, uy, uz, mm, mux, muy, muz, mig, mrhs, mc, cx_, cy_, cz_, cg, tmp32, tmp16,
):
    lane = lane_of((CY, CZ))
    lane8 = lane_of((8, CZ))

    def assemble(f, _):
        for b, brick in enumerate((xl, x0, xr)):
            parts = (
                (0, 8, lambda p: yl[f, GYX * b + p], lane8),
                (8, CY, lambda p: brick[f, p], lane),
                (8 + CY, 8, lambda p: yr[f, GYX * b + p], lane8),
            )
            for start, rows, get, at in parts:
                from_left, from_right = get(CX), get(CX + 1)
                for p in range(CX):
                    v = get(p)
                    le = pltpu.roll(from_left, (CZ - ZH - ZH * p) % CZ, 1) if p < 7 else from_left
                    ri = pltpu.roll(from_right, CZ - ZH * p, 1) if p else from_right
                    ext[f, CX * b + p, start : start + rows, 0:CZ] = v
                    ext[f, CX * b + p, start : start + rows, CZ:LANES] = jnp.where(
                        at < ZH, ri, jnp.where(at >= CZ - ZH, le, v)
                    )
        return 0

    lax.fori_loop(0, FIELDS, assemble, 0)

    lo_x, hi_x, lo_y, hi_y, lo_z, hi_z = (ends[i] for i in range(6))
    shape = (ROWS, LANES)
    row = lax.broadcasted_iota(jnp.int32, shape, 0)
    col = lane_of(shape)
    half_y = jnp.where(((row == 7) & (lo_y == 1)) | ((row == 7 + CY) & (hi_y == 1)), 0.0, 0.5)
    half_z = jnp.where(((col == LANES - 1) & (lo_z == 1)) | ((col == CZ - 1) & (hi_z == 1)), 0.0, 0.5)

    def links(p, _):
        here = ext[0, p]
        cut = ((p == 7) & (lo_x == 1)) | ((p == 7 + CX) & (hi_x == 1))
        ux[p] = jnp.where(cut, 0.0, 0.5) * (here + ext[0, jnp.minimum(p + 1, PLANES - 1)])
        uy[p] = half_y * (here + after(here, 1, 0))
        uz[p] = half_z * (here + after(here, 1, 1))
        return 0

    lax.fori_loop(0, PLANES, links, 0)

    def smooth(p, _):
        g = 0.1 * ext[0, p] + ux[p] + ux[p - 1]
        g = g + uy[p] + before(uy[p], 1, 0) + uz[p] + before(uz[p], 1, 1)
        ig = damping / g
        for c in range(3):
            mm[c, p] = ext[4 + c, p] * ext[1 + c, p] * ig

        @pl.when((p >= 6) & (p < 18))
        def _():
            o_ig[p - 6] = ig
            o_ux[p - 6] = ux[p]
            o_uy[p - 6] = uy[p]
            o_uz[p - 6] = uz[p]
            for c in range(3):
                o_r[c, p - 6] = ext[1 + c, p]
                o_free[c, p - 6] = ext[4 + c, p]

        return 0

    lax.fori_loop(1, PLANES - 1, smooth, 0)

    def mid_links(q, _):
        p = 2 * q
        a, b = restrict_rows(tmp32, ux[p + 1])
        mux[q] = pair_sum(a + b, 1)
        _, b = restrict_rows(tmp32, uy[p] + uy[p + 1])
        muy[q] = pair_sum(b, 1)
        a, b = restrict_rows(tmp32, uz[p] + uz[p + 1])
        muz[q] = odd_group(a + b, 1)
        a, b = restrict_rows(tmp32, ext[0, p] + ext[0, p + 1])
        mig[q] = 0.1 * pair_sum(a + b, 1)
        return 0

    lax.fori_loop(0, 12, mid_links, 0)

    def mid_rhs(q, _):
        p = 2 * q
        g = mig[q] + mux[q] + mux[q - 1]
        g = g + muy[q] + before(muy[q], 1, 0) + muz[q] + before(muz[q], 2, 1)
        ig = damping / g
        for c in range(3):
            total = jnp.zeros(shape, F32)
            for i in range(2):
                near = neighbours(ux[p + i], ux[p + i - 1], uy[p + i], uz[p + i], mm[c, p + i], mm[c, p + i - 1], mm[c, p + i + 1], 1)
                total = total + keep * ext[1 + c, p + i] + ext[4 + c, p + i] * near
            a, b = restrict_rows(tmp32, total)
            rhs = pair_sum(a + b, 1)
            mrhs[c, q] = rhs
            mc[c, q] = ig * rhs

        @pl.when((q >= 2) & (q < 10))
        def _():
            o_mig[q - 2] = ig
            o_mux[q - 2] = mux[q]
            o_muy[q - 2] = muy[q]
            o_muz[q - 2] = muz[q]
            for c in range(3):
                o_mc[c, q - 2] = mc[c, q]

        return 0

    lax.fori_loop(1, 11, mid_rhs, 0)

    for s in range(5):
        q = 2 * s
        a, b = restrict_rows(tmp16, mux[q + 1])
        cx_[s] = pair_sum(a + b, 2)
        _, b = restrict_rows(tmp16, muy[q] + muy[q + 1])
        cy_[s] = pair_sum(b, 2)
        a, b = restrict_rows(tmp16, muz[q] + muz[q + 1])
        cz_[s] = odd_group(a + b, 2)
        a, b = restrict_rows(tmp16, mig[q] + mig[q + 1])
        cg[s] = pair_sum(a + b, 2)

    quad = lane_of((8, LANES)) % 4
    for s in range(1, 5):
        g = cg[s] + cx_[s] + cx_[s - 1]
        g = g + cy_[s] + before(cy_[s], 1, 0) + cz_[s] + before(cz_[s], 4, 1)
        rhs = []
        for c in range(3):
            total = jnp.zeros((ROWS // 2, LANES), F32)
            for q in (2 * s, 2 * s + 1):
                near = neighbours(mux[q], mux[q - 1], muy[q], muz[q], mc[c, q], mc[c, q - 1], mc[c, q + 1], 2)
                total = total + keep * mrhs[c, q] + near
            a, b = restrict_rows(tmp16, total)
            rhs.append(pair_sum(a + b, 2))
        first = jnp.where(quad == 0, rhs[0], jnp.where(quad == 1, rhs[1], jnp.where(quad == 2, rhs[2], g)))
        second = jnp.where(quad == 0, cx_[s], jnp.where(quad == 1, cy_[s], cz_[s]))
        for i, v in enumerate((first, second)):
            if s <= 3:
                o_right[i, s - 1] = v
            if s >= 2:
                o_left[i, s - 2] = v
            if s in (2, 3):
                o_own[i, s - 2] = v


def turn_kernel(xl, own, xr, up, down):
    for i in range(2):
        for s in range(8):
            for j in range(3):
                for out, first in ((up, 3), (down, 2)):
                    at = slice(first + j, first + j + 1)
                    src = xl[i, s, at] if s < 3 else own[i, s - 3, at] if s < 5 else xr[i, s - 5, at]
                    out[i, j, s : s + 1] = src


def solve_kernel(
    xl, own, xr, yl, yr, r, free, ux, uy, uz, ig, mc, mux, muy, muz, mig,
    direction, image, sums,
    packed, cc, pm, pf, m1, base, d, tmp16,
):
    quad = lane_of((16, LANES)) % 4
    field = [[None] * 8 for _ in range(7)]
    for i in range(2):
        for s in range(8):
            packed[...] = jnp.zeros((16, LANES), F32)
            packed[4:8] = xl[i, s, 2:6] if s < 3 else own[i, s - 3, 2:6] if s < 5 else xr[i, s - 5, 2:6]
            for j in range(3):
                packed[1 + j : 2 + j] = yl[i, j, s : s + 1]
                packed[8 + j : 9 + j] = yr[i, j, s : s + 1]
            v = packed[...]
            for k in range(4 if i == 0 else 3):
                field[4 * i + k][s] = pair_sum(pair_sum(jnp.where(quad == k, v, 0.0), 1), 2)
    g = [jnp.where(v > 0.0, v, 1.0) for v in field[3]]
    inv = [1.0 / v for v in g]
    cx_, cy_, cz_ = field[4], field[5], field[6]
    ratio = eig_center / eig_halfwidth
    q0 = 1.0 / ratio
    q1 = 1.0 / (2.0 * ratio - q0)
    q2 = 1.0 / (2.0 * ratio - q1)
    for c in range(3):
        rhs = field[c]
        update = [rhs[s] * inv[s] * (1.0 / eig_center) for s in range(8)]
        iterate = list(update)
        for q_old, q_new, lo, hi in ((q0, q1, 1, 7), (q1, q2, 2, 6)):
            new = list(iterate)
            for s in range(lo, hi):
                near = neighbours(cx_[s], cx_[s - 1], cy_[s], cz_[s], iterate[s], iterate[s - 1], iterate[s + 1], 4)
                rest = rhs[s] - g[s] * iterate[s] + near
                update[s] = (q_new * q_old) * update[s] + (2.0 * q_new / eig_halfwidth) * (rest * inv[s])
                new[s] = iterate[s] + update[s]
            iterate = new
        for s in range(4):
            tmp16[...] = iterate[2 + s]
            v = tmp16[2:10]
            v = repeat_rows(cc, v)
            pm[c, 2 * s] = mc[c, 2 * s] + v
            pm[c, 2 * s + 1] = mc[c, 2 * s + 1] + v

    def mid(q, _):
        for c in range(3):
            near = neighbours(mux[q], mux[q - 1], muy[q], muz[q], pm[c, q], pm[c, q - 1], pm[c, q + 1], 2)
            v = keep * pm[c, q] + mc[c, q] + mig[q] * near
            v = repeat_rows(pf, v)
            for i in range(2):
                p = 2 * (q - 1) + i
                fr = free[c, p]
                fc = r[c, p] * (fr * ig[p] + damping * (1.0 - fr))
                corr = fc + v
                m1[c, p] = fr * corr
                base[c, p] = keep * corr + fc
        return 0

    lax.fori_loop(1, 7, mid, 0)

    def fine(p, _):
        for c in range(3):
            near = neighbours(ux[p], ux[p - 1], uy[p], uz[p], m1[c, p], m1[c, p - 1], m1[c, p + 1], 1)
            d[c, p] = base[c, p] + free[c, p] * ig[p] * near
        return 0

    lax.fori_loop(1, 11, fine, 0)

    mine = slice(8, 8 + CY)

    def last(p, total):
        first, second = total
        for c in range(3):
            here = free[c, p] * d[c, p]
            prev = free[c, p - 1] * d[c, p - 1]
            nxt = free[c, p + 1] * d[c, p + 1]
            near = neighbours(ux[p], ux[p - 1], uy[p], uz[p], here, prev, nxt, 1)
            fr = free[c, p]
            im = fr * (damping / ig[p] * d[c, p] - near) + (1.0 - fr) * d[c, p]
            im = im[mine, 0:CZ]
            dd = d[c, p, mine, 0:CZ]
            direction[c, p - 2] = dd
            image[c, p - 2] = im
            first = first + r[c, p, mine, 0:CZ] * dd
            second = second + dd * im
        return first, second

    zero = jnp.zeros((CY, CZ), F32)
    first, second = lax.fori_loop(2, 10, last, (zero, zero))
    sums[0:1] = jnp.sum(first, axis=0, keepdims=True)
    sums[1:2] = jnp.sum(second, axis=0, keepdims=True)


def ring(count, step):
    return [(i, (i + step) % count) for i in range(count)]


def all_sum(v, axes):
    n = 1
    for axis in axes:
        n *= lax.axis_size(axis)
    sent = jnp.broadcast_to(v[None], (n,) + v.shape)
    return lax.all_to_all(sent, axes, 0, 0).sum(axis=0)


def shards(solution, residual, density_bins, fixed_dofs):
    nx, nc, nz = lax.axis_size("gx"), lax.axis_size("gc"), lax.axis_size("gz")
    ny = 2 * nc
    y_axes = ("gc", "co")
    ix, iz = lax.axis_index("gx"), lax.axis_index("gz")
    iy = 2 * lax.axis_index("gc") + lax.axis_index("co")
    ends = jnp.stack([ix == 0, ix == nx - 1, iy == 0, iy == ny - 1, iz == 0, iz == nz - 1]).astype(jnp.int32)

    def both(v, axes, count):
        up, down = v if isinstance(v, tuple) else (v, v)
        return lax.ppermute(up, axes, ring(count, 1)), lax.ppermute(down, axes, ring(count, -1))

    main, to_right, to_left = call(gather_kernel, [(FIELDS, CX, CY, CZ), (FIELDS, CY, CZ), (FIELDS, CY, CZ)])(
        density_bins, residual, fixed_dofs
    )
    zl, zr = both((to_right, to_left), "gz", nz)
    x0 = jnp.concatenate([main, zl[:, None], zr[:, None]], axis=1)
    xl, xr = both(x0, "gx", nx)
    wide = [xl, x0, xr]
    yl, yr = both(
        (
            jnp.concatenate([v[:, :, 8:16] for v in wide], axis=1),
            jnp.concatenate([v[:, :, 0:8] for v in wide], axis=1),
        ),
        y_axes,
        ny,
    )

    full = (12, ROWS, LANES)
    half = (8, ROWS // 2, LANES)
    all_f = (PLANES, ROWS, LANES)
    all_m = (12, ROWS // 2, LANES)
    outs = [(3,) + full, (3,) + full, full, full, full, full, (3,) + half, half, half, half, half]
    outs += [(2, 3, 8, LANES), (2, 3, 8, LANES), (2, 2, 8, LANES)]
    scratch = [(FIELDS,) + all_f, all_f, all_f, all_f, (3,) + all_f, all_m, all_m, all_m, all_m, (3,) + all_m, (3,) + all_m]
    scratch += [(5, 8, LANES)] * 4 + [(2, ROWS, CZ), (2, ROWS // 2, CZ)]
    fine = pl.pallas_call(
        fine_kernel,
        out_shape=[jax.ShapeDtypeStruct(s, F32) for s in outs],
        in_specs=[SMEM] + [VMEM] * 5,
        out_specs=[VMEM] * len(outs),
        scratch_shapes=[pltpu.VMEM(s, F32) for s in scratch],
        compiler_params=pltpu.CompilerParams(vmem_limit_bytes=48 * 1024 * 1024),
    )(ends, x0, xl, xr, yl, yr)
    kept, (to_right, to_left, own) = fine[:-3], fine[-3:]
    cl, cr = both((to_right, to_left), "gx", nx)
    up, down = call(turn_kernel, [(2, 3, 8, LANES)] * 2)(cl, own, cr)
    dl, dr = both((up, down), y_axes, ny)
    direction, image, sums = call(
        solve_kernel,
        [(3, CX, CY, CZ), (3, CX, CY, CZ), (2, CZ)],
        [(16, LANES), (2, ROWS // 2, CZ), (3,) + half, (2, ROWS, CZ), (3,) + full, (3,) + full, (3,) + full, (16, LANES)],
    )(cl, own, cr, dl, dr, *kept)
    sums = jnp.broadcast_to(jnp.sum(sums, axis=1)[:, None, None], (2, 4, CZ)).reshape(8, CZ)
    sums = all_sum(all_sum(sums, ("gc", "gz")), ("gx", "co"))
    alpha = sums[0, 0] / sums[4, 0]
    return (solution + alpha * direction, residual - alpha * image, direction)


def solution(mesh):
    nx, ny, nz = mesh.devices.shape
    split = Mesh(mesh.devices.reshape(nx, ny // 2, 2, nz), ("gx", "gc", "co", "gz"))
    field = P(None, "gx", ("gc", "co"), "gz")
    return jax.shard_map(
        shards,
        mesh=split,
        in_specs=(field, field, P("gx", ("gc", "co"), "gz"), field),
        out_specs=(field, field, field),
        check_vma=False,
    )
```

time: 389 us -> 140 us (0.36); the launches traced: 383 us -> 140 us
  starting transfers between devices: 153 us -> 35.5 us
  blocking collectives: 120 us -> 38.9 us
  waiting for transfers between devices: 58.6 us -> 32.1 us
  local copies, waits for them, and re-layouts: 29.7 us -> 6.22 us
  Pallas kernels: 0 us -> 20.8 us
  other arithmetic: 18.6 us -> 3.95 us
    psum x1 -> x0, blocking collectives: 120 us -> none  [shards(): precond_inner = lax.psum(jnp.sum(residual * direction), ('gx', 'gy', 'gz'))]
    ppermute x48 -> x10, starting transfers between devices: 153 us -> 35.5 us  [the longest x5 22.1 us: both(): lax.ppermute(down, axes, ring(count, -1))]
    all_to_all x0 -> x2, blocking collectives: none -> 38.9 us  [all_sum(): return lax.all_to_all(sent, axes, 0, 0).sum(axis=0)]
    ppermute x48 -> x10, waiting for transfers between devices: 58.6 us -> 32.1 us  [the longest x5 17.1 us: both(): lax.ppermute(down, axes, ring(count, -1))]
    pallas_call x0 -> x4, Pallas kernels: none -> 20.8 us  [the longest x1 12.4 us: shards(): pl.pallas_call(fine_kernel, out_shape=[jax.ShapeDtypeStruct(s, F32) for s...]
    reshape x6 -> x0, local copies, waits for them, and re-layouts: 16.6 us -> none  [the longest x2 15.5 us: restrict(): field.reshape(channels, size_x // 2, 2, size_y // 2, 2, size_z // 2, 2)]
    reduce_sum x17 -> x3, other arithmetic: 12.7 us -> 0.18 us  [the longest x1 0.12 us: shards(): jnp.sum(sums, axis=1)[:, None, None]]
    another operation x2 -> x1, local copies, waits for them, and re-layouts: 6.05 us -> 0.1 us  [shards(): jnp.stack([ix == 0, ix == nx - 1, iy == 0, iy == ny - 1, iz == 0, iz == n...]
  transfers between devices with their start and end apart: 48 -> 10, of which waited for: 29 -> 8; matrix products, arithmetic and copies ran while one was open for 5% -> 1% of each run, Pallas kernels for 0% -> 0%
where the time goes in v1:
time: 140 us
  blocking collectives  38.9 us (28%)
  starting transfers between devices  35.5 us (25%)
  waiting for transfers between devices  32.1 us (23%)
  Pallas kernels  20.8 us (15%)
  local copies, waits for them, and re-layouts  6.22 us (4%)
  other arithmetic  3.95 us (3%)
  between operations  2.11 us (2%)
    all_to_all x2, blocking collectives, all_sum(): return lax.all_to_all(sent, axes, 0, 0).sum(axis=0)  38.9 us
    ppermute x5, starting transfers between devices, both(): lax.ppermute(down, axes, ring(count, -1))  22.1 us
    ppermute x5, waiting for transfers between devices, both(): lax.ppermute(down, axes, ring(count, -1))  17.1 us
    ppermute x5, waiting for transfers between devices, both(): lax.ppermute(up, axes, ring(count, 1))  15 us
    ppermute x5, starting transfers between devices, both(): lax.ppermute(up, axes, ring(count, 1))  13.4 us
    pallas_call x1, Pallas kernels, shards(): pl.pallas_call(fine_kernel, out_shape=[jax.ShapeDtypeStruct(s, F32) for s...  12.4 us
    pallas_call x1, Pallas kernels, shards(): call(solve_kernel, [(3, CX, CY, CZ), (3, CX, CY, CZ), (2, CZ)], [(16, LAN...  8.07 us
    unnamed x14, local copies, waits for them, and re-layouts  5.24 us
  transfers between devices with their start and end apart: 10, of which 8 were waited for; matrix products, arithmetic and copies ran while one was open for 1% of the time, Pallas kernels for 0%

profile of v1, /device:TPU:1, one launch (start us, length us, event | category | flops | bytes accessed | tf_op | source)
XLA Modules:
  0.0 139.5 jit_solution(8613326669444190165)
XLA Ops:
  0.6 0.0 copy-start.2
  0.6 0.9 copy-done.2
  1.6 0.0 copy-start.4
  1.6 0.9 copy-done.4
  2.5 0.0 copy-start.5
  2.5 0.8 copy-done.5
  3.3 0.3 shard_map.67
  3.6 3.9 %collective-permute-start = (f32[7,16,128]{2,1,0:T(8,128)S(1)}, f32[7,16,128]{2,1,0:T(8,128)S(1)}, u32[]{:S(2)}, u32[]{:S(2)}) collective-permute-start(f32[7,16,128]{2,1,0:T(8,128)S(1)} %get-tuple-element.26), channel_id=1, source_target_pairs={{0,1},{1,2},{2,3},{3,0},{4,5},{5,6},{6,7},{7,4},{8,9},{9,10},{10,1... | collective-permute-start | bytes 172040 | tf_op jit(solution)/shard_map/ppermute | solution.py:379
  7.6 3.2 %collective-permute-start.1 = (f32[7,16,128]{2,1,0:T(8,128)S(1)}, f32[7,16,128]{2,1,0:T(8,128)S(1)}, u32[]{:S(2)}, u32[]{:S(2)}) collective-permute-start(f32[7,16,128]{2,1,0:T(8,128)S(1)} %get-tuple-element.27), channel_id=1, source_target_pairs={{0,3},{1,0},{2,1},{3,2},{4,7},{5,4},{6,5},{7,6},{8,11},{9,8},{10,9... | collective-permute-start | bytes 172040 | tf_op jit(solution)/shard_map/ppermute | solution.py:379
  10.8 0.0 collective-permute-done
  10.8 1.7 %collective-permute-done.1 = f32[7,16,128]{2,1,0:T(8,128)S(1)} collective-permute-done((f32[7,16,128]{2,1,0:T(8,128)S(1)}, f32[7,16,128]{2,1,0:T(8,128)S(1)}, u32[]{:S(2)}, u32[]{:S(2)}) %collective-permute-start.1) | collective-permute-done | bytes 57376 | tf_op jit(solution)/shard_map/ppermute | solution.py:379
  12.5 14.3 %collective-permute-start.3 = (f32[7,10,16,128]{3,2,1,0:T(8,128)S(1)}, f32[7,10,16,128]{3,2,1,0:T(8,128)S(1)}, u32[]{:S(2)}, u32[]{:S(2)}) collective-permute-start(f32[7,10,16,128]{3,2,1,0:T(8,128)S(1)} %pad_maximum_fusion.2.x0), channel_id=1, source_target_pairs={{0,704},{64,0},{128,64},{192,128},{256,192},{320,256},{384,320},{4... | collective-permute-start | bytes 1720328 | tf_op jit(solution)/shard_map/ppermute | solution.py:379
  26.9 1.9 %collective-permute-start.2 = (f32[7,10,16,128]{3,2,1,0:T(8,128)S(1)}, f32[7,10,16,128]{3,2,1,0:T(8,128)S(1)}, u32[]{:S(2)}, u32[]{:S(2)}) collective-permute-start(f32[7,10,16,128]{3,2,1,0:T(8,128)S(1)} %pad_maximum_fusion.2.x0), channel_id=1, source_target_pairs={{0,64},{64,128},{128,192},{192,256},{256,320},{320,384},{384,448},... | collective-permute-start | bytes 1720328 | tf_op jit(solution)/shard_map/ppermute | solution.py:379
  28.8 8.2 %collective-permute-done.3.xr = f32[7,10,16,128]{3,2,1,0:T(8,128)S(1)} collective-permute-done((f32[7,10,16,128]{3,2,1,0:T(8,128)S(1)}, f32[7,10,16,128]{3,2,1,0:T(8,128)S(1)}, u32[]{:S(2)}, u32[]{:S(2)}) %collective-permute-start.3) | collective-permute-done | bytes 573472 | tf_op jit(solution)/shard_map/ppermute | solution.py:379
  37.0 5.0 %collective-permute-done.2.xl = f32[7,10,16,128]{3,2,1,0:T(8,128)S(1)} collective-permute-done((f32[7,10,16,128]{3,2,1,0:T(8,128)S(1)}, f32[7,10,16,128]{3,2,1,0:T(8,128)S(1)}, u32[]{:S(2)}, u32[]{:S(2)}) %collective-permute-start.2) | collective-permute-done | bytes 573472 | tf_op jit(solution)/shard_map/ppermute | solution.py:379
  42.1 1.0 pad_maximum_fusion
  43.1 4.5 %collective-permute-start.4 = (f32[7,30,8,128]{3,2,1,0:T(8,128)}, f32[7,30,8,128]{3,2,1,0:T(8,128)S(1)}, u32[]{:S(2)}, u32[]{:S(2)}) collective-permute-start(f32[7,30,8,128]{3,2,1,0:T(8,128)} %pad_maximum_fusion), channel_id=1, source_target_pairs={{0,4},{4,8},{8,12},{12,16},{16,20},{20,24},{24,28},{28,32},{32,36}... | collective-permute-start | bytes 2580488 | tf_op jit(solution)/shard_map/ppermute | solution.py:379
  47.6 1.0 pad_maximum_fusion.1
  48.6 0.0 collective-permute-start.5
  48.6 0.1 stack.27
  48.7 8.9 %collective-permute-done.4.yl = f32[7,30,8,128]{3,2,1,0:T(8,128)S(1)} collective-permute-done((f32[7,30,8,128]{3,2,1,0:T(8,128)}, f32[7,30,8,128]{3,2,1,0:T(8,128)S(1)}, u32[]{:S(2)}, u32[]{:S(2)}) %collective-permute-start.4) | collective-permute-done | bytes 860192 | tf_op jit(solution)/shard_map/ppermute | solution.py:379
  57.6 3.4 %collective-permute-done.5.yr = f32[7,30,8,128]{3,2,1,0:T(8,128)S(1)} collective-permute-done((f32[7,30,8,128]{3,2,1,0:T(8,128)}, f32[7,30,8,128]{3,2,1,0:T(8,128)S(1)}, u32[]{:S(2)}, u32[]{:S(2)}) %collective-permute-start.5) | collective-permute-done | bytes 860192 | tf_op jit(solution)/shard_map/ppermute | solution.py:379
  61.0 12.4 %shard_map.68 = (f32[3,12,32,256]{3,2,1,0:T(8,128)}, f32[3,12,32,256]{3,2,1,0:T(8,128)}, f32[12,32,256]{2,1,0:T(8,128)S(1)}, f32[12,32,256]{2,1,0:T(8,128)S(1)},...) custom-call(s32[6]{0:T(128)S(1)} %convert_element_type.3.ends, ...), custom_call_target="tpu_custom_call" | custom-call | tf_op jit(solution)/shard_map/pallas_call | solution.py:405
  73.4 1.9 %collective-permute-start.6 = (f32[2,3,8,256]{3,2,1,0:T(8,128)S(1)}, f32[2,3,8,256]{3,2,1,0:T(8,128)S(1)}, u32[]{:S(2)}, u32[]{:S(2)}) collective-permute-start(f32[2,3,8,256]{3,2,1,0:T(8,128)S(1)} %get-tuple-element.28), channel_id=1, source_target_pairs={{0,64},{64,128},{128,192},{192,256},{256,320},{320,384},{384,448},... | collective-permute-start | bytes 147464 | tf_op jit(solution)/shard_map/ppermute | solution.py:379
  75.3 4.6 %collective-permute-start.7 = (f32[2,3,8,256]{3,2,1,0:T(8,128)S(1)}, f32[2,3,8,256]{3,2,1,0:T(8,128)S(1)}, u32[]{:S(2)}, u32[]{:S(2)}) collective-permute-start(f32[2,3,8,256]{3,2,1,0:T(8,128)S(1)} %get-tuple-element.30), channel_id=1, source_target_pairs={{0,704},{64,0},{128,64},{192,128},{256,192},{320,256},{384,320},{4... | collective-permute-start | bytes 147464 | tf_op jit(solution)/shard_map/ppermute | solution.py:379
  79.9 0.0 collective-permute-done.6.xl
  79.9 1.1 collective-permute-done.7.xr
  81.1 1.1 collective-permute-start.8
  82.2 0.1 collective-permute-start.9
  82.2 1.1 collective-permute-done.8.yl
  83.4 2.6 %collective-permute-done.9.yr = f32[2,3,8,256]{3,2,1,0:T(8,128)S(1)} collective-permute-done((f32[2,3,8,256]{3,2,1,0:T(8,128)S(1)}, f32[2,3,8,256]{3,2,1,0:T(8,128)S(1)}, u32[]{:S(2)}, u32[]{:S(2)}) %collective-permute-start.9) | collective-permute-done | bytes 49184 | tf_op jit(solution)/shard_map/ppermute | solution.py:379
  86.0 0.0 copy-start
  86.0 1.3 copy-done
  87.3 0.0 copy-start.1
  87.3 1.3 copy-done.1
  88.5 0.0 copy-start.3
  88.5 0.0 copy-start.6
  88.5 8.1 %shard_map.70 = (f32[3,8,16,128]{3,2,1,0:T(8,128)}, f32[3,8,16,128]{3,2,1,0:T(8,128)S(1)}, f32[2,128]{1,0:T(2,128)S(1)}) custom-call(f32[2,3,8,256]{3,2,1,0:T(8,128)S(1)} %collective-permute-done.6.xl, f32[2,2,8,256]{3,2,1,0:T(8,128)S(1)} %get-tuple-element.29.own, f32[2,3,8,256]{3,2,1,0:T(8,128)S(1)} %collective-permute-done.7.xr, ...), custom_call_target="tpu_custom_call" | custom-call | tf_op jit(solution)/shard_map/pallas_call | solution.py:417
  96.6 0.1 reduce_sum.27
  96.7 0.1 broadcast_in_dim.27
  96.8 0.1 broadcast_in_dim.28
  96.9 0.1 broadcast_in_dim.29
  97.0 20.4 %all_to_all.10 = f32[32,8,128]{2,1,0:T(8,128)S(1)} all-to-all(f32[32,8,128]{2,1,0:T(8,128)S(1)} %broadcast_in_dim.29), channel_id=1, replica_groups=mesh['gx'=12,'gc'=8,'co'=2,'gz'=4] {'gc','gz'}, dimensions={0} | all-to-all | bytes 262144 | tf_op jit(solution)/shard_map/all_to_all | solution.py:366
  117.4 18.5 %all_to_all.11 = f32[24,8,128]{2,1,0:T(8,128)S(1)} all-to-all(f32[24,8,128]{2,1,0:T(8,128)S(1)} %broadcast_in_dim.30), channel_id=1, replica_groups=mesh['gx'=12,'gc'=8,'co'=2,'gz'=4] {'gx','co'}, dimensions={0} | all-to-all | bytes 196608 | tf_op jit(solution)/shard_map/all_to_all | solution.py:366
  135.9 0.5 fusion.3
  137.8 0.0 copy-done.3
  137.8 0.0 copy-done.6
  137.8 1.7 %multiply_subtract_fusion = (f32[3,8,16,128]{3,2,1,0:T(8,128)}, f32[3,8,16,128]{3,2,1,0:T(8,128)}) fusion(f32[3,8,16,128]{3,2,1,0:T(8,128)S(1)} %copy-done.3, f32[3,8,16,128]{3,2,1,0:T(8,128)S(1)} %get-tuple-element.46, f32[]{:T(128)} %bitcast.8, f32[3,8,16,128]{3,2,1,0:T(8,128)S(1)} %copy-done.6, f32[3,8,16,128]{3,2,1,0:T(8,128)} %get-tuple-element.24), kind=kLoop, calls=%fused_computation.3 | loop fusion | flops 196608 | bytes 1179652 | tf_op jit(solution)/shard_map/sub | solution.py:425
  (9 shorter events, 0.3 us)
Async XLA Ops:
  0.6 0.9 copy-start.2
  1.6 0.9 copy-start.4
  2.5 0.8 copy-start.5
  3.6 7.2 %collective-permute-start = (f32[7,16,128]{2,1,0:T(8,128)S(1)}, f32[7,16,128]{2,1,0:T(8,128)S(1)}, u32[]{:S(2)}, u32[]{:S(2)}) collective-permute-start(f32[7,16,128]{2,1,0:T(8,128)S(1)} %get-tuple-element.26), channel_id=1, source_target_pairs={{0,1},{1,2},{2,3},{3,0},{4,5},{5,6},{6,7},{7,4},{8,9},{9,10},{10,1... | collective-permute-start | bytes 172040 | tf_op jit(solution)/shard_map/ppermute | solution.py:379
  7.6 4.9 %collective-permute-start.1 = (f32[7,16,128]{2,1,0:T(8,128)S(1)}, f32[7,16,128]{2,1,0:T(8,128)S(1)}, u32[]{:S(2)}, u32[]{:S(2)}) collective-permute-start(f32[7,16,128]{2,1,0:T(8,128)S(1)} %get-tuple-element.27), channel_id=1, source_target_pairs={{0,3},{1,0},{2,1},{3,2},{4,7},{5,4},{6,5},{7,6},{8,11},{9,8},{10,9... | collective-permute-start | bytes 172040 | tf_op jit(solution)/shard_map/ppermute | solution.py:379
  12.5 24.5 %collective-permute-start.3 = (f32[7,10,16,128]{3,2,1,0:T(8,128)S(1)}, f32[7,10,16,128]{3,2,1,0:T(8,128)S(1)}, u32[]{:S(2)}, u32[]{:S(2)}) collective-permute-start(f32[7,10,16,128]{3,2,1,0:T(8,128)S(1)} %pad_maximum_fusion.2.x0), channel_id=1, source_target_pairs={{0,704},{64,0},{128,64},{192,128},{256,192},{320,256},{384,320},{4... | collective-permute-start | bytes 1720328 | tf_op jit(solution)/shard_map/ppermute | solution.py:379
  26.9 15.2 %collective-permute-start.2 = (f32[7,10,16,128]{3,2,1,0:T(8,128)S(1)}, f32[7,10,16,128]{3,2,1,0:T(8,128)S(1)}, u32[]{:S(2)}, u32[]{:S(2)}) collective-permute-start(f32[7,10,16,128]{3,2,1,0:T(8,128)S(1)} %pad_maximum_fusion.2.x0), channel_id=1, source_target_pairs={{0,64},{64,128},{128,192},{192,256},{256,320},{320,384},{384,448},... | collective-permute-start | bytes 1720328 | tf_op jit(solution)/shard_map/ppermute | solution.py:379
  43.1 14.5 %collective-permute-start.4 = (f32[7,30,8,128]{3,2,1,0:T(8,128)}, f32[7,30,8,128]{3,2,1,0:T(8,128)S(1)}, u32[]{:S(2)}, u32[]{:S(2)}) collective-permute-start(f32[7,30,8,128]{3,2,1,0:T(8,128)} %pad_maximum_fusion), channel_id=1, source_target_pairs={{0,4},{4,8},{8,12},{12,16},{16,20},{20,24},{24,28},{28,32},{32,36}... | collective-permute-start | bytes 2580488 | tf_op jit(solution)/shard_map/ppermute | solution.py:379
  48.6 12.4 %collective-permute-start.5 = (f32[7,30,8,128]{3,2,1,0:T(8,128)}, f32[7,30,8,128]{3,2,1,0:T(8,128)S(1)}, u32[]{:S(2)}, u32[]{:S(2)}) collective-permute-start(f32[7,30,8,128]{3,2,1,0:T(8,128)} %pad_maximum_fusion.1), channel_id=1, source_target_pairs={{0,60},{4,0},{8,4},{12,8},{16,12},{20,16},{24,20},{28,24},{32,28},... | collective-permute-start | bytes 2580488 | tf_op jit(solution)/shard_map/ppermute | solution.py:379
  73.4 6.5 %collective-permute-start.6 = (f32[2,3,8,256]{3,2,1,0:T(8,128)S(1)}, f32[2,3,8,256]{3,2,1,0:T(8,128)S(1)}, u32[]{:S(2)}, u32[]{:S(2)}) collective-permute-start(f32[2,3,8,256]{3,2,1,0:T(8,128)S(1)} %get-tuple-element.28), channel_id=1, source_target_pairs={{0,64},{64,128},{128,192},{192,256},{256,320},{320,384},{384,448},... | collective-permute-start | bytes 147464 | tf_op jit(solution)/shard_map/ppermute | solution.py:379
  75.3 5.7 %collective-permute-start.7 = (f32[2,3,8,256]{3,2,1,0:T(8,128)S(1)}, f32[2,3,8,256]{3,2,1,0:T(8,128)S(1)}, u32[]{:S(2)}, u32[]{:S(2)}) collective-permute-start(f32[2,3,8,256]{3,2,1,0:T(8,128)S(1)} %get-tuple-element.30), channel_id=1, source_target_pairs={{0,704},{64,0},{128,64},{192,128},{256,192},{320,256},{384,320},{4... | collective-permute-start | bytes 147464 | tf_op jit(solution)/shard_map/ppermute | solution.py:379
  81.1 2.3 %collective-permute-start.8 = (f32[2,3,8,256]{3,2,1,0:T(8,128)S(1)}, f32[2,3,8,256]{3,2,1,0:T(8,128)S(1)}, u32[]{:S(2)}, u32[]{:S(2)}) collective-permute-start(f32[2,3,8,256]{3,2,1,0:T(8,128)S(1)} %get-tuple-element.31), channel_id=1, source_target_pairs={{0,4},{4,8},{8,12},{12,16},{16,20},{20,24},{24,28},{28,32},{32,36}... | collective-permute-start | bytes 147464 | tf_op jit(solution)/shard_map/ppermute | solution.py:379
  82.2 3.8 %collective-permute-start.9 = (f32[2,3,8,256]{3,2,1,0:T(8,128)S(1)}, f32[2,3,8,256]{3,2,1,0:T(8,128)S(1)}, u32[]{:S(2)}, u32[]{:S(2)}) collective-permute-start(f32[2,3,8,256]{3,2,1,0:T(8,128)S(1)} %get-tuple-element.32), channel_id=1, source_target_pairs={{0,60},{4,0},{8,4},{12,8},{16,12},{20,16},{24,20},{28,24},{32,28},... | collective-permute-start | bytes 147464 | tf_op jit(solution)/shard_map/ppermute | solution.py:379
  86.0 1.3 copy-start
  87.3 1.3 copy-start.1
  88.5 49.2 %copy-start.3 = (f32[3,8,16,128]{3,2,1,0:T(8,128)S(1)}, f32[3,8,16,128]{3,2,1,0:T(8,128)}, u32[]{:S(2)}) copy-start(f32[3,8,16,128]{3,2,1,0:T(8,128)} %residual.1) | copy-start | bytes 589828
  88.5 49.3 %copy-start.6 = (f32[3,8,16,128]{3,2,1,0:T(8,128)S(1)}, f32[3,8,16,128]{3,2,1,0:T(8,128)}, u32[]{:S(2)}) copy-start(f32[3,8,16,128]{3,2,1,0:T(8,128)} %param.4) | copy-start | bytes 589828

commit v2 on v1

--- a/solution.py
+++ b/solution.py
@@ -20,6 +20,7 @@
 ROWS = CY + 16
 PLANES = CX + 16
 ZH = 16
+LIMIT = 20 * 1024 * 1024
 FIELDS = 7
 GYX = CX + 2
 
@@ -33,7 +34,7 @@
         out_shape=[jax.ShapeDtypeStruct(s, F32) for s in outs],
         out_specs=[VMEM] * len(outs),
         scratch_shapes=[pltpu.VMEM(s, F32) for s in scratch],
-        compiler_params=pltpu.CompilerParams(vmem_limit_bytes=48 * 1024 * 1024),
+        compiler_params=pltpu.CompilerParams(vmem_limit_bytes=LIMIT),
     )
 
 
@@ -70,7 +71,13 @@
     )
 
 
-def gather_kernel(density, residual, fixed, main, to_right, to_left):
+def gather_kernel(density_in, residual_in, fixed_in, main, to_right, to_left, density, residual, fixed, sems):
+    pairs = ((density_in, density), (residual_in, residual), (fixed_in, fixed))
+    copies = [pltpu.make_async_copy(a, b, sems.at[i]) for i, (a, b) in enumerate(pairs)]
+    for copy in copies:
+        copy.start()
+    for copy in copies:
+        copy.wait()
     lane = lane_of((CY, CZ))
 
     def stage(field, values):
@@ -350,8 +357,8 @@
 
     zero = jnp.zeros((CY, CZ), F32)
     first, second = lax.fori_loop(2, 10, last, (zero, zero))
-    sums[0:1] = jnp.sum(first, axis=0, keepdims=True)
-    sums[1:2] = jnp.sum(second, axis=0, keepdims=True)
+    sums[0:1] = jnp.full((1, CZ), jnp.sum(first), F32)
+    sums[1:2] = jnp.full((1, CZ), jnp.sum(second), F32)
 
 
 def ring(count, step):
@@ -378,9 +385,20 @@
         up, down = v if isinstance(v, tuple) else (v, v)
         return lax.ppermute(up, axes, ring(count, 1)), lax.ppermute(down, axes, ring(count, -1))
 
-    main, to_right, to_left = call(gather_kernel, [(FIELDS, CX, CY, CZ), (FIELDS, CY, CZ), (FIELDS, CY, CZ)])(
-        density_bins, residual, fixed_dofs
-    )
+    shapes = [(FIELDS, CX, CY, CZ), (FIELDS, CY, CZ), (FIELDS, CY, CZ)]
+    main, to_right, to_left = pl.pallas_call(
+        gather_kernel,
+        out_shape=[jax.ShapeDtypeStruct(s, F32) for s in shapes],
+        in_specs=[pl.BlockSpec(memory_space=pltpu.HBM)] * 3,
+        out_specs=[VMEM] * 3,
+        scratch_shapes=[
+            pltpu.VMEM((CX, CY, CZ), jnp.int32),
+            pltpu.VMEM((3, CX, CY, CZ), F32),
+            pltpu.VMEM((3, CX, CY, CZ), jnp.int32),
+            pltpu.SemaphoreType.DMA((3,)),
+        ],
+        compiler_params=pltpu.CompilerParams(vmem_limit_bytes=LIMIT),
+    )(density_bins, residual, fixed_dofs)
     zl, zr = both((to_right, to_left), "gz", nz)
     x0 = jnp.concatenate([main, zl[:, None], zr[:, None]], axis=1)
     xl, xr = both(x0, "gx", nx)
@@ -408,7 +426,7 @@
         in_specs=[SMEM] + [VMEM] * 5,
         out_specs=[VMEM] * len(outs),
         scratch_shapes=[pltpu.VMEM(s, F32) for s in scratch],
-        compiler_params=pltpu.CompilerParams(vmem_limit_bytes=48 * 1024 * 1024),
+        compiler_params=pltpu.CompilerParams(vmem_limit_bytes=LIMIT),
     )(ends, x0, xl, xr, yl, yr)
     kept, (to_right, to_left, own) = fine[:-3], fine[-3:]
     cl, cr = both((to_right, to_left), "gx", nx)
@@ -419,9 +437,8 @@
         [(3, CX, CY, CZ), (3, CX, CY, CZ), (2, CZ)],
         [(16, LANES), (2, ROWS // 2, CZ), (3,) + half, (2, ROWS, CZ), (3,) + full, (3,) + full, (3,) + full, (16, LANES)],
     )(cl, own, cr, dl, dr, *kept)
-    sums = jnp.broadcast_to(jnp.sum(sums, axis=1)[:, None, None], (2, 4, CZ)).reshape(8, CZ)
     sums = all_sum(all_sum(sums, ("gc", "gz")), ("gx", "co"))
-    alpha = sums[0, 0] / sums[4, 0]
+    alpha = (sums[0] / sums[1])[None, None, None]
     return (solution + alpha * direction, residual - alpha * image, direction)
 
 

time: 140 us -> 133 us (0.950)
  local copies, waits for them, and re-layouts: 6.22 us -> 2.93 us
  blocking collectives: 38.9 us -> 36.1 us
    all_to_all x2, blocking collectives: 38.9 us -> 36.1 us  [all_sum(): return lax.all_to_all(sent, axes, 0, 0).sum(axis=0)]
    unnamed x14 -> x10, local copies, waits for them, and re-layouts: 5.24 us -> 2.69 us
where the time goes in v2:
time: 133 us; the launch traced here: 132 us
  blocking collectives  36.1 us (27%)
  starting transfers between devices  35.5 us (27%)
  waiting for transfers between devices  32.1 us (24%)
  Pallas kernels  21 us (16%)
  other arithmetic  3.85 us (3%)
  local copies, waits for them, and re-layouts  2.93 us (2%)
    all_to_all x2, blocking collectives, all_sum(): return lax.all_to_all(sent, axes, 0, 0).sum(axis=0)  36.1 us
    ppermute x5, starting transfers between devices, both(): lax.ppermute(down, axes, ring(count, -1))  22.1 us
    ppermute x5, waiting for transfers between devices, both(): lax.ppermute(down, axes, ring(count, -1))  17.1 us
    ppermute x5, waiting for transfers between devices, both(): lax.ppermute(up, axes, ring(count, 1))  15 us
    ppermute x5, starting transfers between devices, both(): lax.ppermute(up, axes, ring(count, 1))  13.4 us
    pallas_call x1, Pallas kernels, shards(): pl.pallas_call(fine_kernel, out_shape=[jax.ShapeDtypeStruct(s, F32) for s...  12 us
    pallas_call x1, Pallas kernels, shards(): call(solve_kernel, [(3, CX, CY, CZ), (3, CX, CY, CZ), (2, CZ)], [(16, LAN...  8.12 us
    unnamed x10, local copies, waits for them, and re-layouts  2.69 us
  transfers between devices with their start and end apart: 10, of which 8 were waited for; matrix products, arithmetic and copies ran while one was open for 1% of the time, Pallas kernels for 0%

profile of v2, /device:TPU:1, one launch (start us, length us, event | category | flops | bytes accessed | tf_op | source)
XLA Modules:
  0.0 132.2 jit_solution(4097224847728238513)
XLA Ops:
  0.6 0.0 copy-start
  0.6 0.9 copy-done
  1.6 0.0 copy-start.2
  1.6 0.9 copy-done.2
  2.5 0.0 copy-start.3
  2.5 0.8 copy-done.3
  3.3 0.9 shard_map.67
  4.2 3.9 %collective-permute-start = (f32[7,16,128]{2,1,0:T(8,128)S(1)}, f32[7,16,128]{2,1,0:T(8,128)S(1)}, u32[]{:S(2)}, u32[]{:S(2)}) collective-permute-start(f32[7,16,128]{2,1,0:T(8,128)S(1)} %get-tuple-element.26), channel_id=1, source_target_pairs={{0,1},{1,2},{2,3},{3,0},{4,5},{5,6},{6,7},{7,4},{8,9},{9,10},{10,1... | collective-permute-start | bytes 172040 | tf_op jit(solution)/shard_map/ppermute | solution.py:386
  8.2 3.2 %collective-permute-start.1 = (f32[7,16,128]{2,1,0:T(8,128)S(1)}, f32[7,16,128]{2,1,0:T(8,128)S(1)}, u32[]{:S(2)}, u32[]{:S(2)}) collective-permute-start(f32[7,16,128]{2,1,0:T(8,128)S(1)} %get-tuple-element.27), channel_id=1, source_target_pairs={{0,3},{1,0},{2,1},{3,2},{4,7},{5,4},{6,5},{7,6},{8,11},{9,8},{10,9... | collective-permute-start | bytes 172040 | tf_op jit(solution)/shard_map/ppermute | solution.py:386
  11.4 0.0 collective-permute-done
  11.4 1.7 %collective-permute-done.1 = f32[7,16,128]{2,1,0:T(8,128)S(1)} collective-permute-done((f32[7,16,128]{2,1,0:T(8,128)S(1)}, f32[7,16,128]{2,1,0:T(8,128)S(1)}, u32[]{:S(2)}, u32[]{:S(2)}) %collective-permute-start.1) | collective-permute-done | bytes 57376 | tf_op jit(solution)/shard_map/ppermute | solution.py:386
  13.1 14.3 %collective-permute-start.3 = (f32[7,10,16,128]{3,2,1,0:T(8,128)S(1)}, f32[7,10,16,128]{3,2,1,0:T(8,128)S(1)}, u32[]{:S(2)}, u32[]{:S(2)}) collective-permute-start(f32[7,10,16,128]{3,2,1,0:T(8,128)S(1)} %pad_maximum_fusion.2.x0), channel_id=1, source_target_pairs={{0,704},{64,0},{128,64},{192,128},{256,192},{320,256},{384,320},{4... | collective-permute-start | bytes 1720328 | tf_op jit(solution)/shard_map/ppermute | solution.py:386
  27.4 1.9 %collective-permute-start.2 = (f32[7,10,16,128]{3,2,1,0:T(8,128)S(1)}, f32[7,10,16,128]{3,2,1,0:T(8,128)S(1)}, u32[]{:S(2)}, u32[]{:S(2)}) collective-permute-start(f32[7,10,16,128]{3,2,1,0:T(8,128)S(1)} %pad_maximum_fusion.2.x0), channel_id=1, source_target_pairs={{0,64},{64,128},{128,192},{192,256},{256,320},{320,384},{384,448},... | collective-permute-start | bytes 1720328 | tf_op jit(solution)/shard_map/ppermute | solution.py:386
  29.4 8.2 %collective-permute-done.3.xr = f32[7,10,16,128]{3,2,1,0:T(8,128)S(1)} collective-permute-done((f32[7,10,16,128]{3,2,1,0:T(8,128)S(1)}, f32[7,10,16,128]{3,2,1,0:T(8,128)S(1)}, u32[]{:S(2)}, u32[]{:S(2)}) %collective-permute-start.3) | collective-permute-done | bytes 573472 | tf_op jit(solution)/shard_map/ppermute | solution.py:386
  37.6 5.0 %collective-permute-done.2.xl = f32[7,10,16,128]{3,2,1,0:T(8,128)S(1)} collective-permute-done((f32[7,10,16,128]{3,2,1,0:T(8,128)S(1)}, f32[7,10,16,128]{3,2,1,0:T(8,128)S(1)}, u32[]{:S(2)}, u32[]{:S(2)}) %collective-permute-start.2) | collective-permute-done | bytes 573472 | tf_op jit(solution)/shard_map/ppermute | solution.py:386
  42.7 1.0 pad_maximum_fusion
  43.6 4.5 %collective-permute-start.4 = (f32[7,30,8,128]{3,2,1,0:T(8,128)}, f32[7,30,8,128]{3,2,1,0:T(8,128)S(1)}, u32[]{:S(2)}, u32[]{:S(2)}) collective-permute-start(f32[7,30,8,128]{3,2,1,0:T(8,128)} %pad_maximum_fusion), channel_id=1, source_target_pairs={{0,4},{4,8},{8,12},{12,16},{16,20},{20,24},{24,28},{28,32},{32,36}... | collective-permute-start | bytes 2580488 | tf_op jit(solution)/shard_map/ppermute | solution.py:386
  48.1 1.0 pad_maximum_fusion.1
  49.2 0.0 collective-permute-start.5
  49.2 0.1 stack.27
  49.3 8.9 %collective-permute-done.4.yl = f32[7,30,8,128]{3,2,1,0:T(8,128)S(1)} collective-permute-done((f32[7,30,8,128]{3,2,1,0:T(8,128)}, f32[7,30,8,128]{3,2,1,0:T(8,128)S(1)}, u32[]{:S(2)}, u32[]{:S(2)}) %collective-permute-start.4) | collective-permute-done | bytes 860192 | tf_op jit(solution)/shard_map/ppermute | solution.py:386
  58.2 3.4 %collective-permute-done.5.yr = f32[7,30,8,128]{3,2,1,0:T(8,128)S(1)} collective-permute-done((f32[7,30,8,128]{3,2,1,0:T(8,128)}, f32[7,30,8,128]{3,2,1,0:T(8,128)S(1)}, u32[]{:S(2)}, u32[]{:S(2)}) %collective-permute-start.5) | collective-permute-done | bytes 860192 | tf_op jit(solution)/shard_map/ppermute | solution.py:386
  61.6 12.0 %shard_map.68 = (f32[3,12,32,256]{3,2,1,0:T(8,128)S(1)}, f32[3,12,32,256]{3,2,1,0:T(8,128)S(1)}, f32[12,32,256]{2,1,0:T(8,128)S(1)}, f32[12,32,256]{2,1,0:T(8,12...) custom-call(s32[6]{0:T(128)S(1)} %convert_element_type.3.ends, ...), custom_call_target="tpu_custom_call" | custom-call | tf_op jit(solution)/shard_map/pallas_call | solution.py:423
  73.6 1.9 %collective-permute-start.6 = (f32[2,3,8,256]{3,2,1,0:T(8,128)S(1)}, f32[2,3,8,256]{3,2,1,0:T(8,128)S(1)}, u32[]{:S(2)}, u32[]{:S(2)}) collective-permute-start(f32[2,3,8,256]{3,2,1,0:T(8,128)S(1)} %get-tuple-element.28), channel_id=1, source_target_pairs={{0,64},{64,128},{128,192},{192,256},{256,320},{320,384},{384,448},... | collective-permute-start | bytes 147464 | tf_op jit(solution)/shard_map/ppermute | solution.py:386
  75.5 4.6 %collective-permute-start.7 = (f32[2,3,8,256]{3,2,1,0:T(8,128)S(1)}, f32[2,3,8,256]{3,2,1,0:T(8,128)S(1)}, u32[]{:S(2)}, u32[]{:S(2)}) collective-permute-start(f32[2,3,8,256]{3,2,1,0:T(8,128)S(1)} %get-tuple-element.30), channel_id=1, source_target_pairs={{0,704},{64,0},{128,64},{192,128},{256,192},{320,256},{384,320},{4... | collective-permute-start | bytes 147464 | tf_op jit(solution)/shard_map/ppermute | solution.py:386
  80.1 0.0 collective-permute-done.6.xl
  80.1 1.1 collective-permute-done.7.xr
  81.3 1.1 collective-permute-start.8
  82.4 0.1 collective-permute-start.9
  82.4 1.1 collective-permute-done.8.yl
  83.5 2.6 %collective-permute-done.9.yr = f32[2,3,8,256]{3,2,1,0:T(8,128)S(1)} collective-permute-done((f32[2,3,8,256]{3,2,1,0:T(8,128)S(1)}, f32[2,3,8,256]{3,2,1,0:T(8,128)S(1)}, u32[]{:S(2)}, u32[]{:S(2)}) %collective-permute-start.9) | collective-permute-done | bytes 49184 | tf_op jit(solution)/shard_map/ppermute | solution.py:386
  86.2 0.0 copy-start.1
  86.2 0.0 copy-start.4
  86.2 8.1 %shard_map.70 = (f32[3,8,16,128]{3,2,1,0:T(8,128)}, f32[3,8,16,128]{3,2,1,0:T(8,128)S(1)}, f32[2,128]{1,0:T(2,128)S(1)}) custom-call(f32[2,3,8,256]{3,2,1,0:T(8,128)S(1)} %collective-permute-done.6.xl, f32[2,2,8,256]{3,2,1,0:T(8,128)S(1)} %get-tuple-element.29.own, f32[2,3,8,256]{3,2,1,0:T(8,128)S(1)} %collective-permute-done.7.xr, ...), custom_call_target="tpu_custom_call" | custom-call | tf_op jit(solution)/shard_map/pallas_call | solution.py:435
  94.3 19.2 %all_to_all.10 = f32[32,2,128]{2,1,0:T(2,128)S(1)} all-to-all(f32[32,2,128]{2,1,0:T(2,128)S(1)} %broadcast_in_dim.10), channel_id=1, replica_groups=mesh['gx'=12,'gc'=8,'co'=2,'gz'=4] {'gc','gz'}, dimensions={0} | all-to-all | bytes 65536 | tf_op jit(solution)/shard_map/all_to_all | solution.py:373
  113.6 16.8 %all_to_all.11 = f32[24,2,128]{2,1,0:T(2,128)S(1)} all-to-all(f32[24,2,128]{2,1,0:T(2,128)S(1)} %broadcast_in_dim.22), channel_id=1, replica_groups=mesh['gx'=12,'gc'=8,'co'=2,'gz'=4] {'gx','co'}, dimensions={0} | all-to-all | bytes 49152 | tf_op jit(solution)/shard_map/all_to_all | solution.py:373
  130.5 0.0 copy-done.1
  130.5 0.0 copy-done.4
  130.5 1.7 %multiply_subtract_fusion = (f32[3,8,16,128]{3,2,1,0:T(8,128)}, f32[3,8,16,128]{3,2,1,0:T(8,128)}) fusion(f32[3,8,16,128]{3,2,1,0:T(8,128)S(1)} %copy-done.1, f32[3,8,16,128]{3,2,1,0:T(8,128)S(1)} %get-tuple-element.46, f32[128]{0:T(128)S(1)} %fusion, f32[3,8,16,128]{3,2,1,0:T(8,128)S(1)} %copy-done.4, f32[3,8,16,128]{3,2,1,0:T(8,128)} %get-tuple-element.24), kind=kLoop, calls=%fused_computation.3 | loop fusion | flops 196608 | bytes 1180160 | tf_op jit(solution)/shard_map/sub | solution.py:442
  (11 shorter events, 0.3 us)
Async XLA Ops:
  0.6 0.9 copy-start
  1.6 0.9 copy-start.2
  2.5 0.8 copy-start.3
  4.2 7.2 %collective-permute-start = (f32[7,16,128]{2,1,0:T(8,128)S(1)}, f32[7,16,128]{2,1,0:T(8,128)S(1)}, u32[]{:S(2)}, u32[]{:S(2)}) collective-permute-start(f32[7,16,128]{2,1,0:T(8,128)S(1)} %get-tuple-element.26), channel_id=1, source_target_pairs={{0,1},{1,2},{2,3},{3,0},{4,5},{5,6},{6,7},{7,4},{8,9},{9,10},{10,1... | collective-permute-start | bytes 172040 | tf_op jit(solution)/shard_map/ppermute | solution.py:386
  8.2 4.9 %collective-permute-start.1 = (f32[7,16,128]{2,1,0:T(8,128)S(1)}, f32[7,16,128]{2,1,0:T(8,128)S(1)}, u32[]{:S(2)}, u32[]{:S(2)}) collective-permute-start(f32[7,16,128]{2,1,0:T(8,128)S(1)} %get-tuple-element.27), channel_id=1, source_target_pairs={{0,3},{1,0},{2,1},{3,2},{4,7},{5,4},{6,5},{7,6},{8,11},{9,8},{10,9... | collective-permute-start | bytes 172040 | tf_op jit(solution)/shard_map/ppermute | solution.py:386
  13.1 24.5 %collective-permute-start.3 = (f32[7,10,16,128]{3,2,1,0:T(8,128)S(1)}, f32[7,10,16,128]{3,2,1,0:T(8,128)S(1)}, u32[]{:S(2)}, u32[]{:S(2)}) collective-permute-start(f32[7,10,16,128]{3,2,1,0:T(8,128)S(1)} %pad_maximum_fusion.2.x0), channel_id=1, source_target_pairs={{0,704},{64,0},{128,64},{192,128},{256,192},{320,256},{384,320},{4... | collective-permute-start | bytes 1720328 | tf_op jit(solution)/shard_map/ppermute | solution.py:386
  27.4 15.2 %collective-permute-start.2 = (f32[7,10,16,128]{3,2,1,0:T(8,128)S(1)}, f32[7,10,16,128]{3,2,1,0:T(8,128)S(1)}, u32[]{:S(2)}, u32[]{:S(2)}) collective-permute-start(f32[7,10,16,128]{3,2,1,0:T(8,128)S(1)} %pad_maximum_fusion.2.x0), channel_id=1, source_target_pairs={{0,64},{64,128},{128,192},{192,256},{256,320},{320,384},{384,448},... | collective-permute-start | bytes 1720328 | tf_op jit(solution)/shard_map/ppermute | solution.py:386
  43.6 14.5 %collective-permute-start.4 = (f32[7,30,8,128]{3,2,1,0:T(8,128)}, f32[7,30,8,128]{3,2,1,0:T(8,128)S(1)}, u32[]{:S(2)}, u32[]{:S(2)}) collective-permute-start(f32[7,30,8,128]{3,2,1,0:T(8,128)} %pad_maximum_fusion), channel_id=1, source_target_pairs={{0,4},{4,8},{8,12},{12,16},{16,20},{20,24},{24,28},{28,32},{32,36}... | collective-permute-start | bytes 2580488 | tf_op jit(solution)/shard_map/ppermute | solution.py:386
  49.2 12.4 %collective-permute-start.5 = (f32[7,30,8,128]{3,2,1,0:T(8,128)}, f32[7,30,8,128]{3,2,1,0:T(8,128)S(1)}, u32[]{:S(2)}, u32[]{:S(2)}) collective-permute-start(f32[7,30,8,128]{3,2,1,0:T(8,128)} %pad_maximum_fusion.1), channel_id=1, source_target_pairs={{0,60},{4,0},{8,4},{12,8},{16,12},{20,16},{24,20},{28,24},{32,28},... | collective-permute-start | bytes 2580488 | tf_op jit(solution)/shard_map/ppermute | solution.py:386
  73.6 6.5 %collective-permute-start.6 = (f32[2,3,8,256]{3,2,1,0:T(8,128)S(1)}, f32[2,3,8,256]{3,2,1,0:T(8,128)S(1)}, u32[]{:S(2)}, u32[]{:S(2)}) collective-permute-start(f32[2,3,8,256]{3,2,1,0:T(8,128)S(1)} %get-tuple-element.28), channel_id=1, source_target_pairs={{0,64},{64,128},{128,192},{192,256},{256,320},{320,384},{384,448},... | collective-permute-start | bytes 147464 | tf_op jit(solution)/shard_map/ppermute | solution.py:386
  75.5 5.7 %collective-permute-start.7 = (f32[2,3,8,256]{3,2,1,0:T(8,128)S(1)}, f32[2,3,8,256]{3,2,1,0:T(8,128)S(1)}, u32[]{:S(2)}, u32[]{:S(2)}) collective-permute-start(f32[2,3,8,256]{3,2,1,0:T(8,128)S(1)} %get-tuple-element.30), channel_id=1, source_target_pairs={{0,704},{64,0},{128,64},{192,128},{256,192},{320,256},{384,320},{4... | collective-permute-start | bytes 147464 | tf_op jit(solution)/shard_map/ppermute | solution.py:386
  81.3 2.3 %collective-permute-start.8 = (f32[2,3,8,256]{3,2,1,0:T(8,128)S(1)}, f32[2,3,8,256]{3,2,1,0:T(8,128)S(1)}, u32[]{:S(2)}, u32[]{:S(2)}) collective-permute-start(f32[2,3,8,256]{3,2,1,0:T(8,128)S(1)} %get-tuple-element.31), channel_id=1, source_target_pairs={{0,4},{4,8},{8,12},{12,16},{16,20},{20,24},{24,28},{28,32},{32,36}... | collective-permute-start | bytes 147464 | tf_op jit(solution)/shard_map/ppermute | solution.py:386
  82.4 3.8 %collective-permute-start.9 = (f32[2,3,8,256]{3,2,1,0:T(8,128)S(1)}, f32[2,3,8,256]{3,2,1,0:T(8,128)S(1)}, u32[]{:S(2)}, u32[]{:S(2)}) collective-permute-start(f32[2,3,8,256]{3,2,1,0:T(8,128)S(1)} %get-tuple-element.32), channel_id=1, source_target_pairs={{0,60},{4,0},{8,4},{12,8},{16,12},{20,16},{24,20},{28,24},{32,28},... | collective-permute-start | bytes 147464 | tf_op jit(solution)/shard_map/ppermute | solution.py:386
  86.2 44.3 %copy-start.1 = (f32[3,8,16,128]{3,2,1,0:T(8,128)S(1)}, f32[3,8,16,128]{3,2,1,0:T(8,128)}, u32[]{:S(2)}) copy-start(f32[3,8,16,128]{3,2,1,0:T(8,128)} %residual_in.1) | copy-start | bytes 589828
  86.2 44.3 %copy-start.4 = (f32[3,8,16,128]{3,2,1,0:T(8,128)S(1)}, f32[3,8,16,128]{3,2,1,0:T(8,128)}, u32[]{:S(2)}) copy-start(f32[3,8,16,128]{3,2,1,0:T(8,128)} %param.4) | copy-start | bytes 589828

commit v3 on v1

--- a/solution.py
+++ b/solution.py
@@ -20,6 +20,7 @@
 ROWS = CY + 16
 PLANES = CX + 16
 ZH = 16
+LIMIT = 20 * 1024 * 1024
 FIELDS = 7
 GYX = CX + 2
 
@@ -33,7 +34,7 @@
         out_shape=[jax.ShapeDtypeStruct(s, F32) for s in outs],
         out_specs=[VMEM] * len(outs),
         scratch_shapes=[pltpu.VMEM(s, F32) for s in scratch],
-        compiler_params=pltpu.CompilerParams(vmem_limit_bytes=48 * 1024 * 1024),
+        compiler_params=pltpu.CompilerParams(vmem_limit_bytes=LIMIT),
     )
 
 
@@ -94,6 +95,15 @@
         stage(4 + c, [1.0 - fixed[c, x].astype(F32) for x in range(CX)])
 
 
+def steps(start, stop, each, body):
+    def step(i, _):
+        for j in range(each):
+            body(start + each * i + j)
+        return 0
+
+    lax.fori_loop(0, (stop - start) // each, step, 0)
+
+
 def restrict_rows(tmp, v):
     n = v.shape[0] // 2
     for h in range(2):
@@ -110,19 +120,19 @@
 
 
 def fine_kernel(
-    ends, x0, xl, xr, yl, yr,
-    o_r, o_free, o_ux, o_uy, o_uz, o_ig, o_mc, o_mux, o_muy, o_muz, o_mig, o_right, o_left, o_own,
-    ext, ux, uy, uz, mm, mux, muy, muz, mig, mrhs, mc, cx_, cy_, cz_, cg, tmp32, tmp16,
+    ends, xl, x0, xr, yll, yl0, ylr, yrl, yr0, yrr,
+    ext, ux, uy, uz, inv, mux, muy, muz, mig, mc, o_right, o_left, o_own,
+    mm, spring, mrhs, cx_, cy_, cz_, cg, tmp32, tmp16,
 ):
     lane = lane_of((CY, CZ))
     lane8 = lane_of((8, CZ))
 
     def assemble(f, _):
-        for b, brick in enumerate((xl, x0, xr)):
+        for b, (lower, brick, upper) in enumerate(((yll, xl, yrl), (yl0, x0, yr0), (ylr, xr, yrr))):
             parts = (
-                (0, 8, lambda p: yl[f, GYX * b + p], lane8),
+                (0, 8, lambda p: lower[f, p], lane8),
                 (8, CY, lambda p: brick[f, p], lane),
-                (8 + CY, 8, lambda p: yr[f, GYX * b + p], lane8),
+                (8 + CY, 8, lambda p: upper[f, p], lane8),
             )
             for start, rows, get, at in parts:
                 from_left, from_right = get(CX), get(CX + 1)
@@ -145,38 +155,26 @@
     half_y = jnp.where(((row == 7) & (lo_y == 1)) | ((row == 7 + CY) & (hi_y == 1)), 0.0, 0.5)
     half_z = jnp.where(((col == LANES - 1) & (lo_z == 1)) | ((col == CZ - 1) & (hi_z == 1)), 0.0, 0.5)
 
-    def links(p, _):
+    def links(p):
         here = ext[0, p]
         cut = ((p == 7) & (lo_x == 1)) | ((p == 7 + CX) & (hi_x == 1))
         ux[p] = jnp.where(cut, 0.0, 0.5) * (here + ext[0, jnp.minimum(p + 1, PLANES - 1)])
         uy[p] = half_y * (here + after(here, 1, 0))
         uz[p] = half_z * (here + after(here, 1, 1))
-        return 0
-
-    lax.fori_loop(0, PLANES, links, 0)
-
-    def smooth(p, _):
+
+    steps(0, PLANES, 4, links)
+
+    def smooth(p):
         g = 0.1 * ext[0, p] + ux[p] + ux[p - 1]
         g = g + uy[p] + before(uy[p], 1, 0) + uz[p] + before(uz[p], 1, 1)
         ig = damping / g
+        inv[p] = ig
         for c in range(3):
             mm[c, p] = ext[4 + c, p] * ext[1 + c, p] * ig
 
-        @pl.when((p >= 6) & (p < 18))
-        def _():
-            o_ig[p - 6] = ig
-            o_ux[p - 6] = ux[p]
-            o_uy[p - 6] = uy[p]
-            o_uz[p - 6] = uz[p]
-            for c in range(3):
-                o_r[c, p - 6] = ext[1 + c, p]
-                o_free[c, p - 6] = ext[4 + c, p]
-
-        return 0
-
-    lax.fori_loop(1, PLANES - 1, smooth, 0)
-
-    def mid_links(q, _):
+    steps(1, PLANES - 1, 2, smooth)
+
+    def mid_links(q, tmp32=tmp32):
         p = 2 * q
         a, b = restrict_rows(tmp32, ux[p + 1])
         mux[q] = pair_sum(a + b, 1)
@@ -185,16 +183,16 @@
         a, b = restrict_rows(tmp32, uz[p] + uz[p + 1])
         muz[q] = odd_group(a + b, 1)
         a, b = restrict_rows(tmp32, ext[0, p] + ext[0, p + 1])
-        mig[q] = 0.1 * pair_sum(a + b, 1)
-        return 0
-
-    lax.fori_loop(0, 12, mid_links, 0)
-
-    def mid_rhs(q, _):
+        spring[q] = 0.1 * pair_sum(a + b, 1)
+
+    steps(0, 12, 2, mid_links)
+
+    def mid_rhs(q):
         p = 2 * q
-        g = mig[q] + mux[q] + mux[q - 1]
+        g = spring[q] + mux[q] + mux[q - 1]
         g = g + muy[q] + before(muy[q], 1, 0) + muz[q] + before(muz[q], 2, 1)
         ig = damping / g
+        mig[q] = ig
         for c in range(3):
             total = jnp.zeros(shape, F32)
             for i in range(2):
@@ -205,18 +203,7 @@
             mrhs[c, q] = rhs
             mc[c, q] = ig * rhs
 
-        @pl.when((q >= 2) & (q < 10))
-        def _():
-            o_mig[q - 2] = ig
-            o_mux[q - 2] = mux[q]
-            o_muy[q - 2] = muy[q]
-            o_muz[q - 2] = muz[q]
-            for c in range(3):
-                o_mc[c, q - 2] = mc[c, q]
-
-        return 0
-
-    lax.fori_loop(1, 11, mid_rhs, 0)
+    steps(1, 11, 2, mid_rhs)
 
     for s in range(5):
         q = 2 * s
@@ -226,7 +213,7 @@
         cy_[s] = pair_sum(b, 2)
         a, b = restrict_rows(tmp16, muz[q] + muz[q + 1])
         cz_[s] = odd_group(a + b, 2)
-        a, b = restrict_rows(tmp16, mig[q] + mig[q + 1])
+        a, b = restrict_rows(tmp16, spring[q] + spring[q + 1])
         cg[s] = pair_sum(a + b, 2)
 
     quad = lane_of((8, LANES)) % 4
@@ -263,10 +250,13 @@
 
 
 def solve_kernel(
-    xl, own, xr, yl, yr, r, free, ux, uy, uz, ig, mc, mux, muy, muz, mig,
+    xl, own, xr, yl, yr, ext, ux_, uy_, uz_, ig_, mux_, muy_, muz_, mig_, mc_,
     direction, image, sums,
     packed, cc, pm, pf, m1, base, d, tmp16,
 ):
+    r, free = ext.at[1:4, 6:18], ext.at[4:7, 6:18]
+    ux, uy, uz, ig = (a.at[6:18] for a in (ux_, uy_, uz_, ig_))
+    mux, muy, muz, mig, mc = *(a.at[2:10] for a in (mux_, muy_, muz_, mig_)), mc_.at[:, 2:10]
     quad = lane_of((16, LANES)) % 4
     field = [[None] * 8 for _ in range(7)]
     for i in range(2):
@@ -350,8 +340,8 @@
 
     zero = jnp.zeros((CY, CZ), F32)
     first, second = lax.fori_loop(2, 10, last, (zero, zero))
-    sums[0:1] = jnp.sum(first, axis=0, keepdims=True)
-    sums[1:2] = jnp.sum(second, axis=0, keepdims=True)
+    sums[0:1] = jnp.full((1, CZ), jnp.sum(first), F32)
+    sums[1:2] = jnp.full((1, CZ), jnp.sum(second), F32)
 
 
 def ring(count, step):
@@ -384,32 +374,25 @@
     zl, zr = both((to_right, to_left), "gz", nz)
     x0 = jnp.concatenate([main, zl[:, None], zr[:, None]], axis=1)
     xl, xr = both(x0, "gx", nx)
-    wide = [xl, x0, xr]
-    yl, yr = both(
-        (
-            jnp.concatenate([v[:, :, 8:16] for v in wide], axis=1),
-            jnp.concatenate([v[:, :, 0:8] for v in wide], axis=1),
-        ),
-        y_axes,
-        ny,
-    )
+    halves = [both((v[:, :, 8:16], v[:, :, 0:8]), y_axes, ny) for v in (xl, x0, xr)]
+    yl, yr = zip(*halves)
 
     full = (12, ROWS, LANES)
     half = (8, ROWS // 2, LANES)
     all_f = (PLANES, ROWS, LANES)
     all_m = (12, ROWS // 2, LANES)
-    outs = [(3,) + full, (3,) + full, full, full, full, full, (3,) + half, half, half, half, half]
+    outs = [(FIELDS,) + all_f, all_f, all_f, all_f, all_f, all_m, all_m, all_m, all_m, (3,) + all_m]
     outs += [(2, 3, 8, LANES), (2, 3, 8, LANES), (2, 2, 8, LANES)]
-    scratch = [(FIELDS,) + all_f, all_f, all_f, all_f, (3,) + all_f, all_m, all_m, all_m, all_m, (3,) + all_m, (3,) + all_m]
+    scratch = [(3,) + all_f, all_m, (3,) + all_m]
     scratch += [(5, 8, LANES)] * 4 + [(2, ROWS, CZ), (2, ROWS // 2, CZ)]
     fine = pl.pallas_call(
         fine_kernel,
         out_shape=[jax.ShapeDtypeStruct(s, F32) for s in outs],
-        in_specs=[SMEM] + [VMEM] * 5,
+        in_specs=[SMEM] + [VMEM] * 9,
         out_specs=[VMEM] * len(outs),
         scratch_shapes=[pltpu.VMEM(s, F32) for s in scratch],
-        compiler_params=pltpu.CompilerParams(vmem_limit_bytes=48 * 1024 * 1024),
-    )(ends, x0, xl, xr, yl, yr)
+        compiler_params=pltpu.CompilerParams(vmem_limit_bytes=LIMIT),
+    )(ends, xl, x0, xr, *yl, *yr)
     kept, (to_right, to_left, own) = fine[:-3], fine[-3:]
     cl, cr = both((to_right, to_left), "gx", nx)
     up, down = call(turn_kernel, [(2, 3, 8, LANES)] * 2)(cl, own, cr)
@@ -419,9 +402,8 @@
         [(3, CX, CY, CZ), (3, CX, CY, CZ), (2, CZ)],
         [(16, LANES), (2, ROWS // 2, CZ), (3,) + half, (2, ROWS, CZ), (3,) + full, (3,) + full, (3,) + full, (16, LANES)],
     )(cl, own, cr, dl, dr, *kept)
-    sums = jnp.broadcast_to(jnp.sum(sums, axis=1)[:, None, None], (2, 4, CZ)).reshape(8, CZ)
     sums = all_sum(all_sum(sums, ("gc", "gz")), ("gx", "co"))
-    alpha = sums[0, 0] / sums[4, 0]
+    alpha = (sums[0] / sums[1])[None, None, None]
     return (solution + alpha * direction, residual - alpha * image, direction)
 
 

time: 140 us -> 122 us (0.87)
  waiting for transfers between devices: 32.1 us -> 14.3 us
  starting transfers between devices: 35.5 us -> 45.5 us
  Pallas kernels: 20.8 us -> 17.9 us
  blocking collectives: 38.9 us -> 36.3 us
  other arithmetic: 3.95 us -> 1.86 us
    ppermute x5 -> x7, waiting for transfers between devices: 15 us -> 0.72 us  [both(): lax.ppermute(up, axes, ring(count, 1))]
    ppermute x5 -> x7, starting transfers between devices: 22.1 us -> 31.4 us  [both(): lax.ppermute(down, axes, ring(count, -1))]
    ppermute x5 -> x7, waiting for transfers between devices: 17.1 us -> 13.6 us  [both(): lax.ppermute(down, axes, ring(count, -1))]
    pallas_call x1, Pallas kernels: 12.4 us -> 9.47 us  [shards(): pl.pallas_call(fine_kernel, out_shape=[jax.ShapeDtypeStruct(s, F32) for s...]
    all_to_all x2, blocking collectives: 38.9 us -> 36.3 us  [all_sum(): return lax.all_to_all(sent, axes, 0, 0).sum(axis=0)]
    unnamed x14 -> x10, local copies, waits for them, and re-layouts: 5.24 us -> 2.7 us
    slice x3, local copies, waits for them, and re-layouts: 0.12 us -> 2.5 us  [shards(): v[:, :, 0:8]]
    concatenate x2 -> x0, other arithmetic: 1.99 us -> none  [the longest x1 1.02 us: shards(): jnp.concatenate([v[:, :, 0:8] for v in wide], axis=1)]
  transfers between devices with their start and end apart: 10 -> 14, of which waited for: 8 -> 6; matrix products, arithmetic and copies ran while one was open for 1% -> 2% of each run, Pallas kernels for 0% -> 0%
where the time goes in v3:
time: 122 us
  starting transfers between devices  45.5 us (37%)
  blocking collectives  36.3 us (30%)
  Pallas kernels  17.9 us (15%)
  waiting for transfers between devices  14.3 us (12%)
  local copies, waits for them, and re-layouts  5.33 us (4%)
  other arithmetic  1.86 us (2%)
    all_to_all x2, blocking collectives, all_sum(): return lax.all_to_all(sent, axes, 0, 0).sum(axis=0)  36.3 us
    ppermute x7, starting transfers between devices, both(): lax.ppermute(down, axes, ring(count, -1))  31.4 us
    ppermute x7, starting transfers between devices, both(): lax.ppermute(up, axes, ring(count, 1))  14.1 us
    ppermute x7, waiting for transfers between devices, both(): lax.ppermute(down, axes, ring(count, -1))  13.6 us
    pallas_call x1, Pallas kernels, shards(): pl.pallas_call(fine_kernel, out_shape=[jax.ShapeDtypeStruct(s, F32) for s...  9.47 us
    pallas_call x1, Pallas kernels, shards(): call(solve_kernel, [(3, CX, CY, CZ), (3, CX, CY, CZ), (2, CZ)], [(16, LAN...  8.09 us
    unnamed x10, local copies, waits for them, and re-layouts  2.7 us
    slice x3, local copies, waits for them, and re-layouts, shards(): v[:, :, 0:8]  2.5 us
  transfers between devices with their start and end apart: 14, of which 6 were waited for; matrix products, arithmetic and copies ran while one was open for 2% of the time, Pallas kernels for 0%

profile of v3, /device:TPU:1, one launch (start us, length us, event | category | flops | bytes accessed | tf_op | source)
XLA Modules:
  0.0 122.0 jit_solution(254903267843940295)
XLA Ops:
  0.6 0.0 copy-start
  0.6 0.9 copy-done
  1.6 0.0 copy-start.2
  1.6 0.9 copy-done.2
  2.5 0.0 copy-start.3
  2.5 0.8 copy-done.3
  3.3 0.3 shard_map.67
  3.6 3.9 %collective-permute-start = (f32[7,16,128]{2,1,0:T(8,128)S(1)}, f32[7,16,128]{2,1,0:T(8,128)S(1)}, u32[]{:S(2)}, u32[]{:S(2)}) collective-permute-start(f32[7,16,128]{2,1,0:T(8,128)S(1)} %get-tuple-element.25), channel_id=1, source_target_pairs={{0,1},{1,2},{2,3},{3,0},{4,5},{5,6},{6,7},{7,4},{8,9},{9,10},{10,1... | collective-permute-start | bytes 172040 | tf_op jit(solution)/shard_map/ppermute | solution.py:369
  7.6 3.2 %collective-permute-start.1 = (f32[7,16,128]{2,1,0:T(8,128)S(1)}, f32[7,16,128]{2,1,0:T(8,128)S(1)}, u32[]{:S(2)}, u32[]{:S(2)}) collective-permute-start(f32[7,16,128]{2,1,0:T(8,128)S(1)} %get-tuple-element.26), channel_id=1, source_target_pairs={{0,3},{1,0},{2,1},{3,2},{4,7},{5,4},{6,5},{7,6},{8,11},{9,8},{10,9... | collective-permute-start | bytes 172040 | tf_op jit(solution)/shard_map/ppermute | solution.py:369
  10.8 0.0 collective-permute-done
  10.8 1.7 %collective-permute-done.1 = f32[7,16,128]{2,1,0:T(8,128)S(1)} collective-permute-done((f32[7,16,128]{2,1,0:T(8,128)S(1)}, f32[7,16,128]{2,1,0:T(8,128)S(1)}, u32[]{:S(2)}, u32[]{:S(2)}) %collective-permute-start.1) | collective-permute-done | bytes 57376 | tf_op jit(solution)/shard_map/ppermute | solution.py:369
  12.5 14.3 %collective-permute-start.3 = (f32[7,10,16,128]{3,2,1,0:T(8,128)S(1)}, f32[7,10,16,128]{3,2,1,0:T(8,128)S(1)}, u32[]{:S(2)}, u32[]{:S(2)}) collective-permute-start(f32[7,10,16,128]{3,2,1,0:T(8,128)S(1)} %pad_maximum_fusion.x0), channel_id=1, source_target_pairs={{0,704},{64,0},{128,64},{192,128},{256,192},{320,256},{384,320},{4... | collective-permute-start | bytes 1720328 | tf_op jit(solution)/shard_map/ppermute | solution.py:369
  26.9 1.9 %collective-permute-start.2 = (f32[7,10,16,128]{3,2,1,0:T(8,128)S(1)}, f32[7,10,16,128]{3,2,1,0:T(8,128)S(1)}, u32[]{:S(2)}, u32[]{:S(2)}) collective-permute-start(f32[7,10,16,128]{3,2,1,0:T(8,128)S(1)} %pad_maximum_fusion.x0), channel_id=1, source_target_pairs={{0,64},{64,128},{128,192},{192,256},{256,320},{320,384},{384,448},... | collective-permute-start | bytes 1720328 | tf_op jit(solution)/shard_map/ppermute | solution.py:369
  28.8 0.7 fusion.2
  29.5 2.4 %collective-permute-start.8 = (f32[7,10,8,128]{3,2,1,0:T(8,128)S(1)}, f32[7,10,8,128]{3,2,1,0:T(8,128)S(1)}, u32[]{:S(2)}, u32[]{:S(2)}) collective-permute-start(f32[7,10,8,128]{3,2,1,0:T(8,128)S(1)} %get-tuple-element.47), channel_id=1, source_target_pairs={{0,60},{4,0},{8,4},{12,8},{16,12},{20,16},{24,20},{28,24},{32,28},... | collective-permute-start | bytes 860168 | tf_op jit(solution)/shard_map/ppermute | solution.py:369
  31.9 1.2 collective-permute-start.5
  33.1 3.9 %collective-permute-done.3.xr = f32[7,10,16,128]{3,2,1,0:T(8,128)S(1)} collective-permute-done((f32[7,10,16,128]{3,2,1,0:T(8,128)S(1)}, f32[7,10,16,128]{3,2,1,0:T(8,128)S(1)}, u32[]{:S(2)}, u32[]{:S(2)}) %collective-permute-start.3) | collective-permute-done | bytes 573472 | tf_op jit(solution)/shard_map/ppermute | solution.py:369
  37.0 0.9 fusion.1
  37.9 3.0 %collective-permute-start.9 = (f32[7,10,8,128]{3,2,1,0:T(8,128)}, f32[7,10,8,128]{3,2,1,0:T(8,128)S(1)}, u32[]{:S(2)}, u32[]{:S(2)}) collective-permute-start(f32[7,10,8,128]{3,2,1,0:T(8,128)} %get-tuple-element.45), channel_id=1, source_target_pairs={{0,60},{4,0},{8,4},{12,8},{16,12},{20,16},{24,20},{28,24},{32,28},... | collective-permute-start | bytes 860168 | tf_op jit(solution)/shard_map/ppermute | solution.py:369
  40.9 1.2 collective-permute-start.6
  42.1 0.0 collective-permute-done.2.xl
  42.1 0.9 fusion.3
  43.0 3.2 %collective-permute-start.7 = (f32[7,10,8,128]{3,2,1,0:T(8,128)}, f32[7,10,8,128]{3,2,1,0:T(8,128)S(1)}, u32[]{:S(2)}, u32[]{:S(2)}) collective-permute-start(f32[7,10,8,128]{3,2,1,0:T(8,128)} %get-tuple-element.49), channel_id=1, source_target_pairs={{0,60},{4,0},{8,4},{12,8},{16,12},{20,16},{24,20},{28,24},{32,28},... | collective-permute-start | bytes 860168 | tf_op jit(solution)/shard_map/ppermute | solution.py:369
  46.2 0.0 collective-permute-done.8.yr0
  46.2 1.2 collective-permute-start.4
  47.4 0.1 stack.27
  47.5 0.0 collective-permute-done.5.yl0
  47.5 0.0 collective-permute-done.9.yrr
  47.5 0.0 collective-permute-done.6.ylr
  47.5 4.7 %collective-permute-done.7.yrl = f32[7,10,8,128]{3,2,1,0:T(8,128)S(1)} collective-permute-done((f32[7,10,8,128]{3,2,1,0:T(8,128)}, f32[7,10,8,128]{3,2,1,0:T(8,128)S(1)}, u32[]{:S(2)}, u32[]{:S(2)}) %collective-permute-start.7) | collective-permute-done | bytes 286752 | tf_op jit(solution)/shard_map/ppermute | solution.py:369
  52.2 0.0 collective-permute-done.4.yll
  52.2 9.5 %shard_map.68 = (f32[7,24,32,256]{3,2,1,0:T(8,128)S(1)}, f32[24,32,256]{2,1,0:T(8,128)S(1)}, f32[24,32,256]{2,1,0:T(8,128)S(1)}, f32[24,32,256]{2,1,0:T(8,128)S(...) custom-call(s32[6]{0:T(128)S(1)} %convert_element_type.3.ends, ...), custom_call_target="tpu_custom_call" | custom-call | tf_op jit(solution)/shard_map/pallas_call | solution.py:388
  61.7 0.0 copy-start.1
  61.7 0.0 copy-start.4
  61.7 2.1 %collective-permute-start.10 = (f32[2,3,8,256]{3,2,1,0:T(8,128)S(1)}, f32[2,3,8,256]{3,2,1,0:T(8,128)S(1)}, u32[]{:S(2)}, u32[]{:S(2)}) collective-permute-start(f32[2,3,8,256]{3,2,1,0:T(8,128)S(1)} %get-tuple-element.27), channel_id=1, source_target_pairs={{0,64},{64,128},{128,192},{192,256},{256,320},{320,384},{384,448},... | collective-permute-start | bytes 147464 | tf_op jit(solution)/shard_map/ppermute | solution.py:369
  63.8 4.6 %collective-permute-start.11 = (f32[2,3,8,256]{3,2,1,0:T(8,128)S(1)}, f32[2,3,8,256]{3,2,1,0:T(8,128)S(1)}, u32[]{:S(2)}, u32[]{:S(2)}) collective-permute-start(f32[2,3,8,256]{3,2,1,0:T(8,128)S(1)} %get-tuple-element.29), channel_id=1, source_target_pairs={{0,704},{64,0},{128,64},{192,128},{256,192},{320,256},{384,320},{4... | collective-permute-start | bytes 147464 | tf_op jit(solution)/shard_map/ppermute | solution.py:369
  68.4 0.0 collective-permute-done.10.xl
  68.4 1.1 collective-permute-done.11.xr
  69.6 2.6 %collective-permute-start.12 = (f32[2,3,8,256]{3,2,1,0:T(8,128)S(1)}, f32[2,3,8,256]{3,2,1,0:T(8,128)S(1)}, u32[]{:S(2)}, u32[]{:S(2)}) collective-permute-start(f32[2,3,8,256]{3,2,1,0:T(8,128)S(1)} %get-tuple-element.30), channel_id=1, source_target_pairs={{0,4},{4,8},{8,12},{12,16},{16,20},{20,24},{24,28},{28,32},{32,36}... | collective-permute-start | bytes 147464 | tf_op jit(solution)/shard_map/ppermute | solution.py:369
  72.2 0.7 collective-permute-start.13
  72.9 0.7 collective-permute-done.12.yl
  73.6 2.1 %collective-permute-done.13.yr = f32[2,3,8,256]{3,2,1,0:T(8,128)S(1)} collective-permute-done((f32[2,3,8,256]{3,2,1,0:T(8,128)S(1)}, f32[2,3,8,256]{3,2,1,0:T(8,128)S(1)}, u32[]{:S(2)}, u32[]{:S(2)}) %collective-permute-start.13) | collective-permute-done | bytes 49184 | tf_op jit(solution)/shard_map/ppermute | solution.py:369
  75.7 8.1 %shard_map.70 = (f32[3,8,16,128]{3,2,1,0:T(8,128)}, f32[3,8,16,128]{3,2,1,0:T(8,128)S(1)}, f32[2,128]{1,0:T(2,128)S(1)}) custom-call(f32[2,3,8,256]{3,2,1,0:T(8,128)S(1)} %collective-permute-done.10.xl, f32[2,2,8,256]{3,2,1,0:T(8,128)S(1)} %get-tuple-element.28.own, f32[2,3,8,256]{3,2,1,0:T(8,128)S(1)} %collective-permute-done.11.xr, ...), custom_call_target="tpu_custom_call" | custom-call | tf_op jit(solution)/shard_map/pallas_call | solution.py:400
  83.8 19.5 %all_to_all.10 = f32[32,2,128]{2,1,0:T(2,128)S(1)} all-to-all(f32[32,2,128]{2,1,0:T(2,128)S(1)} %broadcast_in_dim.10), channel_id=1, replica_groups=mesh['gx'=12,'gc'=8,'co'=2,'gz'=4] {'gc','gz'}, dimensions={0} | all-to-all | bytes 65536 | tf_op jit(solution)/shard_map/all_to_all | solution.py:356
  103.4 16.8 %all_to_all.11 = f32[24,2,128]{2,1,0:T(2,128)S(1)} all-to-all(f32[24,2,128]{2,1,0:T(2,128)S(1)} %broadcast_in_dim.22), channel_id=1, replica_groups=mesh['gx'=12,'gc'=8,'co'=2,'gz'=4] {'gx','co'}, dimensions={0} | all-to-all | bytes 49152 | tf_op jit(solution)/shard_map/all_to_all | solution.py:356
  120.2 0.0 copy-done.1
  120.2 0.0 copy-done.4
  120.2 1.7 %multiply_subtract_fusion = (f32[3,8,16,128]{3,2,1,0:T(8,128)}, f32[3,8,16,128]{3,2,1,0:T(8,128)}) fusion(f32[3,8,16,128]{3,2,1,0:T(8,128)S(1)} %copy-done.1, f32[3,8,16,128]{3,2,1,0:T(8,128)S(1)} %get-tuple-element.44, f32[128]{0:T(128)S(1)} %fusion, f32[3,8,16,128]{3,2,1,0:T(8,128)S(1)} %copy-done.4, f32[3,8,16,128]{3,2,1,0:T(8,128)} %get-tuple-element.23), kind=kLoop, calls=%fused_computation.1 | loop fusion | flops 196608 | bytes 1180160 | tf_op jit(solution)/shard_map/sub | solution.py:407
  (8 shorter events, 0.2 us)
Async XLA Ops:
  0.6 0.9 copy-start
  1.6 0.9 copy-start.2
  2.5 0.8 copy-start.3
  3.6 7.2 %collective-permute-start = (f32[7,16,128]{2,1,0:T(8,128)S(1)}, f32[7,16,128]{2,1,0:T(8,128)S(1)}, u32[]{:S(2)}, u32[]{:S(2)}) collective-permute-start(f32[7,16,128]{2,1,0:T(8,128)S(1)} %get-tuple-element.25), channel_id=1, source_target_pairs={{0,1},{1,2},{2,3},{3,0},{4,5},{5,6},{6,7},{7,4},{8,9},{9,10},{10,1... | collective-permute-start | bytes 172040 | tf_op jit(solution)/shard_map/ppermute | solution.py:369
  7.6 4.9 %collective-permute-start.1 = (f32[7,16,128]{2,1,0:T(8,128)S(1)}, f32[7,16,128]{2,1,0:T(8,128)S(1)}, u32[]{:S(2)}, u32[]{:S(2)}) collective-permute-start(f32[7,16,128]{2,1,0:T(8,128)S(1)} %get-tuple-element.26), channel_id=1, source_target_pairs={{0,3},{1,0},{2,1},{3,2},{4,7},{5,4},{6,5},{7,6},{8,11},{9,8},{10,9... | collective-permute-start | bytes 172040 | tf_op jit(solution)/shard_map/ppermute | solution.py:369
  12.5 24.5 %collective-permute-start.3 = (f32[7,10,16,128]{3,2,1,0:T(8,128)S(1)}, f32[7,10,16,128]{3,2,1,0:T(8,128)S(1)}, u32[]{:S(2)}, u32[]{:S(2)}) collective-permute-start(f32[7,10,16,128]{3,2,1,0:T(8,128)S(1)} %pad_maximum_fusion.x0), channel_id=1, source_target_pairs={{0,704},{64,0},{128,64},{192,128},{256,192},{320,256},{384,320},{4... | collective-permute-start | bytes 1720328 | tf_op jit(solution)/shard_map/ppermute | solution.py:369
  26.9 15.2 %collective-permute-start.2 = (f32[7,10,16,128]{3,2,1,0:T(8,128)S(1)}, f32[7,10,16,128]{3,2,1,0:T(8,128)S(1)}, u32[]{:S(2)}, u32[]{:S(2)}) collective-permute-start(f32[7,10,16,128]{3,2,1,0:T(8,128)S(1)} %pad_maximum_fusion.x0), channel_id=1, source_target_pairs={{0,64},{64,128},{128,192},{192,256},{256,320},{320,384},{384,448},... | collective-permute-start | bytes 1720328 | tf_op jit(solution)/shard_map/ppermute | solution.py:369
  29.5 16.7 %collective-permute-start.8 = (f32[7,10,8,128]{3,2,1,0:T(8,128)S(1)}, f32[7,10,8,128]{3,2,1,0:T(8,128)S(1)}, u32[]{:S(2)}, u32[]{:S(2)}) collective-permute-start(f32[7,10,8,128]{3,2,1,0:T(8,128)S(1)} %get-tuple-element.47), channel_id=1, source_target_pairs={{0,60},{4,0},{8,4},{12,8},{16,12},{20,16},{24,20},{28,24},{32,28},... | collective-permute-start | bytes 860168 | tf_op jit(solution)/shard_map/ppermute | solution.py:369
  31.9 15.6 %collective-permute-start.5 = (f32[7,10,8,128]{3,2,1,0:T(8,128)}, f32[7,10,8,128]{3,2,1,0:T(8,128)S(1)}, u32[]{:S(2)}, u32[]{:S(2)}) collective-permute-start(f32[7,10,8,128]{3,2,1,0:T(8,128)} %get-tuple-element.48), channel_id=1, source_target_pairs={{0,4},{4,8},{8,12},{12,16},{16,20},{20,24},{24,28},{28,32},{32,36}... | collective-permute-start | bytes 860168 | tf_op jit(solution)/shard_map/ppermute | solution.py:369
  37.9 9.6 %collective-permute-start.9 = (f32[7,10,8,128]{3,2,1,0:T(8,128)}, f32[7,10,8,128]{3,2,1,0:T(8,128)S(1)}, u32[]{:S(2)}, u32[]{:S(2)}) collective-permute-start(f32[7,10,8,128]{3,2,1,0:T(8,128)} %get-tuple-element.45), channel_id=1, source_target_pairs={{0,60},{4,0},{8,4},{12,8},{16,12},{20,16},{24,20},{28,24},{32,28},... | collective-permute-start | bytes 860168 | tf_op jit(solution)/shard_map/ppermute | solution.py:369
  40.9 6.6 %collective-permute-start.6 = (f32[7,10,8,128]{3,2,1,0:T(8,128)}, f32[7,10,8,128]{3,2,1,0:T(8,128)S(1)}, u32[]{:S(2)}, u32[]{:S(2)}) collective-permute-start(f32[7,10,8,128]{3,2,1,0:T(8,128)} %get-tuple-element.46), channel_id=1, source_target_pairs={{0,4},{4,8},{8,12},{12,16},{16,20},{20,24},{24,28},{28,32},{32,36}... | collective-permute-start | bytes 860168 | tf_op jit(solution)/shard_map/ppermute | solution.py:369
  43.0 9.3 %collective-permute-start.7 = (f32[7,10,8,128]{3,2,1,0:T(8,128)}, f32[7,10,8,128]{3,2,1,0:T(8,128)S(1)}, u32[]{:S(2)}, u32[]{:S(2)}) collective-permute-start(f32[7,10,8,128]{3,2,1,0:T(8,128)} %get-tuple-element.49), channel_id=1, source_target_pairs={{0,60},{4,0},{8,4},{12,8},{16,12},{20,16},{24,20},{28,24},{32,28},... | collective-permute-start | bytes 860168 | tf_op jit(solution)/shard_map/ppermute | solution.py:369
  46.2 6.0 %collective-permute-start.4 = (f32[7,10,8,128]{3,2,1,0:T(8,128)}, f32[7,10,8,128]{3,2,1,0:T(8,128)S(1)}, u32[]{:S(2)}, u32[]{:S(2)}) collective-permute-start(f32[7,10,8,128]{3,2,1,0:T(8,128)} %get-tuple-element.50), channel_id=1, source_target_pairs={{0,4},{4,8},{8,12},{12,16},{16,20},{20,24},{24,28},{28,32},{32,36}... | collective-permute-start | bytes 860168 | tf_op jit(solution)/shard_map/ppermute | solution.py:369
  61.7 58.5 %copy-start.1 = (f32[3,8,16,128]{3,2,1,0:T(8,128)S(1)}, f32[3,8,16,128]{3,2,1,0:T(8,128)}, u32[]{:S(2)}) copy-start(f32[3,8,16,128]{3,2,1,0:T(8,128)} %residual.1) | copy-start | bytes 589828
  61.7 58.5 %copy-start.4 = (f32[3,8,16,128]{3,2,1,0:T(8,128)S(1)}, f32[3,8,16,128]{3,2,1,0:T(8,128)}, u32[]{:S(2)}) copy-start(f32[3,8,16,128]{3,2,1,0:T(8,128)} %param.4) | copy-start | bytes 589828
  61.7 6.6 %collective-permute-start.10 = (f32[2,3,8,256]{3,2,1,0:T(8,128)S(1)}, f32[2,3,8,256]{3,2,1,0:T(8,128)S(1)}, u32[]{:S(2)}, u32[]{:S(2)}) collective-permute-start(f32[2,3,8,256]{3,2,1,0:T(8,128)S(1)} %get-tuple-element.27), channel_id=1, source_target_pairs={{0,64},{64,128},{128,192},{192,256},{256,320},{320,384},{384,448},... | collective-permute-start | bytes 147464 | tf_op jit(solution)/shard_map/ppermute | solution.py:369
  63.8 5.7 %collective-permute-start.11 = (f32[2,3,8,256]{3,2,1,0:T(8,128)S(1)}, f32[2,3,8,256]{3,2,1,0:T(8,128)S(1)}, u32[]{:S(2)}, u32[]{:S(2)}) collective-permute-start(f32[2,3,8,256]{3,2,1,0:T(8,128)S(1)} %get-tuple-element.29), channel_id=1, source_target_pairs={{0,704},{64,0},{128,64},{192,128},{256,192},{320,256},{384,320},{4... | collective-permute-start | bytes 147464 | tf_op jit(solution)/shard_map/ppermute | solution.py:369
  69.6 4.0 %collective-permute-start.12 = (f32[2,3,8,256]{3,2,1,0:T(8,128)S(1)}, f32[2,3,8,256]{3,2,1,0:T(8,128)S(1)}, u32[]{:S(2)}, u32[]{:S(2)}) collective-permute-start(f32[2,3,8,256]{3,2,1,0:T(8,128)S(1)} %get-tuple-element.30), channel_id=1, source_target_pairs={{0,4},{4,8},{8,12},{12,16},{16,20},{20,24},{24,28},{28,32},{32,36}... | collective-permute-start | bytes 147464 | tf_op jit(solution)/shard_map/ppermute | solution.py:369
  72.2 3.5 %collective-permute-start.13 = (f32[2,3,8,256]{3,2,1,0:T(8,128)S(1)}, f32[2,3,8,256]{3,2,1,0:T(8,128)S(1)}, u32[]{:S(2)}, u32[]{:S(2)}) collective-permute-start(f32[2,3,8,256]{3,2,1,0:T(8,128)S(1)} %get-tuple-element.31), channel_id=1, source_target_pairs={{0,60},{4,0},{8,4},{12,8},{16,12},{20,16},{24,20},{28,24},{32,28},... | collective-permute-start | bytes 147464 | tf_op jit(solution)/shard_map/ppermute | solution.py:369

commit v4 on v3

--- a/solution.py
+++ b/solution.py
@@ -22,7 +22,6 @@
 ZH = 16
 LIMIT = 20 * 1024 * 1024
 FIELDS = 7
-GYX = CX + 2
 
 VMEM = pl.BlockSpec(memory_space=pltpu.VMEM)
 SMEM = pl.BlockSpec(memory_space=pltpu.SMEM)
@@ -71,28 +70,41 @@
     )
 
 
-def gather_kernel(density, residual, fixed, main, to_right, to_left):
+def gather_kernel(density, residual, fixed, main, up, down):
+    f = (density[...].astype(F32) + 1.0) / BINS
+    main[0] = 0.05 + 0.95 * f * f * f
+    main[1:4] = residual[...]
+    main[4:7] = 1.0 - fixed[...].astype(F32)
+    up[...] = main[:, :, 8:16]
+    down[...] = main[:, :, 0:8]
+
+
+def edge_kernel(xl, x0, xr, to_right, to_left, up_l, down_l, up_r, down_r):
     lane = lane_of((CY, CZ))
 
-    def stage(field, values):
-        right = jnp.zeros((CY, CZ), F32)
-        left = jnp.zeros((CY, CZ), F32)
-        for x, v in enumerate(values):
-            main[field, x] = v
-            mine = (lane >= ZH * x) & (lane < ZH * (x + 1))
-            right = jnp.where(mine, pltpu.roll(v, (ZH * x + ZH) % CZ, 1), right)
-            left = jnp.where(mine, pltpu.roll(v, ZH * x, 1) if x else v, left)
-        to_right[field] = right
-        to_left[field] = left
-
-    def modulus(bins):
-        f = (bins.astype(F32) + 1.0) / BINS
-        return 0.05 + 0.95 * f * f * f
-
-    stage(0, [modulus(density[x]) for x in range(CX)])
-    for c in range(3):
-        stage(1 + c, [residual[c, x] for x in range(CX)])
-        stage(4 + c, [1.0 - fixed[c, x].astype(F32) for x in range(CX)])
+    def field(f, _):
+        for b, brick in enumerate((xl, x0, xr)):
+            right = jnp.zeros((CY, CZ), F32)
+            left = jnp.zeros((CY, CZ), F32)
+            for p in range(CX):
+                v = brick[f, p]
+                mine = (lane >= ZH * p) & (lane < ZH * (p + 1))
+                right = jnp.where(mine, pltpu.roll(v, (ZH * p + ZH) % CZ, 1) if p < 7 else v, right)
+                left = jnp.where(mine, pltpu.roll(v, ZH * p, 1) if p else v, left)
+            to_right[f, b] = right
+            to_left[f, b] = left
+        for brick, up, down in ((xl, up_l, down_l), (xr, up_r, down_r)):
+            up[f] = brick[f, :, 8:16]
+            down[f] = brick[f, :, 0:8]
+        return 0
+
+    lax.fori_loop(0, FIELDS, field, 0)
+
+
+def half_kernel(zl, zr, up, down):
+    for i, v in enumerate((zl, zr)):
+        up[:, 3 * i : 3 * i + 3] = v[:, :, 8:16]
+        down[:, 3 * i : 3 * i + 3] = v[:, :, 0:8]
 
 
 def steps(start, stop, each, body):
@@ -120,7 +132,7 @@
 
 
 def fine_kernel(
-    ends, xl, x0, xr, yll, yl0, ylr, yrl, yr0, yrr,
+    ends, xl, x0, xr, yll, yl0, ylr, yrl, yr0, yrr, zl, zr, zlower, zupper,
     ext, ux, uy, uz, inv, mux, muy, muz, mig, mc, o_right, o_left, o_own,
     mm, spring, mrhs, cx_, cy_, cz_, cg, tmp32, tmp16,
 ):
@@ -130,14 +142,13 @@
     def assemble(f, _):
         for b, (lower, brick, upper) in enumerate(((yll, xl, yrl), (yl0, x0, yr0), (ylr, xr, yrr))):
             parts = (
-                (0, 8, lambda p: lower[f, p], lane8),
-                (8, CY, lambda p: brick[f, p], lane),
-                (8 + CY, 8, lambda p: upper[f, p], lane8),
+                (0, 8, lower, zlower[f, b], zlower[f, 3 + b], lane8),
+                (8, CY, brick, zl[f, b], zr[f, b], lane),
+                (8 + CY, 8, upper, zupper[f, b], zupper[f, 3 + b], lane8),
             )
-            for start, rows, get, at in parts:
-                from_left, from_right = get(CX), get(CX + 1)
+            for start, rows, src, from_left, from_right, at in parts:
                 for p in range(CX):
-                    v = get(p)
+                    v = src[f, p]
                     le = pltpu.roll(from_left, (CZ - ZH - ZH * p) % CZ, 1) if p < 7 else from_left
                     ri = pltpu.roll(from_right, CZ - ZH * p, 1) if p else from_right
                     ext[f, CX * b + p, start : start + rows, 0:CZ] = v
@@ -368,14 +379,16 @@
         up, down = v if isinstance(v, tuple) else (v, v)
         return lax.ppermute(up, axes, ring(count, 1)), lax.ppermute(down, axes, ring(count, -1))
 
-    main, to_right, to_left = call(gather_kernel, [(FIELDS, CX, CY, CZ), (FIELDS, CY, CZ), (FIELDS, CY, CZ)])(
-        density_bins, residual, fixed_dofs
-    )
+    brick, slab = (FIELDS, CX, CY, CZ), (FIELDS, CX, 8, CZ)
+    packs, halves = (FIELDS, 3, CY, CZ), (FIELDS, 6, 8, CZ)
+    x0, up, down = call(gather_kernel, [brick, slab, slab])(density_bins, residual, fixed_dofs)
+    xl, xr = both(x0, "gx", nx)
+    yl0, yr0 = both((up, down), y_axes, ny)
+    to_right, to_left, up_l, down_l, up_r, down_r = call(edge_kernel, [packs, packs, slab, slab, slab, slab])(xl, x0, xr)
     zl, zr = both((to_right, to_left), "gz", nz)
-    x0 = jnp.concatenate([main, zl[:, None], zr[:, None]], axis=1)
-    xl, xr = both(x0, "gx", nx)
-    halves = [both((v[:, :, 8:16], v[:, :, 0:8]), y_axes, ny) for v in (xl, x0, xr)]
-    yl, yr = zip(*halves)
+    yll, yrl = both((up_l, down_l), y_axes, ny)
+    ylr, yrr = both((up_r, down_r), y_axes, ny)
+    zlower, zupper = both(tuple(call(half_kernel, [halves, halves])(zl, zr)), y_axes, ny)
 
     full = (12, ROWS, LANES)
     half = (8, ROWS // 2, LANES)
@@ -388,11 +401,11 @@
     fine = pl.pallas_call(
         fine_kernel,
         out_shape=[jax.ShapeDtypeStruct(s, F32) for s in outs],
-        in_specs=[SMEM] + [VMEM] * 9,
+        in_specs=[SMEM] + [VMEM] * 13,
         out_specs=[VMEM] * len(outs),
         scratch_shapes=[pltpu.VMEM(s, F32) for s in scratch],
         compiler_params=pltpu.CompilerParams(vmem_limit_bytes=LIMIT),
-    )(ends, xl, x0, xr, *yl, *yr)
+    )(ends, xl, x0, xr, yll, yl0, ylr, yrl, yr0, yrr, zl, zr, zlower, zupper)
     kept, (to_right, to_left, own) = fine[:-3], fine[-3:]
     cl, cr = both((to_right, to_left), "gx", nx)
     up, down = call(turn_kernel, [(2, 3, 8, LANES)] * 2)(cl, own, cr)

time: 122 us -> 124 us (1.016)
  local copies, waits for them, and re-layouts: 5.33 us -> 2.82 us
  Pallas kernels: 17.9 us -> 20.3 us
  waiting for transfers between devices: 14.3 us -> 16.2 us
    ppermute x7 -> x8, waiting for transfers between devices: 0.72 us -> 5.72 us  [both(): lax.ppermute(up, axes, ring(count, 1))]
    ppermute x7 -> x8, waiting for transfers between devices: 13.6 us -> 10.5 us  [both(): lax.ppermute(down, axes, ring(count, -1))]
    slice x3 -> x0, local copies, waits for them, and re-layouts: 2.5 us -> none  [shards(): v[:, :, 0:8]]
    pallas_call x1 -> x3, Pallas kernels: 0.28 us -> 2.72 us  [the longest x1 1.91 us: shards(): call(edge_kernel, [packs, packs, slab, slab, slab, slab])(xl, x0, xr)]
    ppermute x7 -> x8, starting transfers between devices: 31.4 us -> 32.5 us  [both(): lax.ppermute(down, axes, ring(count, -1))]
    ppermute x7 -> x8, starting transfers between devices: 14.1 us -> 13.2 us  [both(): lax.ppermute(up, axes, ring(count, 1))]
  transfers between devices with their start and end apart: 14 -> 16, of which waited for: 6 -> 8; matrix products, arithmetic and copies ran while one was open for 2% -> 0% of each run, Pallas kernels for 0% -> 2%
where the time goes in v4:
time: 124 us
  starting transfers between devices  45.8 us (37%)
  blocking collectives  36.1 us (29%)
  Pallas kernels  20.3 us (16%)
  waiting for transfers between devices  16.2 us (13%)
  local copies, waits for them, and re-layouts  2.82 us (2%)
  other arithmetic  1.81 us (1%)
    all_to_all x2, blocking collectives, all_sum(): return lax.all_to_all(sent, axes, 0, 0).sum(axis=0)  36.1 us
    ppermute x8, starting transfers between devices, both(): lax.ppermute(down, axes, ring(count, -1))  32.5 us
    ppermute x8, starting transfers between devices, both(): lax.ppermute(up, axes, ring(count, 1))  13.2 us
    ppermute x8, waiting for transfers between devices, both(): lax.ppermute(down, axes, ring(count, -1))  10.5 us
    pallas_call x1, Pallas kernels, shards(): pl.pallas_call(fine_kernel, out_shape=[jax.ShapeDtypeStruct(s, F32) for s...  9.47 us
    pallas_call x1, Pallas kernels, shards(): call(solve_kernel, [(3, CX, CY, CZ), (3, CX, CY, CZ), (2, CZ)], [(16, LAN...  8.09 us
    ppermute x8, waiting for transfers between devices, both(): lax.ppermute(up, axes, ring(count, 1))  5.72 us
    unnamed x10, local copies, waits for them, and re-layouts  2.7 us
  transfers between devices with their start and end apart: 16, of which 8 were waited for; matrix products, arithmetic and copies ran while one was open for 0% of the time, Pallas kernels for 2%

profile of v4, /device:TPU:1, one launch (start us, length us, event | category | flops | bytes accessed | tf_op | source)
XLA Modules:
  0.0 123.8 jit_solution(14612861264981796227)
XLA Ops:
  0.6 0.0 copy-start
  0.6 0.9 copy-done
  1.6 0.9 copy-done.2
  2.5 0.8 copy-done.3
  3.3 0.1 shard_map.67
  3.4 15.1 %collective-permute-start.1 = (f32[7,8,16,128]{3,2,1,0:T(8,128)S(1)}, f32[7,8,16,128]{3,2,1,0:T(8,128)S(1)}, u32[]{:S(2)}, u32[]{:S(2)}) collective-permute-start(f32[7,8,16,128]{3,2,1,0:T(8,128)S(1)} %get-tuple-element.32.x0), channel_id=1, source_target_pairs={{0,704},{64,0},{128,64},{192,128},{256,192},{320,256},{384,320},{4... | collective-permute-start | bytes 1376264 | tf_op jit(solution)/shard_map/ppermute | solution.py:380
  18.5 1.9 %collective-permute-start = (f32[7,8,16,128]{3,2,1,0:T(8,128)S(1)}, f32[7,8,16,128]{3,2,1,0:T(8,128)S(1)}, u32[]{:S(2)}, u32[]{:S(2)}) collective-permute-start(f32[7,8,16,128]{3,2,1,0:T(8,128)S(1)} %get-tuple-element.32.x0), channel_id=1, source_target_pairs={{0,64},{64,128},{128,192},{192,256},{256,320},{320,384},{384,448},... | collective-permute-start | bytes 1376264 | tf_op jit(solution)/shard_map/ppermute | solution.py:380
  20.5 2.1 %collective-permute-start.3 = (f32[7,8,8,128]{3,2,1,0:T(8,128)S(1)}, f32[7,8,8,128]{3,2,1,0:T(8,128)S(1)}, u32[]{:S(2)}, u32[]{:S(2)}) collective-permute-start(f32[7,8,8,128]{3,2,1,0:T(8,128)S(1)} %get-tuple-element.34), channel_id=1, source_target_pairs={{0,4},{4,8},{8,12},{12,16},{16,20},{20,24},{24,28},{28,32},{32,36}... | collective-permute-start | bytes 688136 | tf_op jit(solution)/shard_map/ppermute | solution.py:380
  22.6 5.1 %collective-permute-done.1.xr = f32[7,8,16,128]{3,2,1,0:T(8,128)S(1)} collective-permute-done((f32[7,8,16,128]{3,2,1,0:T(8,128)S(1)}, f32[7,8,16,128]{3,2,1,0:T(8,128)S(1)}, u32[]{:S(2)}, u32[]{:S(2)}) %collective-permute-start.1) | collective-permute-done | bytes 458784 | tf_op jit(solution)/shard_map/ppermute | solution.py:380
  27.7 5.0 %collective-permute-done.xl = f32[7,8,16,128]{3,2,1,0:T(8,128)S(1)} collective-permute-done((f32[7,8,16,128]{3,2,1,0:T(8,128)S(1)}, f32[7,8,16,128]{3,2,1,0:T(8,128)S(1)}, u32[]{:S(2)}, u32[]{:S(2)}) %collective-permute-start) | collective-permute-done | bytes 458784 | tf_op jit(solution)/shard_map/ppermute | solution.py:380
  32.7 1.9 %shard_map.68 = (f32[7,3,16,128]{3,2,1,0:T(8,128)S(1)}, f32[7,3,16,128]{3,2,1,0:T(8,128)S(1)}, f32[7,8,8,128]{3,2,1,0:T(8,128)S(1)}, f32[7,8,8,128]{3,2,1,0:T(8,...) custom-call(f32[7,8,16,128]{3,2,1,0:T(8,128)S(1)} %collective-permute-done.xl, ...), custom_call_target="tpu_custom_call" | custom-call | tf_op jit(solution)/shard_map/pallas_call | solution.py:387
  34.6 3.1 %collective-permute-start.8 = (f32[7,3,16,128]{3,2,1,0:T(8,128)S(1)}, f32[7,3,16,128]{3,2,1,0:T(8,128)S(1)}, u32[]{:S(2)}, u32[]{:S(2)}) collective-permute-start(f32[7,3,16,128]{3,2,1,0:T(8,128)S(1)} %get-tuple-element.39), channel_id=1, source_target_pairs={{0,1},{1,2},{2,3},{3,0},{4,5},{5,6},{6,7},{7,4},{8,9},{9,10},{10,1... | collective-permute-start | bytes 516104 | tf_op jit(solution)/shard_map/ppermute | solution.py:380
  37.7 2.2 %collective-permute-start.6 = (f32[7,8,8,128]{3,2,1,0:T(8,128)S(1)}, f32[7,8,8,128]{3,2,1,0:T(8,128)S(1)}, u32[]{:S(2)}, u32[]{:S(2)}) collective-permute-start(f32[7,8,8,128]{3,2,1,0:T(8,128)S(1)} %get-tuple-element.37), channel_id=1, source_target_pairs={{0,60},{4,0},{8,4},{12,8},{16,12},{20,16},{24,20},{28,24},{32,28},... | collective-permute-start | bytes 688136 | tf_op jit(solution)/shard_map/ppermute | solution.py:380
  39.9 3.4 %collective-permute-start.9 = (f32[7,3,16,128]{3,2,1,0:T(8,128)S(1)}, f32[7,3,16,128]{3,2,1,0:T(8,128)S(1)}, u32[]{:S(2)}, u32[]{:S(2)}) collective-permute-start(f32[7,3,16,128]{3,2,1,0:T(8,128)S(1)} %get-tuple-element.40), channel_id=1, source_target_pairs={{0,3},{1,0},{2,1},{3,2},{4,7},{5,4},{6,5},{7,6},{8,11},{9,8},{10,9... | collective-permute-start | bytes 516104 | tf_op jit(solution)/shard_map/ppermute | solution.py:380
  43.3 1.5 %collective-permute-start.2 = (f32[7,8,8,128]{3,2,1,0:T(8,128)S(1)}, f32[7,8,8,128]{3,2,1,0:T(8,128)S(1)}, u32[]{:S(2)}, u32[]{:S(2)}) collective-permute-start(f32[7,8,8,128]{3,2,1,0:T(8,128)S(1)} %get-tuple-element.33), channel_id=1, source_target_pairs={{0,4},{4,8},{8,12},{12,16},{16,20},{20,24},{24,28},{28,32},{32,36}... | collective-permute-start | bytes 688136 | tf_op jit(solution)/shard_map/ppermute | solution.py:380
  44.8 0.0 collective-permute-done.3.yl0
  44.8 0.2 collective-permute-start.4
  45.0 0.0 collective-permute-done.8.zl
  45.0 0.3 collective-permute-start.5
  45.3 0.8 collective-permute-done.9.zr
  46.0 2.6 %collective-permute-start.7 = (f32[7,8,8,128]{3,2,1,0:T(8,128)}, f32[7,8,8,128]{3,2,1,0:T(8,128)S(1)}, u32[]{:S(2)}, u32[]{:S(2)}) collective-permute-start(f32[7,8,8,128]{3,2,1,0:T(8,128)} %get-tuple-element.38), channel_id=1, source_target_pairs={{0,60},{4,0},{8,4},{12,8},{16,12},{20,16},{24,20},{28,24},{32,28},... | collective-permute-start | bytes 688136 | tf_op jit(solution)/shard_map/ppermute | solution.py:380
  48.6 0.7 shard_map.69
  49.4 0.0 collective-permute-done.6.yr0
  49.4 1.1 collective-permute-start.10
  50.5 0.0 collective-permute-done.2.yll
  50.5 1.6 %collective-permute-start.11 = (f32[7,6,8,128]{3,2,1,0:T(8,128)}, f32[7,6,8,128]{3,2,1,0:T(8,128)S(1)}, u32[]{:S(2)}, u32[]{:S(2)}) collective-permute-start(f32[7,6,8,128]{3,2,1,0:T(8,128)} %get-tuple-element.42), channel_id=1, source_target_pairs={{0,60},{4,0},{8,4},{12,8},{16,12},{20,16},{24,20},{28,24},{32,28},... | collective-permute-start | bytes 516104 | tf_op jit(solution)/shard_map/ppermute | solution.py:380
  52.1 0.1 stack.27
  52.2 0.0 collective-permute-done.4.ylr
  52.2 0.0 collective-permute-done.5.yrl
  52.2 1.5 %collective-permute-done.7.yrr = f32[7,8,8,128]{3,2,1,0:T(8,128)S(1)} collective-permute-done((f32[7,8,8,128]{3,2,1,0:T(8,128)}, f32[7,8,8,128]{3,2,1,0:T(8,128)S(1)}, u32[]{:S(2)}, u32[]{:S(2)}) %collective-permute-start.7) | collective-permute-done | bytes 229408 | tf_op jit(solution)/shard_map/ppermute | solution.py:380
  53.7 0.0 collective-permute-done.10.zlower
  53.7 1.8 %collective-permute-done.11.zupper = f32[7,6,8,128]{3,2,1,0:T(8,128)S(1)} collective-permute-done((f32[7,6,8,128]{3,2,1,0:T(8,128)}, f32[7,6,8,128]{3,2,1,0:T(8,128)S(1)}, u32[]{:S(2)}, u32[]{:S(2)}) %collective-permute-start.11) | collective-permute-done | bytes 172064 | tf_op jit(solution)/shard_map/ppermute | solution.py:380
  55.5 9.5 %shard_map.70 = (f32[7,24,32,256]{3,2,1,0:T(8,128)S(1)}, f32[24,32,256]{2,1,0:T(8,128)S(1)}, f32[24,32,256]{2,1,0:T(8,128)S(1)}, f32[24,32,256]{2,1,0:T(8,128)S(...) custom-call(s32[6]{0:T(128)S(1)} %convert_element_type.3.ends, ...), custom_call_target="tpu_custom_call" | custom-call | tf_op jit(solution)/shard_map/pallas_call | solution.py:401
  65.0 0.0 copy-start.1
  65.0 0.0 copy-start.4
  65.1 2.1 %collective-permute-start.12 = (f32[2,3,8,256]{3,2,1,0:T(8,128)S(1)}, f32[2,3,8,256]{3,2,1,0:T(8,128)S(1)}, u32[]{:S(2)}, u32[]{:S(2)}) collective-permute-start(f32[2,3,8,256]{3,2,1,0:T(8,128)S(1)} %get-tuple-element.43), channel_id=1, source_target_pairs={{0,64},{64,128},{128,192},{192,256},{256,320},{320,384},{384,448},... | collective-permute-start | bytes 147464 | tf_op jit(solution)/shard_map/ppermute | solution.py:380
  67.1 4.6 %collective-permute-start.13 = (f32[2,3,8,256]{3,2,1,0:T(8,128)S(1)}, f32[2,3,8,256]{3,2,1,0:T(8,128)S(1)}, u32[]{:S(2)}, u32[]{:S(2)}) collective-permute-start(f32[2,3,8,256]{3,2,1,0:T(8,128)S(1)} %get-tuple-element.45), channel_id=1, source_target_pairs={{0,704},{64,0},{128,64},{192,128},{256,192},{320,256},{384,320},{4... | collective-permute-start | bytes 147464 | tf_op jit(solution)/shard_map/ppermute | solution.py:380
  71.7 0.0 collective-permute-done.12.xl
  71.7 1.1 collective-permute-done.13.xr
  72.9 1.2 collective-permute-start.14
  74.1 2.8 %collective-permute-start.15 = (f32[2,3,8,256]{3,2,1,0:T(8,128)S(1)}, f32[2,3,8,256]{3,2,1,0:T(8,128)S(1)}, u32[]{:S(2)}, u32[]{:S(2)}) collective-permute-start(f32[2,3,8,256]{3,2,1,0:T(8,128)S(1)} %get-tuple-element.47), channel_id=1, source_target_pairs={{0,60},{4,0},{8,4},{12,8},{16,12},{20,16},{24,20},{28,24},{32,28},... | collective-permute-start | bytes 147464 | tf_op jit(solution)/shard_map/ppermute | solution.py:380
  76.9 0.7 collective-permute-done.14.yl
  77.6 0.2 collective-permute-done.15.yr
  77.8 8.1 %shard_map.72 = (f32[3,8,16,128]{3,2,1,0:T(8,128)}, f32[3,8,16,128]{3,2,1,0:T(8,128)S(1)}, f32[2,128]{1,0:T(2,128)S(1)}) custom-call(f32[2,3,8,256]{3,2,1,0:T(8,128)S(1)} %collective-permute-done.12.xl, f32[2,2,8,256]{3,2,1,0:T(8,128)S(1)} %get-tuple-element.44.own, f32[2,3,8,256]{3,2,1,0:T(8,128)S(1)} %collective-permute-done.13.xr, ...), custom_call_target="tpu_custom_call" | custom-call | tf_op jit(solution)/shard_map/pallas_call | solution.py:413
  85.9 19.3 %all_to_all.10 = f32[32,2,128]{2,1,0:T(2,128)S(1)} all-to-all(f32[32,2,128]{2,1,0:T(2,128)S(1)} %broadcast_in_dim.4), channel_id=1, replica_groups=mesh['gx'=12,'gc'=8,'co'=2,'gz'=4] {'gc','gz'}, dimensions={0} | all-to-all | bytes 65536 | tf_op jit(solution)/shard_map/all_to_all | solution.py:367
  105.3 16.8 %all_to_all.11 = f32[24,2,128]{2,1,0:T(2,128)S(1)} all-to-all(f32[24,2,128]{2,1,0:T(2,128)S(1)} %broadcast_in_dim.5), channel_id=1, replica_groups=mesh['gx'=12,'gc'=8,'co'=2,'gz'=4] {'gx','co'}, dimensions={0} | all-to-all | bytes 49152 | tf_op jit(solution)/shard_map/all_to_all | solution.py:367
  122.1 0.0 copy-done.1
  122.1 1.7 %multiply_subtract_fusion = (f32[3,8,16,128]{3,2,1,0:T(8,128)}, f32[3,8,16,128]{3,2,1,0:T(8,128)}) fusion(f32[3,8,16,128]{3,2,1,0:T(8,128)S(1)} %copy-done.1, f32[3,8,16,128]{3,2,1,0:T(8,128)S(1)} %get-tuple-element.60, f32[128]{0:T(128)S(1)} %fusion, f32[3,8,16,128]{3,2,1,0:T(8,128)S(1)} %copy-done.4, f32[3,8,16,128]{3,2,1,0:T(8,128)} %get-tuple-element.31), kind=kLoop, calls=%fused_computation | loop fusion | flops 196608 | bytes 1180160 | tf_op jit(solution)/shard_map/sub | solution.py:420
  (10 shorter events, 0.2 us)
Async XLA Ops:
  0.6 0.9 copy-start
  1.6 0.9 copy-start.2
  2.5 0.8 copy-start.3
  3.4 24.3 %collective-permute-start.1 = (f32[7,8,16,128]{3,2,1,0:T(8,128)S(1)}, f32[7,8,16,128]{3,2,1,0:T(8,128)S(1)}, u32[]{:S(2)}, u32[]{:S(2)}) collective-permute-start(f32[7,8,16,128]{3,2,1,0:T(8,128)S(1)} %get-tuple-element.32.x0), channel_id=1, source_target_pairs={{0,704},{64,0},{128,64},{192,128},{256,192},{320,256},{384,320},{4... | collective-permute-start | bytes 1376264 | tf_op jit(solution)/shard_map/ppermute | solution.py:380
  18.5 14.2 %collective-permute-start = (f32[7,8,16,128]{3,2,1,0:T(8,128)S(1)}, f32[7,8,16,128]{3,2,1,0:T(8,128)S(1)}, u32[]{:S(2)}, u32[]{:S(2)}) collective-permute-start(f32[7,8,16,128]{3,2,1,0:T(8,128)S(1)} %get-tuple-element.32.x0), channel_id=1, source_target_pairs={{0,64},{64,128},{128,192},{192,256},{256,320},{320,384},{384,448},... | collective-permute-start | bytes 1376264 | tf_op jit(solution)/shard_map/ppermute | solution.py:380
  20.5 24.3 %collective-permute-start.3 = (f32[7,8,8,128]{3,2,1,0:T(8,128)S(1)}, f32[7,8,8,128]{3,2,1,0:T(8,128)S(1)}, u32[]{:S(2)}, u32[]{:S(2)}) collective-permute-start(f32[7,8,8,128]{3,2,1,0:T(8,128)S(1)} %get-tuple-element.34), channel_id=1, source_target_pairs={{0,4},{4,8},{8,12},{12,16},{16,20},{20,24},{24,28},{28,32},{32,36}... | collective-permute-start | bytes 688136 | tf_op jit(solution)/shard_map/ppermute | solution.py:380
  34.6 10.4 %collective-permute-start.8 = (f32[7,3,16,128]{3,2,1,0:T(8,128)S(1)}, f32[7,3,16,128]{3,2,1,0:T(8,128)S(1)}, u32[]{:S(2)}, u32[]{:S(2)}) collective-permute-start(f32[7,3,16,128]{3,2,1,0:T(8,128)S(1)} %get-tuple-element.39), channel_id=1, source_target_pairs={{0,1},{1,2},{2,3},{3,0},{4,5},{5,6},{6,7},{7,4},{8,9},{9,10},{10,1... | collective-permute-start | bytes 516104 | tf_op jit(solution)/shard_map/ppermute | solution.py:380
  37.7 11.6 %collective-permute-start.6 = (f32[7,8,8,128]{3,2,1,0:T(8,128)S(1)}, f32[7,8,8,128]{3,2,1,0:T(8,128)S(1)}, u32[]{:S(2)}, u32[]{:S(2)}) collective-permute-start(f32[7,8,8,128]{3,2,1,0:T(8,128)S(1)} %get-tuple-element.37), channel_id=1, source_target_pairs={{0,60},{4,0},{8,4},{12,8},{16,12},{20,16},{24,20},{28,24},{32,28},... | collective-permute-start | bytes 688136 | tf_op jit(solution)/shard_map/ppermute | solution.py:380
  39.9 6.1 %collective-permute-start.9 = (f32[7,3,16,128]{3,2,1,0:T(8,128)S(1)}, f32[7,3,16,128]{3,2,1,0:T(8,128)S(1)}, u32[]{:S(2)}, u32[]{:S(2)}) collective-permute-start(f32[7,3,16,128]{3,2,1,0:T(8,128)S(1)} %get-tuple-element.40), channel_id=1, source_target_pairs={{0,3},{1,0},{2,1},{3,2},{4,7},{5,4},{6,5},{7,6},{8,11},{9,8},{10,9... | collective-permute-start | bytes 516104 | tf_op jit(solution)/shard_map/ppermute | solution.py:380
  43.3 7.2 %collective-permute-start.2 = (f32[7,8,8,128]{3,2,1,0:T(8,128)S(1)}, f32[7,8,8,128]{3,2,1,0:T(8,128)S(1)}, u32[]{:S(2)}, u32[]{:S(2)}) collective-permute-start(f32[7,8,8,128]{3,2,1,0:T(8,128)S(1)} %get-tuple-element.33), channel_id=1, source_target_pairs={{0,4},{4,8},{8,12},{12,16},{16,20},{20,24},{24,28},{28,32},{32,36}... | collective-permute-start | bytes 688136 | tf_op jit(solution)/shard_map/ppermute | solution.py:380
  44.8 7.5 %collective-permute-start.4 = (f32[7,8,8,128]{3,2,1,0:T(8,128)}, f32[7,8,8,128]{3,2,1,0:T(8,128)S(1)}, u32[]{:S(2)}, u32[]{:S(2)}) collective-permute-start(f32[7,8,8,128]{3,2,1,0:T(8,128)} %get-tuple-element.35), channel_id=1, source_target_pairs={{0,4},{4,8},{8,12},{12,16},{16,20},{20,24},{24,28},{28,32},{32,36}... | collective-permute-start | bytes 688136 | tf_op jit(solution)/shard_map/ppermute | solution.py:380
  45.0 7.3 %collective-permute-start.5 = (f32[7,8,8,128]{3,2,1,0:T(8,128)}, f32[7,8,8,128]{3,2,1,0:T(8,128)S(1)}, u32[]{:S(2)}, u32[]{:S(2)}) collective-permute-start(f32[7,8,8,128]{3,2,1,0:T(8,128)} %get-tuple-element.36), channel_id=1, source_target_pairs={{0,60},{4,0},{8,4},{12,8},{16,12},{20,16},{24,20},{28,24},{32,28},... | collective-permute-start | bytes 688136 | tf_op jit(solution)/shard_map/ppermute | solution.py:380
  46.0 7.7 %collective-permute-start.7 = (f32[7,8,8,128]{3,2,1,0:T(8,128)}, f32[7,8,8,128]{3,2,1,0:T(8,128)S(1)}, u32[]{:S(2)}, u32[]{:S(2)}) collective-permute-start(f32[7,8,8,128]{3,2,1,0:T(8,128)} %get-tuple-element.38), channel_id=1, source_target_pairs={{0,60},{4,0},{8,4},{12,8},{16,12},{20,16},{24,20},{28,24},{32,28},... | collective-permute-start | bytes 688136 | tf_op jit(solution)/shard_map/ppermute | solution.py:380
  49.4 4.3 %collective-permute-start.10 = (f32[7,6,8,128]{3,2,1,0:T(8,128)}, f32[7,6,8,128]{3,2,1,0:T(8,128)S(1)}, u32[]{:S(2)}, u32[]{:S(2)}) collective-permute-start(f32[7,6,8,128]{3,2,1,0:T(8,128)} %get-tuple-element.41), channel_id=1, source_target_pairs={{0,4},{4,8},{8,12},{12,16},{16,20},{20,24},{24,28},{28,32},{32,36}... | collective-permute-start | bytes 516104 | tf_op jit(solution)/shard_map/ppermute | solution.py:380
  50.5 5.0 %collective-permute-start.11 = (f32[7,6,8,128]{3,2,1,0:T(8,128)}, f32[7,6,8,128]{3,2,1,0:T(8,128)S(1)}, u32[]{:S(2)}, u32[]{:S(2)}) collective-permute-start(f32[7,6,8,128]{3,2,1,0:T(8,128)} %get-tuple-element.42), channel_id=1, source_target_pairs={{0,60},{4,0},{8,4},{12,8},{16,12},{20,16},{24,20},{28,24},{32,28},... | collective-permute-start | bytes 516104 | tf_op jit(solution)/shard_map/ppermute | solution.py:380
  65.0 57.1 %copy-start.1 = (f32[3,8,16,128]{3,2,1,0:T(8,128)S(1)}, f32[3,8,16,128]{3,2,1,0:T(8,128)}, u32[]{:S(2)}) copy-start(f32[3,8,16,128]{3,2,1,0:T(8,128)} %residual.1) | copy-start | bytes 589828
  65.0 57.1 %copy-start.4 = (f32[3,8,16,128]{3,2,1,0:T(8,128)S(1)}, f32[3,8,16,128]{3,2,1,0:T(8,128)}, u32[]{:S(2)}) copy-start(f32[3,8,16,128]{3,2,1,0:T(8,128)} %param.4) | copy-start | bytes 589828
  65.1 6.6 %collective-permute-start.12 = (f32[2,3,8,256]{3,2,1,0:T(8,128)S(1)}, f32[2,3,8,256]{3,2,1,0:T(8,128)S(1)}, u32[]{:S(2)}, u32[]{:S(2)}) collective-permute-start(f32[2,3,8,256]{3,2,1,0:T(8,128)S(1)} %get-tuple-element.43), channel_id=1, source_target_pairs={{0,64},{64,128},{128,192},{192,256},{256,320},{320,384},{384,448},... | collective-permute-start | bytes 147464 | tf_op jit(solution)/shard_map/ppermute | solution.py:380
  67.1 5.7 %collective-permute-start.13 = (f32[2,3,8,256]{3,2,1,0:T(8,128)S(1)}, f32[2,3,8,256]{3,2,1,0:T(8,128)S(1)}, u32[]{:S(2)}, u32[]{:S(2)}) collective-permute-start(f32[2,3,8,256]{3,2,1,0:T(8,128)S(1)} %get-tuple-element.45), channel_id=1, source_target_pairs={{0,704},{64,0},{128,64},{192,128},{256,192},{320,256},{384,320},{4... | collective-permute-start | bytes 147464 | tf_op jit(solution)/shard_map/ppermute | solution.py:380
  72.9 4.7 %collective-permute-start.14 = (f32[2,3,8,256]{3,2,1,0:T(8,128)S(1)}, f32[2,3,8,256]{3,2,1,0:T(8,128)S(1)}, u32[]{:S(2)}, u32[]{:S(2)}) collective-permute-start(f32[2,3,8,256]{3,2,1,0:T(8,128)S(1)} %get-tuple-element.46), channel_id=1, source_target_pairs={{0,4},{4,8},{8,12},{12,16},{16,20},{20,24},{24,28},{28,32},{32,36}... | collective-permute-start | bytes 147464 | tf_op jit(solution)/shard_map/ppermute | solution.py:380
  74.1 3.7 %collective-permute-start.15 = (f32[2,3,8,256]{3,2,1,0:T(8,128)S(1)}, f32[2,3,8,256]{3,2,1,0:T(8,128)S(1)}, u32[]{:S(2)}, u32[]{:S(2)}) collective-permute-start(f32[2,3,8,256]{3,2,1,0:T(8,128)S(1)} %get-tuple-element.47), channel_id=1, source_target_pairs={{0,60},{4,0},{8,4},{12,8},{16,12},{20,16},{24,20},{28,24},{32,28},... | collective-permute-start | bytes 147464 | tf_op jit(solution)/shard_map/ppermute | solution.py:380

commit v5 on v4

--- a/solution.py
+++ b/solution.py
@@ -70,32 +70,26 @@
     )
 
 
-def gather_kernel(density, residual, fixed, main, up, down):
-    f = (density[...].astype(F32) + 1.0) / BINS
-    main[0] = 0.05 + 0.95 * f * f * f
-    main[1:4] = residual[...]
-    main[4:7] = 1.0 - fixed[...].astype(F32)
-    up[...] = main[:, :, 8:16]
-    down[...] = main[:, :, 0:8]
-
-
-def edge_kernel(xl, x0, xr, to_right, to_left, up_l, down_l, up_r, down_r):
-    lane = lane_of((CY, CZ))
+def slab_kernel(brick, up, down):
+    up[...] = brick[:, :, 8:16]
+    down[...] = brick[:, :, 0:8]
+
+
+def edge_kernel(xl, x0, xr, to_right, to_left, up, down):
+    block = lane_of((CY, CZ)) // ZH
 
     def field(f, _):
         for b, brick in enumerate((xl, x0, xr)):
-            right = jnp.zeros((CY, CZ), F32)
-            left = jnp.zeros((CY, CZ), F32)
-            for p in range(CX):
-                v = brick[f, p]
-                mine = (lane >= ZH * p) & (lane < ZH * (p + 1))
-                right = jnp.where(mine, pltpu.roll(v, (ZH * p + ZH) % CZ, 1) if p < 7 else v, right)
-                left = jnp.where(mine, pltpu.roll(v, ZH * p, 1) if p else v, left)
+            turned = [pltpu.roll(brick[f, p], ZH * p, 1) if p else brick[f, p] for p in range(CX)]
+            right, left = turned[0], turned[0]
+            for p in range(1, CX):
+                right = jnp.where(block == p - 1, turned[p], right)
+                left = jnp.where(block == p, turned[p], left)
             to_right[f, b] = right
             to_left[f, b] = left
-        for brick, up, down in ((xl, up_l, down_l), (xr, up_r, down_r)):
-            up[f] = brick[f, :, 8:16]
-            down[f] = brick[f, :, 0:8]
+        for i, brick in ((0, xl), (CX, xr)):
+            up[f, i : i + CX] = brick[f, :, 8:16]
+            down[f, i : i + CX] = brick[f, :, 0:8]
         return 0
 
     lax.fori_loop(0, FIELDS, field, 0)
@@ -132,29 +126,26 @@
 
 
 def fine_kernel(
-    ends, xl, x0, xr, yll, yl0, ylr, yrl, yr0, yrr, zl, zr, zlower, zupper,
+    ends, xl, x0, xr, lower0, upper0, lower, upper, zl, zr, zlower, zupper,
     ext, ux, uy, uz, inv, mux, muy, muz, mig, mc, o_right, o_left, o_own,
     mm, spring, mrhs, cx_, cy_, cz_, cg, tmp32, tmp16,
 ):
-    lane = lane_of((CY, CZ))
-    lane8 = lane_of((8, CZ))
+    block = lane_of((CY, CZ)) // ZH
+    block8 = lane_of((8, CZ)) // ZH
 
     def assemble(f, _):
-        for b, (lower, brick, upper) in enumerate(((yll, xl, yrl), (yl0, x0, yr0), (ylr, xr, yrr))):
+        for b, brick in enumerate((xl, x0, xr)):
+            below, above, first = (lower0, upper0, 0) if b == 1 else (lower, upper, 0 if b == 0 else CX)
             parts = (
-                (0, 8, lower, zlower[f, b], zlower[f, 3 + b], lane8),
-                (8, CY, brick, zl[f, b], zr[f, b], lane),
-                (8 + CY, 8, upper, zupper[f, b], zupper[f, 3 + b], lane8),
+                (0, 8, below, first, zlower[f, b], zlower[f, 3 + b], block8),
+                (8, CY, brick, 0, zl[f, b], zr[f, b], block),
+                (8 + CY, 8, above, first, zupper[f, b], zupper[f, 3 + b], block8),
             )
-            for start, rows, src, from_left, from_right, at in parts:
+            for start, rows, src, offset, from_left, from_right, at in parts:
                 for p in range(CX):
-                    v = src[f, p]
-                    le = pltpu.roll(from_left, (CZ - ZH - ZH * p) % CZ, 1) if p < 7 else from_left
-                    ri = pltpu.roll(from_right, CZ - ZH * p, 1) if p else from_right
-                    ext[f, CX * b + p, start : start + rows, 0:CZ] = v
-                    ext[f, CX * b + p, start : start + rows, CZ:LANES] = jnp.where(
-                        at < ZH, ri, jnp.where(at >= CZ - ZH, le, v)
-                    )
+                    halo = jnp.where(at == p, from_right, from_left)
+                    ext[f, CX * b + p, start : start + rows, 0:CZ] = src[f, offset + p]
+                    ext[f, CX * b + p, start : start + rows, CZ:LANES] = pltpu.roll(halo, CZ - ZH * p, 1) if p else halo
         return 0
 
     lax.fori_loop(0, FIELDS, assemble, 0)
@@ -248,6 +239,18 @@
                 o_left[i, s - 2] = v
             if s in (2, 3):
                 o_own[i, s - 2] = v
+
+
+def unpack(v, quad, count):
+    at = {0: v}
+    for k in range(1, 4):
+        at[k] = before(v, k, 1)
+    for k in range(1, count):
+        at[-k] = after(v, k, 1)
+    return [
+        jnp.where(quad == 0, at[-j], jnp.where(quad == 1, at[1 - j], jnp.where(quad == 2, at[2 - j], at[3 - j])))
+        for j in range(count)
+    ]
 
 
 def turn_kernel(xl, own, xr, up, down):
@@ -278,8 +281,8 @@
                 packed[1 + j : 2 + j] = yl[i, j, s : s + 1]
                 packed[8 + j : 9 + j] = yr[i, j, s : s + 1]
             v = packed[...]
-            for k in range(4 if i == 0 else 3):
-                field[4 * i + k][s] = pair_sum(pair_sum(jnp.where(quad == k, v, 0.0), 1), 2)
+            for k, u in enumerate(unpack(v, quad, 4 if i == 0 else 3)):
+                field[4 * i + k][s] = u
     g = [jnp.where(v > 0.0, v, 1.0) for v in field[3]]
     inv = [1.0 / v for v in g]
     cx_, cy_, cz_ = field[4], field[5], field[6]
@@ -379,15 +382,17 @@
         up, down = v if isinstance(v, tuple) else (v, v)
         return lax.ppermute(up, axes, ring(count, 1)), lax.ppermute(down, axes, ring(count, -1))
 
-    brick, slab = (FIELDS, CX, CY, CZ), (FIELDS, CX, 8, CZ)
+    slab, slabs = (FIELDS, CX, 8, CZ), (FIELDS, 2 * CX, 8, CZ)
     packs, halves = (FIELDS, 3, CY, CZ), (FIELDS, 6, 8, CZ)
-    x0, up, down = call(gather_kernel, [brick, slab, slab])(density_bins, residual, fixed_dofs)
+    f = (density_bins.astype(F32) + 1.0) / BINS
+    modulus = 0.05 + 0.95 * f * f * f
+    x0 = jnp.concatenate([modulus[None], residual, 1.0 - fixed_dofs.astype(F32)], axis=0)
     xl, xr = both(x0, "gx", nx)
-    yl0, yr0 = both((up, down), y_axes, ny)
-    to_right, to_left, up_l, down_l, up_r, down_r = call(edge_kernel, [packs, packs, slab, slab, slab, slab])(xl, x0, xr)
+    lower0, upper0 = both(tuple(call(slab_kernel, [slab, slab])(x0)), y_axes, ny)
+    xl, xr, lower0, upper0 = lax.optimization_barrier((xl, xr, lower0, upper0))
+    to_right, to_left, up, down = call(edge_kernel, [packs, packs, slabs, slabs])(xl, x0, xr)
     zl, zr = both((to_right, to_left), "gz", nz)
-    yll, yrl = both((up_l, down_l), y_axes, ny)
-    ylr, yrr = both((up_r, down_r), y_axes, ny)
+    lower, upper = both((up, down), y_axes, ny)
     zlower, zupper = both(tuple(call(half_kernel, [halves, halves])(zl, zr)), y_axes, ny)
 
     full = (12, ROWS, LANES)
@@ -401,11 +406,11 @@
     fine = pl.pallas_call(
         fine_kernel,
         out_shape=[jax.ShapeDtypeStruct(s, F32) for s in outs],
-        in_specs=[SMEM] + [VMEM] * 13,
+        in_specs=[SMEM] + [VMEM] * 11,
         out_specs=[VMEM] * len(outs),
         scratch_shapes=[pltpu.VMEM(s, F32) for s in scratch],
         compiler_params=pltpu.CompilerParams(vmem_limit_bytes=LIMIT),
-    )(ends, xl, x0, xr, yll, yl0, ylr, yrl, yr0, yrr, zl, zr, zlower, zupper)
+    )(ends, xl, x0, xr, lower0, upper0, lower, upper, zl, zr, zlower, zupper)
     kept, (to_right, to_left, own) = fine[:-3], fine[-3:]
     cl, cr = both((to_right, to_left), "gx", nx)
     up, down = call(turn_kernel, [(2, 3, 8, LANES)] * 2)(cl, own, cr)

time: 124 us -> 122 us (0.984)
  waiting for transfers between devices: 16.2 us -> 22.3 us
  starting transfers between devices: 45.8 us -> 40.4 us
  Pallas kernels: 20.3 us -> 16 us
  other arithmetic: 1.81 us -> 4.58 us
  local copies, waits for them, and re-layouts: 2.82 us -> 0.14 us
    ppermute x8 -> x7, starting transfers between devices: 32.5 us -> 23.8 us  [both(): lax.ppermute(down, axes, ring(count, -1))]
    ppermute x8 -> x7, waiting for transfers between devices: 5.72 us -> 11.7 us  [both(): lax.ppermute(up, axes, ring(count, 1))]
    pallas_call x1, Pallas kernels: 8.09 us -> 4.48 us  [shards(): call(solve_kernel, [(3, CX, CY, CZ), (3, CX, CY, CZ), (2, CZ)], [(16, LAN...]
    ppermute x8 -> x7, starting transfers between devices: 13.2 us -> 16.6 us  [both(): lax.ppermute(up, axes, ring(count, 1))]
    unnamed x10 -> x4, local copies, waits for them, and re-layouts: 2.7 us -> 0.01 us
    ppermute x8 -> x7, waiting for transfers between devices: 10.5 us -> 10.6 us  [both(): lax.ppermute(down, axes, ring(count, -1))]
  transfers between devices with their start and end apart: 16 -> 14, of which waited for: 8 -> 10; matrix products, arithmetic and copies ran while one was open for 0% -> 0% of each run, Pallas kernels for 2% -> 1%
where the time goes in v5:
time: 122 us; the launch traced here: 121 us
  starting transfers between devices  40.4 us (33%)
  blocking collectives  37 us (30%)
  waiting for transfers between devices  22.3 us (18%)
  Pallas kernels  16 us (13%)
  other arithmetic  4.58 us (4%)
    all_to_all x2, blocking collectives, all_sum(): return lax.all_to_all(sent, axes, 0, 0).sum(axis=0)  37 us
    ppermute x7, starting transfers between devices, both(): lax.ppermute(down, axes, ring(count, -1))  23.8 us
    ppermute x7, starting transfers between devices, both(): lax.ppermute(up, axes, ring(count, 1))  16.6 us
    ppermute x7, waiting for transfers between devices, both(): lax.ppermute(up, axes, ring(count, 1))  11.7 us
    ppermute x7, waiting for transfers between devices, both(): lax.ppermute(down, axes, ring(count, -1))  10.6 us
    pallas_call x1, Pallas kernels, shards(): pl.pallas_call(fine_kernel, out_shape=[jax.ShapeDtypeStruct(s, F32) for s...  9.08 us
    pallas_call x1, Pallas kernels, shards(): call(solve_kernel, [(3, CX, CY, CZ), (3, CX, CY, CZ), (2, CZ)], [(16, LAN...  4.48 us
  transfers between devices with their start and end apart: 14, of which 10 were waited for; matrix products, arithmetic and copies ran while one was open for 0% of the time, Pallas kernels for 1%

profile of v5, /device:TPU:1, one launch (start us, length us, event | category | flops | bytes accessed | tf_op | source)
XLA Modules:
  0.0 121.1 jit_solution(6253119315894581530)
XLA Ops:
  0.6 0.9 fusion.1
  1.5 0.9 convert_subtract_fusion
  2.4 1.0 pad_maximum_fusion.brick.x0
  3.4 15.1 %collective-permute-start.1 = (f32[7,8,16,128]{3,2,1,0:T(8,128)S(1)}, f32[7,8,16,128]{3,2,1,0:T(8,128)S(1)}, u32[]{:S(2)}, u32[]{:S(2)}) collective-permute-start(f32[7,8,16,128]{3,2,1,0:T(8,128)S(1)} %pad_maximum_fusion.brick.x0), channel_id=1, source_target_pairs={{0,704},{64,0},{128,64},{192,128},{256,192},{320,256},{384,320},{4... | collective-permute-start | bytes 1376264 | tf_op jit(solution)/shard_map/ppermute | solution.py:383
  18.5 1.9 %collective-permute-start = (f32[7,8,16,128]{3,2,1,0:T(8,128)S(1)}, f32[7,8,16,128]{3,2,1,0:T(8,128)S(1)}, u32[]{:S(2)}, u32[]{:S(2)}) collective-permute-start(f32[7,8,16,128]{3,2,1,0:T(8,128)S(1)} %pad_maximum_fusion.brick.x0), channel_id=1, source_target_pairs={{0,64},{64,128},{128,192},{192,256},{256,320},{320,384},{384,448},... | collective-permute-start | bytes 1376264 | tf_op jit(solution)/shard_map/ppermute | solution.py:383
  20.5 2.1 %collective-permute-start.2 = (f32[7,8,8,128]{3,2,1,0:T(8,128)S(1)}, f32[7,8,8,128]{3,2,1,0:T(8,128)S(1)}, u32[]{:S(2)}, u32[]{:S(2)}) collective-permute-start(f32[7,8,8,128]{3,2,1,0:T(8,128)S(1)} %get-tuple-element.33), channel_id=1, source_target_pairs={{0,4},{4,8},{8,12},{12,16},{16,20},{20,24},{24,28},{28,32},{32,36}... | collective-permute-start | bytes 688136 | tf_op jit(solution)/shard_map/ppermute | solution.py:383
  22.7 0.0 collective-permute-start.3
  22.7 3.0 %collective-permute-done.2.lower0 = f32[7,8,8,128]{3,2,1,0:T(8,128)S(1)} collective-permute-done((f32[7,8,8,128]{3,2,1,0:T(8,128)S(1)}, f32[7,8,8,128]{3,2,1,0:T(8,128)S(1)}, u32[]{:S(2)}, u32[]{:S(2)}) %collective-permute-start.2) | collective-permute-done | bytes 229408 | tf_op jit(solution)/shard_map/ppermute | solution.py:383
  25.6 2.8 %collective-permute-done.3.upper0 = f32[7,8,8,128]{3,2,1,0:T(8,128)S(1)} collective-permute-done((f32[7,8,8,128]{3,2,1,0:T(8,128)S(1)}, f32[7,8,8,128]{3,2,1,0:T(8,128)S(1)}, u32[]{:S(2)}, u32[]{:S(2)}) %collective-permute-start.3) | collective-permute-done | bytes 229408 | tf_op jit(solution)/shard_map/ppermute | solution.py:383
  28.4 0.0 collective-permute-done.1.xr
  28.4 4.3 %collective-permute-done.xl = f32[7,8,16,128]{3,2,1,0:T(8,128)S(1)} collective-permute-done((f32[7,8,16,128]{3,2,1,0:T(8,128)S(1)}, f32[7,8,16,128]{3,2,1,0:T(8,128)S(1)}, u32[]{:S(2)}, u32[]{:S(2)}) %collective-permute-start) | collective-permute-done | bytes 458784 | tf_op jit(solution)/shard_map/ppermute | solution.py:383
  32.7 1.6 %shard_map.68 = (f32[7,3,16,128]{3,2,1,0:T(8,128)S(1)}, f32[7,3,16,128]{3,2,1,0:T(8,128)S(1)}, f32[7,16,8,128]{3,2,1,0:T(8,128)}, f32[7,16,8,128]{3,2,1,0:T(8,128)}) custom-call(f32[7,8,16,128]{3,2,1,0:T(8,128)S(1)} %collective-permute-done.xl, f32[7,8,16,128]{3,2,1,0:T(8,128)S(1)} %pad_maximum_fusion.brick.x0, f32[7,8,16,128]{3,2,1,0:T(8,128)S(1)} %collective-permute-done.1.xr), custom_call_target="tpu_custom_call" | custom-call | tf_op jit(solution)/shard_map/pallas_call | solution.py:393
  34.4 3.0 %collective-permute-start.4 = (f32[7,16,8,128]{3,2,1,0:T(8,128)}, f32[7,16,8,128]{3,2,1,0:T(8,128)S(1)}, u32[]{:S(2)}, u32[]{:S(2)}) collective-permute-start(f32[7,16,8,128]{3,2,1,0:T(8,128)} %get-tuple-element.39), channel_id=1, source_target_pairs={{0,4},{4,8},{8,12},{12,16},{16,20},{20,24},{24,28},{28,32},{32,36}... | collective-permute-start | bytes 1376264 | tf_op jit(solution)/shard_map/ppermute | solution.py:383
  37.4 0.0 collective-permute-start.5
  37.4 3.1 %collective-permute-start.6 = (f32[7,3,16,128]{3,2,1,0:T(8,128)S(1)}, f32[7,3,16,128]{3,2,1,0:T(8,128)S(1)}, u32[]{:S(2)}, u32[]{:S(2)}) collective-permute-start(f32[7,3,16,128]{3,2,1,0:T(8,128)S(1)} %get-tuple-element.41), channel_id=1, source_target_pairs={{0,1},{1,2},{2,3},{3,0},{4,5},{5,6},{6,7},{7,4},{8,9},{9,10},{10,1... | collective-permute-start | bytes 516104 | tf_op jit(solution)/shard_map/ppermute | solution.py:383
  40.5 3.4 %collective-permute-start.7 = (f32[7,3,16,128]{3,2,1,0:T(8,128)S(1)}, f32[7,3,16,128]{3,2,1,0:T(8,128)S(1)}, u32[]{:S(2)}, u32[]{:S(2)}) collective-permute-start(f32[7,3,16,128]{3,2,1,0:T(8,128)S(1)} %get-tuple-element.42), channel_id=1, source_target_pairs={{0,3},{1,0},{2,1},{3,2},{4,7},{5,4},{6,5},{7,6},{8,11},{9,8},{10,9... | collective-permute-start | bytes 516104 | tf_op jit(solution)/shard_map/ppermute | solution.py:383
  43.9 1.1 collective-permute-done.6.zl
  45.1 1.9 %collective-permute-done.7.zr = f32[7,3,16,128]{3,2,1,0:T(8,128)S(1)} collective-permute-done((f32[7,3,16,128]{3,2,1,0:T(8,128)S(1)}, f32[7,3,16,128]{3,2,1,0:T(8,128)S(1)}, u32[]{:S(2)}, u32[]{:S(2)}) %collective-permute-start.7) | collective-permute-done | bytes 172064 | tf_op jit(solution)/shard_map/ppermute | solution.py:383
  47.0 0.7 shard_map.69
  47.7 3.4 %collective-permute-start.8 = (f32[7,6,8,128]{3,2,1,0:T(8,128)}, f32[7,6,8,128]{3,2,1,0:T(8,128)S(1)}, u32[]{:S(2)}, u32[]{:S(2)}) collective-permute-start(f32[7,6,8,128]{3,2,1,0:T(8,128)} %get-tuple-element.43), channel_id=1, source_target_pairs={{0,4},{4,8},{8,12},{12,16},{16,20},{20,24},{24,28},{28,32},{32,36}... | collective-permute-start | bytes 516104 | tf_op jit(solution)/shard_map/ppermute | solution.py:383
  51.1 0.0 collective-permute-start.9
  51.1 0.1 stack.27
  51.3 2.6 %collective-permute-done.8.zlower = f32[7,6,8,128]{3,2,1,0:T(8,128)S(1)} collective-permute-done((f32[7,6,8,128]{3,2,1,0:T(8,128)}, f32[7,6,8,128]{3,2,1,0:T(8,128)S(1)}, u32[]{:S(2)}, u32[]{:S(2)}) %collective-permute-start.8) | collective-permute-done | bytes 172064 | tf_op jit(solution)/shard_map/ppermute | solution.py:383
  53.8 2.7 %collective-permute-done.9.zupper = f32[7,6,8,128]{3,2,1,0:T(8,128)S(1)} collective-permute-done((f32[7,6,8,128]{3,2,1,0:T(8,128)}, f32[7,6,8,128]{3,2,1,0:T(8,128)S(1)}, u32[]{:S(2)}, u32[]{:S(2)}) %collective-permute-start.9) | collective-permute-done | bytes 172064 | tf_op jit(solution)/shard_map/ppermute | solution.py:383
  56.5 0.0 collective-permute-done.4.lower
  56.5 0.0 collective-permute-done.5.upper
  56.5 9.1 %shard_map.70 = (f32[7,24,32,256]{3,2,1,0:T(8,128)S(1)}, f32[24,32,256]{2,1,0:T(8,128)S(1)}, f32[24,32,256]{2,1,0:T(8,128)S(1)}, f32[24,32,256]{2,1,0:T(8,128)S(...) custom-call(s32[6]{0:T(128)S(1)} %convert_element_type.9.ends, ...), custom_call_target="tpu_custom_call" | custom-call | tf_op jit(solution)/shard_map/pallas_call | solution.py:406
  65.6 0.0 copy-start
  65.6 0.0 copy-start.1
  65.6 2.1 %collective-permute-start.10 = (f32[2,3,8,256]{3,2,1,0:T(8,128)S(1)}, f32[2,3,8,256]{3,2,1,0:T(8,128)S(1)}, u32[]{:S(2)}, u32[]{:S(2)}) collective-permute-start(f32[2,3,8,256]{3,2,1,0:T(8,128)S(1)} %get-tuple-element.45), channel_id=1, source_target_pairs={{0,64},{64,128},{128,192},{192,256},{256,320},{320,384},{384,448},... | collective-permute-start | bytes 147464 | tf_op jit(solution)/shard_map/ppermute | solution.py:383
  67.7 4.6 %collective-permute-start.11 = (f32[2,3,8,256]{3,2,1,0:T(8,128)S(1)}, f32[2,3,8,256]{3,2,1,0:T(8,128)S(1)}, u32[]{:S(2)}, u32[]{:S(2)}) collective-permute-start(f32[2,3,8,256]{3,2,1,0:T(8,128)S(1)} %get-tuple-element.47), channel_id=1, source_target_pairs={{0,704},{64,0},{128,64},{192,128},{256,192},{320,256},{384,320},{4... | collective-permute-start | bytes 147464 | tf_op jit(solution)/shard_map/ppermute | solution.py:383
  72.2 0.0 collective-permute-done.10.xl
  72.2 1.1 collective-permute-done.11.xr
  73.4 0.9 collective-permute-start.12
  74.3 0.7 collective-permute-start.13
  75.0 0.7 collective-permute-done.12.yl
  75.7 2.1 %collective-permute-done.13.yr = f32[2,3,8,256]{3,2,1,0:T(8,128)S(1)} collective-permute-done((f32[2,3,8,256]{3,2,1,0:T(8,128)S(1)}, f32[2,3,8,256]{3,2,1,0:T(8,128)S(1)}, u32[]{:S(2)}, u32[]{:S(2)}) %collective-permute-start.13) | collective-permute-done | bytes 49184 | tf_op jit(solution)/shard_map/ppermute | solution.py:383
  77.9 4.5 %shard_map.72 = (f32[3,8,16,128]{3,2,1,0:T(8,128)}, f32[3,8,16,128]{3,2,1,0:T(8,128)S(1)}, f32[2,128]{1,0:T(2,128)S(1)}) custom-call(f32[2,3,8,256]{3,2,1,0:T(8,128)S(1)} %collective-permute-done.10.xl, f32[2,2,8,256]{3,2,1,0:T(8,128)S(1)} %get-tuple-element.46.own, f32[2,3,8,256]{3,2,1,0:T(8,128)S(1)} %collective-permute-done.11.xr, ...), custom_call_target="tpu_custom_call" | custom-call | tf_op jit(solution)/shard_map/pallas_call | solution.py:418
  82.4 20.2 %all_to_all.10 = f32[32,2,128]{2,1,0:T(2,128)S(1)} all-to-all(f32[32,2,128]{2,1,0:T(2,128)S(1)} %broadcast_in_dim.7), channel_id=1, replica_groups=mesh['gx'=12,'gc'=8,'co'=2,'gz'=4] {'gc','gz'}, dimensions={0} | all-to-all | bytes 65536 | tf_op jit(solution)/shard_map/all_to_all | solution.py:370
  102.6 16.8 %all_to_all.11 = f32[24,2,128]{2,1,0:T(2,128)S(1)} all-to-all(f32[24,2,128]{2,1,0:T(2,128)S(1)} %broadcast_in_dim.8), channel_id=1, replica_groups=mesh['gx'=12,'gc'=8,'co'=2,'gz'=4] {'gx','co'}, dimensions={0} | all-to-all | bytes 49152 | tf_op jit(solution)/shard_map/all_to_all | solution.py:370
  119.4 0.0 copy-done
  119.4 0.0 copy-done.1
  119.4 1.7 %multiply_subtract_fusion = (f32[3,8,16,128]{3,2,1,0:T(8,128)}, f32[3,8,16,128]{3,2,1,0:T(8,128)}) fusion(f32[3,8,16,128]{3,2,1,0:T(8,128)S(1)} %copy-done, f32[3,8,16,128]{3,2,1,0:T(8,128)S(1)} %get-tuple-element.62, f32[128]{0:T(128)S(1)} %fusion.2, f32[3,8,16,128]{3,2,1,0:T(8,128)S(1)} %copy-done.1, f32[3,8,16,128]{3,2,1,0:T(8,128)} %get-tuple-element.32), kind=kLoop, calls=%fused_computation.1 | loop fusion | flops 196608 | bytes 1180160 | tf_op jit(solution)/shard_map/sub | solution.py:425
  (8 shorter events, 0.2 us)
Async XLA Ops:
  3.4 25.0 %collective-permute-start.1 = (f32[7,8,16,128]{3,2,1,0:T(8,128)S(1)}, f32[7,8,16,128]{3,2,1,0:T(8,128)S(1)}, u32[]{:S(2)}, u32[]{:S(2)}) collective-permute-start(f32[7,8,16,128]{3,2,1,0:T(8,128)S(1)} %pad_maximum_fusion.brick.x0), channel_id=1, source_target_pairs={{0,704},{64,0},{128,64},{192,128},{256,192},{320,256},{384,320},{4... | collective-permute-start | bytes 1376264 | tf_op jit(solution)/shard_map/ppermute | solution.py:383
  18.5 14.2 %collective-permute-start = (f32[7,8,16,128]{3,2,1,0:T(8,128)S(1)}, f32[7,8,16,128]{3,2,1,0:T(8,128)S(1)}, u32[]{:S(2)}, u32[]{:S(2)}) collective-permute-start(f32[7,8,16,128]{3,2,1,0:T(8,128)S(1)} %pad_maximum_fusion.brick.x0), channel_id=1, source_target_pairs={{0,64},{64,128},{128,192},{192,256},{256,320},{320,384},{384,448},... | collective-permute-start | bytes 1376264 | tf_op jit(solution)/shard_map/ppermute | solution.py:383
  20.5 5.1 %collective-permute-start.2 = (f32[7,8,8,128]{3,2,1,0:T(8,128)S(1)}, f32[7,8,8,128]{3,2,1,0:T(8,128)S(1)}, u32[]{:S(2)}, u32[]{:S(2)}) collective-permute-start(f32[7,8,8,128]{3,2,1,0:T(8,128)S(1)} %get-tuple-element.33), channel_id=1, source_target_pairs={{0,4},{4,8},{8,12},{12,16},{16,20},{20,24},{24,28},{28,32},{32,36}... | collective-permute-start | bytes 688136 | tf_op jit(solution)/shard_map/ppermute | solution.py:383
  22.7 5.7 %collective-permute-start.3 = (f32[7,8,8,128]{3,2,1,0:T(8,128)S(1)}, f32[7,8,8,128]{3,2,1,0:T(8,128)S(1)}, u32[]{:S(2)}, u32[]{:S(2)}) collective-permute-start(f32[7,8,8,128]{3,2,1,0:T(8,128)S(1)} %get-tuple-element.34), channel_id=1, source_target_pairs={{0,60},{4,0},{8,4},{12,8},{16,12},{20,16},{24,20},{28,24},{32,28},... | collective-permute-start | bytes 688136 | tf_op jit(solution)/shard_map/ppermute | solution.py:383
  34.4 22.1 %collective-permute-start.4 = (f32[7,16,8,128]{3,2,1,0:T(8,128)}, f32[7,16,8,128]{3,2,1,0:T(8,128)S(1)}, u32[]{:S(2)}, u32[]{:S(2)}) collective-permute-start(f32[7,16,8,128]{3,2,1,0:T(8,128)} %get-tuple-element.39), channel_id=1, source_target_pairs={{0,4},{4,8},{8,12},{12,16},{16,20},{20,24},{24,28},{28,32},{32,36}... | collective-permute-start | bytes 1376264 | tf_op jit(solution)/shard_map/ppermute | solution.py:383
  37.4 19.1 %collective-permute-start.5 = (f32[7,16,8,128]{3,2,1,0:T(8,128)}, f32[7,16,8,128]{3,2,1,0:T(8,128)S(1)}, u32[]{:S(2)}, u32[]{:S(2)}) collective-permute-start(f32[7,16,8,128]{3,2,1,0:T(8,128)} %get-tuple-element.40), channel_id=1, source_target_pairs={{0,60},{4,0},{8,4},{12,8},{16,12},{20,16},{24,20},{28,24},{32,28},... | collective-permute-start | bytes 1376264 | tf_op jit(solution)/shard_map/ppermute | solution.py:383
  37.4 7.6 %collective-permute-start.6 = (f32[7,3,16,128]{3,2,1,0:T(8,128)S(1)}, f32[7,3,16,128]{3,2,1,0:T(8,128)S(1)}, u32[]{:S(2)}, u32[]{:S(2)}) collective-permute-start(f32[7,3,16,128]{3,2,1,0:T(8,128)S(1)} %get-tuple-element.41), channel_id=1, source_target_pairs={{0,1},{1,2},{2,3},{3,0},{4,5},{5,6},{6,7},{7,4},{8,9},{9,10},{10,1... | collective-permute-start | bytes 516104 | tf_op jit(solution)/shard_map/ppermute | solution.py:383
  40.5 6.4 %collective-permute-start.7 = (f32[7,3,16,128]{3,2,1,0:T(8,128)S(1)}, f32[7,3,16,128]{3,2,1,0:T(8,128)S(1)}, u32[]{:S(2)}, u32[]{:S(2)}) collective-permute-start(f32[7,3,16,128]{3,2,1,0:T(8,128)S(1)} %get-tuple-element.42), channel_id=1, source_target_pairs={{0,3},{1,0},{2,1},{3,2},{4,7},{5,4},{6,5},{7,6},{8,11},{9,8},{10,9... | collective-permute-start | bytes 516104 | tf_op jit(solution)/shard_map/ppermute | solution.py:383
  47.7 6.1 %collective-permute-start.8 = (f32[7,6,8,128]{3,2,1,0:T(8,128)}, f32[7,6,8,128]{3,2,1,0:T(8,128)S(1)}, u32[]{:S(2)}, u32[]{:S(2)}) collective-permute-start(f32[7,6,8,128]{3,2,1,0:T(8,128)} %get-tuple-element.43), channel_id=1, source_target_pairs={{0,4},{4,8},{8,12},{12,16},{16,20},{20,24},{24,28},{28,32},{32,36}... | collective-permute-start | bytes 516104 | tf_op jit(solution)/shard_map/ppermute | solution.py:383
  51.1 5.3 %collective-permute-start.9 = (f32[7,6,8,128]{3,2,1,0:T(8,128)}, f32[7,6,8,128]{3,2,1,0:T(8,128)S(1)}, u32[]{:S(2)}, u32[]{:S(2)}) collective-permute-start(f32[7,6,8,128]{3,2,1,0:T(8,128)} %get-tuple-element.44), channel_id=1, source_target_pairs={{0,60},{4,0},{8,4},{12,8},{16,12},{20,16},{24,20},{28,24},{32,28},... | collective-permute-start | bytes 516104 | tf_op jit(solution)/shard_map/ppermute | solution.py:383
  65.6 53.8 %copy-start = (f32[3,8,16,128]{3,2,1,0:T(8,128)S(1)}, f32[3,8,16,128]{3,2,1,0:T(8,128)}, u32[]{:S(2)}) copy-start(f32[3,8,16,128]{3,2,1,0:T(8,128)} %param.5) | copy-start | bytes 589828
  65.6 53.8 %copy-start.1 = (f32[3,8,16,128]{3,2,1,0:T(8,128)S(1)}, f32[3,8,16,128]{3,2,1,0:T(8,128)}, u32[]{:S(2)}) copy-start(f32[3,8,16,128]{3,2,1,0:T(8,128)} %param.4) | copy-start | bytes 589828
  65.6 6.6 %collective-permute-start.10 = (f32[2,3,8,256]{3,2,1,0:T(8,128)S(1)}, f32[2,3,8,256]{3,2,1,0:T(8,128)S(1)}, u32[]{:S(2)}, u32[]{:S(2)}) collective-permute-start(f32[2,3,8,256]{3,2,1,0:T(8,128)S(1)} %get-tuple-element.45), channel_id=1, source_target_pairs={{0,64},{64,128},{128,192},{192,256},{256,320},{320,384},{384,448},... | collective-permute-start | bytes 147464 | tf_op jit(solution)/shard_map/ppermute | solution.py:383
  67.7 5.7 %collective-permute-start.11 = (f32[2,3,8,256]{3,2,1,0:T(8,128)S(1)}, f32[2,3,8,256]{3,2,1,0:T(8,128)S(1)}, u32[]{:S(2)}, u32[]{:S(2)}) collective-permute-start(f32[2,3,8,256]{3,2,1,0:T(8,128)S(1)} %get-tuple-element.47), channel_id=1, source_target_pairs={{0,704},{64,0},{128,64},{192,128},{256,192},{320,256},{384,320},{4... | collective-permute-start | bytes 147464 | tf_op jit(solution)/shard_map/ppermute | solution.py:383
  73.4 2.3 %collective-permute-start.12 = (f32[2,3,8,256]{3,2,1,0:T(8,128)S(1)}, f32[2,3,8,256]{3,2,1,0:T(8,128)S(1)}, u32[]{:S(2)}, u32[]{:S(2)}) collective-permute-start(f32[2,3,8,256]{3,2,1,0:T(8,128)S(1)} %get-tuple-element.48), channel_id=1, source_target_pairs={{0,4},{4,8},{8,12},{12,16},{16,20},{20,24},{24,28},{28,32},{32,36}... | collective-permute-start | bytes 147464 | tf_op jit(solution)/shard_map/ppermute | solution.py:383
  74.3 3.5 %collective-permute-start.13 = (f32[2,3,8,256]{3,2,1,0:T(8,128)S(1)}, f32[2,3,8,256]{3,2,1,0:T(8,128)S(1)}, u32[]{:S(2)}, u32[]{:S(2)}) collective-permute-start(f32[2,3,8,256]{3,2,1,0:T(8,128)S(1)} %get-tuple-element.49), channel_id=1, source_target_pairs={{0,60},{4,0},{8,4},{12,8},{16,12},{20,16},{24,20},{28,24},{32,28},... | collective-permute-start | bytes 147464 | tf_op jit(solution)/shard_map/ppermute | solution.py:383

commit v6 on v5

--- a/solution.py
+++ b/solution.py
@@ -21,6 +21,7 @@
 PLANES = CX + 16
 ZH = 16
 LIMIT = 20 * 1024 * 1024
+GYX = CX + 2
 FIELDS = 7
 
 VMEM = pl.BlockSpec(memory_space=pltpu.VMEM)
@@ -70,41 +71,52 @@
     )
 
 
-def slab_kernel(brick, up, down):
-    up[...] = brick[:, :, 8:16]
-    down[...] = brick[:, :, 0:8]
-
-
-def edge_kernel(xl, x0, xr, to_right, to_left, up, down):
+def pack_kernel(density, residual, fixed, main, to_right, to_left):
     block = lane_of((CY, CZ)) // ZH
 
-    def field(f, _):
-        for b, brick in enumerate((xl, x0, xr)):
-            turned = [pltpu.roll(brick[f, p], ZH * p, 1) if p else brick[f, p] for p in range(CX)]
-            right, left = turned[0], turned[0]
-            for p in range(1, CX):
-                right = jnp.where(block == p - 1, turned[p], right)
-                left = jnp.where(block == p, turned[p], left)
-            to_right[f, b] = right
-            to_left[f, b] = left
-        for i, brick in ((0, xl), (CX, xr)):
-            up[f, i : i + CX] = brick[f, :, 8:16]
-            down[f, i : i + CX] = brick[f, :, 0:8]
-        return 0
-
-    lax.fori_loop(0, FIELDS, field, 0)
-
-
-def half_kernel(zl, zr, up, down):
-    for i, v in enumerate((zl, zr)):
-        up[:, 3 * i : 3 * i + 3] = v[:, :, 8:16]
-        down[:, 3 * i : 3 * i + 3] = v[:, :, 0:8]
+    def stage(f, planes):
+        turned = [pltpu.roll(v, ZH * p, 1) if p else v for p, v in enumerate(planes)]
+        right, left = turned[0], turned[0]
+        for p in range(1, CX):
+            right = jnp.where(block == p - 1, turned[p], right)
+            left = jnp.where(block == p, turned[p], left)
+        to_right[f] = right
+        to_left[f] = left
+        for p, v in enumerate(planes):
+            main[f, p] = v
+
+    def modulus(bins):
+        f = (bins.astype(F32) + 1.0) / BINS
+        return 0.05 + 0.95 * f * f * f
+
+    stage(0, [modulus(density[p]) for p in range(CX)])
+    for c in range(3):
+        stage(1 + c, [residual[c, p] for p in range(CX)])
+        stage(4 + c, [1.0 - fixed[c, p].astype(F32) for p in range(CX)])
+
+
+def join_kernel(main, zl, zr, brick, up, down):
+    brick[:, 0:CX] = main[...]
+    brick[:, CX] = zl[...]
+    brick[:, CX + 1] = zr[...]
+    up[:, 0:CX] = main[:, :, 8:16]
+    up[:, CX] = zl[:, 8:16]
+    up[:, CX + 1] = zr[:, 8:16]
+    down[:, 0:CX] = main[:, :, 0:8]
+    down[:, CX] = zl[:, 0:8]
+    down[:, CX + 1] = zr[:, 0:8]
+
+
+def slab_kernel(xl, xr, up, down):
+    for first, brick in ((0, xl), (GYX, xr)):
+        up[:, first : first + GYX] = brick[:, :, 8:16]
+        down[:, first : first + GYX] = brick[:, :, 0:8]
 
 
 def steps(start, stop, each, body):
     def step(i, _):
         for j in range(each):
-            body(start + each * i + j)
+            body(start + each * i + j, j)
         return 0
 
     lax.fori_loop(0, (stop - start) // each, step, 0)
@@ -126,7 +138,7 @@
 
 
 def fine_kernel(
-    ends, xl, x0, xr, lower0, upper0, lower, upper, zl, zr, zlower, zupper,
+    ends, xl, x0, xr, lower0, upper0, lower, upper,
     ext, ux, uy, uz, inv, mux, muy, muz, mig, mc, o_right, o_left, o_own,
     mm, spring, mrhs, cx_, cy_, cz_, cg, tmp32, tmp16,
 ):
@@ -135,13 +147,14 @@
 
     def assemble(f, _):
         for b, brick in enumerate((xl, x0, xr)):
-            below, above, first = (lower0, upper0, 0) if b == 1 else (lower, upper, 0 if b == 0 else CX)
+            below, above, first = (lower0, upper0, 0) if b == 1 else (lower, upper, 0 if b == 0 else GYX)
             parts = (
-                (0, 8, below, first, zlower[f, b], zlower[f, 3 + b], block8),
-                (8, CY, brick, 0, zl[f, b], zr[f, b], block),
-                (8 + CY, 8, above, first, zupper[f, b], zupper[f, 3 + b], block8),
+                (0, 8, below, first, block8),
+                (8, CY, brick, 0, block),
+                (8 + CY, 8, above, first, block8),
             )
-            for start, rows, src, offset, from_left, from_right, at in parts:
+            for start, rows, src, offset, at in parts:
+                from_left, from_right = src[f, offset + CX], src[f, offset + CX + 1]
                 for p in range(CX):
                     halo = jnp.where(at == p, from_right, from_left)
                     ext[f, CX * b + p, start : start + rows, 0:CZ] = src[f, offset + p]
@@ -157,16 +170,16 @@
     half_y = jnp.where(((row == 7) & (lo_y == 1)) | ((row == 7 + CY) & (hi_y == 1)), 0.0, 0.5)
     half_z = jnp.where(((col == LANES - 1) & (lo_z == 1)) | ((col == CZ - 1) & (hi_z == 1)), 0.0, 0.5)
 
-    def links(p):
+    def links(p, _):
         here = ext[0, p]
         cut = ((p == 7) & (lo_x == 1)) | ((p == 7 + CX) & (hi_x == 1))
         ux[p] = jnp.where(cut, 0.0, 0.5) * (here + ext[0, jnp.minimum(p + 1, PLANES - 1)])
         uy[p] = half_y * (here + after(here, 1, 0))
         uz[p] = half_z * (here + after(here, 1, 1))
 
-    steps(0, PLANES, 4, links)
-
-    def smooth(p):
+    steps(0, PLANES, 8, links)
+
+    def smooth(p, _):
         g = 0.1 * ext[0, p] + ux[p] + ux[p - 1]
         g = g + uy[p] + before(uy[p], 1, 0) + uz[p] + before(uz[p], 1, 1)
         ig = damping / g
@@ -174,22 +187,23 @@
         for c in range(3):
             mm[c, p] = ext[4 + c, p] * ext[1 + c, p] * ig
 
-    steps(1, PLANES - 1, 2, smooth)
-
-    def mid_links(q, tmp32=tmp32):
+    steps(1, PLANES - 1, 11, smooth)
+
+    def mid_links(q, j):
+        tmp = [tmp32.at[4 * j + i] for i in range(4)]
         p = 2 * q
-        a, b = restrict_rows(tmp32, ux[p + 1])
+        a, b = restrict_rows(tmp[0], ux[p + 1])
         mux[q] = pair_sum(a + b, 1)
-        _, b = restrict_rows(tmp32, uy[p] + uy[p + 1])
+        _, b = restrict_rows(tmp[1], uy[p] + uy[p + 1])
         muy[q] = pair_sum(b, 1)
-        a, b = restrict_rows(tmp32, uz[p] + uz[p + 1])
+        a, b = restrict_rows(tmp[2], uz[p] + uz[p + 1])
         muz[q] = odd_group(a + b, 1)
-        a, b = restrict_rows(tmp32, ext[0, p] + ext[0, p + 1])
+        a, b = restrict_rows(tmp[3], ext[0, p] + ext[0, p + 1])
         spring[q] = 0.1 * pair_sum(a + b, 1)
 
-    steps(0, 12, 2, mid_links)
-
-    def mid_rhs(q):
+    steps(0, 12, 6, mid_links)
+
+    def mid_rhs(q, j):
         p = 2 * q
         g = spring[q] + mux[q] + mux[q - 1]
         g = g + muy[q] + before(muy[q], 1, 0) + muz[q] + before(muz[q], 2, 1)
@@ -200,7 +214,7 @@
             for i in range(2):
                 near = neighbours(ux[p + i], ux[p + i - 1], uy[p + i], uz[p + i], mm[c, p + i], mm[c, p + i - 1], mm[c, p + i + 1], 1)
                 total = total + keep * ext[1 + c, p + i] + ext[4 + c, p + i] * near
-            a, b = restrict_rows(tmp32, total)
+            a, b = restrict_rows(tmp32.at[3 * j + c], total)
             rhs = pair_sum(a + b, 1)
             mrhs[c, q] = rhs
             mc[c, q] = ig * rhs
@@ -209,13 +223,13 @@
 
     for s in range(5):
         q = 2 * s
-        a, b = restrict_rows(tmp16, mux[q + 1])
+        a, b = restrict_rows(tmp16.at[4 * s], mux[q + 1])
         cx_[s] = pair_sum(a + b, 2)
-        _, b = restrict_rows(tmp16, muy[q] + muy[q + 1])
+        _, b = restrict_rows(tmp16.at[4 * s + 1], muy[q] + muy[q + 1])
         cy_[s] = pair_sum(b, 2)
-        a, b = restrict_rows(tmp16, muz[q] + muz[q + 1])
+        a, b = restrict_rows(tmp16.at[4 * s + 2], muz[q] + muz[q + 1])
         cz_[s] = odd_group(a + b, 2)
-        a, b = restrict_rows(tmp16, spring[q] + spring[q + 1])
+        a, b = restrict_rows(tmp16.at[4 * s + 3], spring[q] + spring[q + 1])
         cg[s] = pair_sum(a + b, 2)
 
     quad = lane_of((8, LANES)) % 4
@@ -228,7 +242,7 @@
             for q in (2 * s, 2 * s + 1):
                 near = neighbours(mux[q], mux[q - 1], muy[q], muz[q], mc[c, q], mc[c, q - 1], mc[c, q + 1], 2)
                 total = total + keep * mrhs[c, q] + near
-            a, b = restrict_rows(tmp16, total)
+            a, b = restrict_rows(tmp16.at[20 + 3 * (s - 1) + c], total)
             rhs.append(pair_sum(a + b, 2))
         first = jnp.where(quad == 0, rhs[0], jnp.where(quad == 1, rhs[1], jnp.where(quad == 2, rhs[2], g)))
         second = jnp.where(quad == 0, cx_[s], jnp.where(quad == 1, cy_[s], cz_[s]))
@@ -275,12 +289,13 @@
     field = [[None] * 8 for _ in range(7)]
     for i in range(2):
         for s in range(8):
-            packed[...] = jnp.zeros((16, LANES), F32)
-            packed[4:8] = xl[i, s, 2:6] if s < 3 else own[i, s - 3, 2:6] if s < 5 else xr[i, s - 5, 2:6]
+            here = packed.at[8 * i + s]
+            here[...] = jnp.zeros((16, LANES), F32)
+            here[4:8] = xl[i, s, 2:6] if s < 3 else own[i, s - 3, 2:6] if s < 5 else xr[i, s - 5, 2:6]
             for j in range(3):
-                packed[1 + j : 2 + j] = yl[i, j, s : s + 1]
-                packed[8 + j : 9 + j] = yr[i, j, s : s + 1]
-            v = packed[...]
+                here[1 + j : 2 + j] = yl[i, j, s : s + 1]
+                here[8 + j : 9 + j] = yr[i, j, s : s + 1]
+            v = here[...]
             for k, u in enumerate(unpack(v, quad, 4 if i == 0 else 3)):
                 field[4 * i + k][s] = u
     g = [jnp.where(v > 0.0, v, 1.0) for v in field[3]]
@@ -303,17 +318,17 @@
                 new[s] = iterate[s] + update[s]
             iterate = new
         for s in range(4):
-            tmp16[...] = iterate[2 + s]
-            v = tmp16[2:10]
-            v = repeat_rows(cc, v)
+            tmp16[4 * c + s] = iterate[2 + s]
+            v = tmp16[4 * c + s, 2:10]
+            v = repeat_rows(cc.at[4 * c + s], v)
             pm[c, 2 * s] = mc[c, 2 * s] + v
             pm[c, 2 * s + 1] = mc[c, 2 * s + 1] + v
 
-    def mid(q, _):
+    def mid(q, j):
         for c in range(3):
             near = neighbours(mux[q], mux[q - 1], muy[q], muz[q], pm[c, q], pm[c, q - 1], pm[c, q + 1], 2)
             v = keep * pm[c, q] + mc[c, q] + mig[q] * near
-            v = repeat_rows(pf, v)
+            v = repeat_rows(pf.at[3 * j + c], v)
             for i in range(2):
                 p = 2 * (q - 1) + i
                 fr = free[c, p]
@@ -321,23 +336,21 @@
                 corr = fc + v
                 m1[c, p] = fr * corr
                 base[c, p] = keep * corr + fc
-        return 0
-
-    lax.fori_loop(1, 7, mid, 0)
+
+    steps(1, 7, 3, mid)
 
     def fine(p, _):
         for c in range(3):
             near = neighbours(ux[p], ux[p - 1], uy[p], uz[p], m1[c, p], m1[c, p - 1], m1[c, p + 1], 1)
             d[c, p] = base[c, p] + free[c, p] * ig[p] * near
-        return 0
-
-    lax.fori_loop(1, 11, fine, 0)
+
+    steps(1, 11, 5, fine)
 
     mine = slice(8, 8 + CY)
 
-    def last(p, total):
+    def last(i, total):
         first, second = total
-        for c in range(3):
+        for p, c in ((2 + 4 * i + j, c) for j in range(4) for c in range(3)):
             here = free[c, p] * d[c, p]
             prev = free[c, p - 1] * d[c, p - 1]
             nxt = free[c, p + 1] * d[c, p + 1]
@@ -353,7 +366,7 @@
         return first, second
 
     zero = jnp.zeros((CY, CZ), F32)
-    first, second = lax.fori_loop(2, 10, last, (zero, zero))
+    first, second = lax.fori_loop(0, 2, last, (zero, zero))
     sums[0:1] = jnp.full((1, CZ), jnp.sum(first), F32)
     sums[1:2] = jnp.full((1, CZ), jnp.sum(second), F32)
 
@@ -382,18 +395,15 @@
         up, down = v if isinstance(v, tuple) else (v, v)
         return lax.ppermute(up, axes, ring(count, 1)), lax.ppermute(down, axes, ring(count, -1))
 
-    slab, slabs = (FIELDS, CX, 8, CZ), (FIELDS, 2 * CX, 8, CZ)
-    packs, halves = (FIELDS, 3, CY, CZ), (FIELDS, 6, 8, CZ)
-    f = (density_bins.astype(F32) + 1.0) / BINS
-    modulus = 0.05 + 0.95 * f * f * f
-    x0 = jnp.concatenate([modulus[None], residual, 1.0 - fixed_dofs.astype(F32)], axis=0)
+    main, brick = (FIELDS, CX, CY, CZ), (FIELDS, GYX, CY, CZ)
+    pack, slab, slabs = (FIELDS, CY, CZ), (FIELDS, GYX, 8, CZ), (FIELDS, 2 * GYX, 8, CZ)
+    x0, to_right, to_left = call(pack_kernel, [main, pack, pack])(density_bins, residual, fixed_dofs)
+    zl, zr = both((to_right, to_left), "gz", nz)
+    x0, up, down = lax.optimization_barrier(tuple(call(join_kernel, [brick, slab, slab])(x0, zl, zr)))
     xl, xr = both(x0, "gx", nx)
-    lower0, upper0 = both(tuple(call(slab_kernel, [slab, slab])(x0)), y_axes, ny)
+    lower0, upper0 = both((up, down), y_axes, ny)
     xl, xr, lower0, upper0 = lax.optimization_barrier((xl, xr, lower0, upper0))
-    to_right, to_left, up, down = call(edge_kernel, [packs, packs, slabs, slabs])(xl, x0, xr)
-    zl, zr = both((to_right, to_left), "gz", nz)
-    lower, upper = both((up, down), y_axes, ny)
-    zlower, zupper = both(tuple(call(half_kernel, [halves, halves])(zl, zr)), y_axes, ny)
+    lower, upper = both(tuple(call(slab_kernel, [slabs, slabs])(xl, xr)), y_axes, ny)
 
     full = (12, ROWS, LANES)
     half = (8, ROWS // 2, LANES)
@@ -402,15 +412,15 @@
     outs = [(FIELDS,) + all_f, all_f, all_f, all_f, all_f, all_m, all_m, all_m, all_m, (3,) + all_m]
     outs += [(2, 3, 8, LANES), (2, 3, 8, LANES), (2, 2, 8, LANES)]
     scratch = [(3,) + all_f, all_m, (3,) + all_m]
-    scratch += [(5, 8, LANES)] * 4 + [(2, ROWS, CZ), (2, ROWS // 2, CZ)]
+    scratch += [(5, 8, LANES)] * 4 + [(24, 2, ROWS, CZ), (32, 2, ROWS // 2, CZ)]
     fine = pl.pallas_call(
         fine_kernel,
         out_shape=[jax.ShapeDtypeStruct(s, F32) for s in outs],
-        in_specs=[SMEM] + [VMEM] * 11,
+        in_specs=[SMEM] + [VMEM] * 7,
         out_specs=[VMEM] * len(outs),
         scratch_shapes=[pltpu.VMEM(s, F32) for s in scratch],
         compiler_params=pltpu.CompilerParams(vmem_limit_bytes=LIMIT),
-    )(ends, xl, x0, xr, lower0, upper0, lower, upper, zl, zr, zlower, zupper)
+    )(ends, xl, x0, xr, lower0, upper0, lower, upper)
     kept, (to_right, to_left, own) = fine[:-3], fine[-3:]
     cl, cr = both((to_right, to_left), "gx", nx)
     up, down = call(turn_kernel, [(2, 3, 8, LANES)] * 2)(cl, own, cr)
@@ -418,7 +428,7 @@
     direction, image, sums = call(
         solve_kernel,
         [(3, CX, CY, CZ), (3, CX, CY, CZ), (2, CZ)],
-        [(16, LANES), (2, ROWS // 2, CZ), (3,) + half, (2, ROWS, CZ), (3,) + full, (3,) + full, (3,) + full, (16, LANES)],
+        [(16, 16, LANES), (12, 2, ROWS // 2, CZ), (3,) + half, (9, 2, ROWS, CZ), (3,) + full, (3,) + full, (3,) + full, (12, 16, LANES)],
     )(cl, own, cr, dl, dr, *kept)
     sums = all_sum(all_sum(sums, ("gc", "gz")), ("gx", "co"))
     alpha = (sums[0] / sums[1])[None, None, None]

time: 122 us -> 120 us (0.984)
  waiting for transfers between devices: 22.3 us -> 25.6 us
  Pallas kernels: 16 us -> 12.8 us
  other arithmetic: 4.58 us -> 1.81 us
  local copies, waits for them, and re-layouts: 0.14 us -> 2.82 us
    ppermute x7 -> x6, waiting for transfers between devices: 11.7 us -> 14.9 us  [both(): lax.ppermute(up, axes, ring(count, 1))]
    unnamed x4 -> x10, local copies, waits for them, and re-layouts: 0.01 us -> 2.7 us
    pallas_call x4, Pallas kernels: 6.9 us -> 5 us  [the longest x1 3.65 us: shards(): call(solve_kernel, [(3, CX, CY, CZ), (3, CX, CY, CZ), (2, CZ)], [(16, 16,...]
    ppermute x7 -> x6, starting transfers between devices: 23.8 us -> 22.1 us  [both(): lax.ppermute(down, axes, ring(count, -1))]
    pallas_call x1, Pallas kernels: 9.08 us -> 7.77 us  [shards(): pl.pallas_call(fine_kernel, out_shape=[jax.ShapeDtypeStruct(s, F32) for s...]
    ppermute x7 -> x6, starting transfers between devices: 16.6 us -> 17.2 us  [both(): lax.ppermute(up, axes, ring(count, 1))]
    ppermute x7 -> x6, waiting for transfers between devices: 10.6 us -> 10.6 us  [both(): lax.ppermute(down, axes, ring(count, -1))]
  transfers between devices with their start and end apart: 14 -> 12, of which waited for: 10 -> 9; matrix products, arithmetic and copies ran while one was open for 0% -> 0% of each run, Pallas kernels for 1% -> 0%
where the time goes in v6:
time: 120 us; the launch traced here: 119 us
  starting transfers between devices  39.3 us (33%)
  blocking collectives  36 us (30%)
  waiting for transfers between devices  25.6 us (21%)
  Pallas kernels  12.8 us (11%)
  local copies, waits for them, and re-layouts  2.82 us (2%)
  other arithmetic  1.81 us (2%)
    all_to_all x2, blocking collectives, all_sum(): return lax.all_to_all(sent, axes, 0, 0).sum(axis=0)  36 us
    ppermute x6, starting transfers between devices, both(): lax.ppermute(down, axes, ring(count, -1))  22.1 us
    ppermute x6, starting transfers between devices, both(): lax.ppermute(up, axes, ring(count, 1))  17.2 us
    ppermute x6, waiting for transfers between devices, both(): lax.ppermute(up, axes, ring(count, 1))  14.9 us
    ppermute x6, waiting for transfers between devices, both(): lax.ppermute(down, axes, ring(count, -1))  10.6 us
    pallas_call x1, Pallas kernels, shards(): pl.pallas_call(fine_kernel, out_shape=[jax.ShapeDtypeStruct(s, F32) for s...  7.77 us
    pallas_call x1, Pallas kernels, shards(): call(solve_kernel, [(3, CX, CY, CZ), (3, CX, CY, CZ), (2, CZ)], [(16, 16,...  3.65 us
    unnamed x10, local copies, waits for them, and re-layouts  2.7 us
  transfers between devices with their start and end apart: 12, of which 9 were waited for; matrix products, arithmetic and copies ran while one was open for 0% of the time, Pallas kernels for 0%

profile of v6, /device:TPU:1, one launch (start us, length us, event | category | flops | bytes accessed | tf_op | source)
XLA Modules:
  0.0 119.0 jit_solution(5765125109309460645)
XLA Ops:
  0.6 0.0 copy-start
  0.6 0.9 copy-done
  1.6 0.0 copy-start.2
  1.6 0.9 copy-done.2
  2.5 0.0 copy-start.3
  2.5 0.8 copy-done.3
  3.3 0.2 shard_map.67
  3.5 3.9 %collective-permute-start = (f32[7,16,128]{2,1,0:T(8,128)S(1)}, f32[7,16,128]{2,1,0:T(8,128)S(1)}, u32[]{:S(2)}, u32[]{:S(2)}) collective-permute-start(f32[7,16,128]{2,1,0:T(8,128)S(1)} %get-tuple-element.34), channel_id=1, source_target_pairs={{0,1},{1,2},{2,3},{3,0},{4,5},{5,6},{6,7},{7,4},{8,9},{9,10},{10,1... | collective-permute-start | bytes 172040 | tf_op jit(solution)/shard_map/ppermute | solution.py:396
  7.5 3.2 %collective-permute-start.1 = (f32[7,16,128]{2,1,0:T(8,128)S(1)}, f32[7,16,128]{2,1,0:T(8,128)S(1)}, u32[]{:S(2)}, u32[]{:S(2)}) collective-permute-start(f32[7,16,128]{2,1,0:T(8,128)S(1)} %get-tuple-element.35), channel_id=1, source_target_pairs={{0,3},{1,0},{2,1},{3,2},{4,7},{5,4},{6,5},{7,6},{8,11},{9,8},{10,9... | collective-permute-start | bytes 172040 | tf_op jit(solution)/shard_map/ppermute | solution.py:396
  10.7 0.0 collective-permute-done.zl
  10.7 1.7 %collective-permute-done.1.zr = f32[7,16,128]{2,1,0:T(8,128)S(1)} collective-permute-done((f32[7,16,128]{2,1,0:T(8,128)S(1)}, f32[7,16,128]{2,1,0:T(8,128)S(1)}, u32[]{:S(2)}, u32[]{:S(2)}) %collective-permute-start.1) | collective-permute-done | bytes 57376 | tf_op jit(solution)/shard_map/ppermute | solution.py:396
  12.4 0.1 shard_map.68
  12.5 14.3 %collective-permute-start.3 = (f32[7,10,16,128]{3,2,1,0:T(8,128)S(1)}, f32[7,10,16,128]{3,2,1,0:T(8,128)S(1)}, u32[]{:S(2)}, u32[]{:S(2)}) collective-permute-start(f32[7,10,16,128]{3,2,1,0:T(8,128)S(1)} %get-tuple-element.36.x0), channel_id=1, source_target_pairs={{0,704},{64,0},{128,64},{192,128},{256,192},{320,256},{384,320},{4... | collective-permute-start | bytes 1720328 | tf_op jit(solution)/shard_map/ppermute | solution.py:396
  26.8 1.9 %collective-permute-start.2 = (f32[7,10,16,128]{3,2,1,0:T(8,128)S(1)}, f32[7,10,16,128]{3,2,1,0:T(8,128)S(1)}, u32[]{:S(2)}, u32[]{:S(2)}) collective-permute-start(f32[7,10,16,128]{3,2,1,0:T(8,128)S(1)} %get-tuple-element.36.x0), channel_id=1, source_target_pairs={{0,64},{64,128},{128,192},{192,256},{256,320},{320,384},{384,448},... | collective-permute-start | bytes 1720328 | tf_op jit(solution)/shard_map/ppermute | solution.py:396
  28.7 3.6 %collective-permute-start.4 = (f32[7,10,8,128]{3,2,1,0:T(8,128)S(1)}, f32[7,10,8,128]{3,2,1,0:T(8,128)S(1)}, u32[]{:S(2)}, u32[]{:S(2)}) collective-permute-start(f32[7,10,8,128]{3,2,1,0:T(8,128)S(1)} %get-tuple-element.37), channel_id=1, source_target_pairs={{0,4},{4,8},{8,12},{12,16},{16,20},{20,24},{24,28},{28,32},{32,36}... | collective-permute-start | bytes 860168 | tf_op jit(solution)/shard_map/ppermute | solution.py:396
  32.3 0.0 collective-permute-start.5
  32.3 3.6 %collective-permute-done.4.lower0 = f32[7,10,8,128]{3,2,1,0:T(8,128)S(1)} collective-permute-done((f32[7,10,8,128]{3,2,1,0:T(8,128)S(1)}, f32[7,10,8,128]{3,2,1,0:T(8,128)S(1)}, u32[]{:S(2)}, u32[]{:S(2)}) %collective-permute-start.4) | collective-permute-done | bytes 286752 | tf_op jit(solution)/shard_map/ppermute | solution.py:396
  35.9 2.8 %collective-permute-done.5.upper0 = f32[7,10,8,128]{3,2,1,0:T(8,128)S(1)} collective-permute-done((f32[7,10,8,128]{3,2,1,0:T(8,128)S(1)}, f32[7,10,8,128]{3,2,1,0:T(8,128)S(1)}, u32[]{:S(2)}, u32[]{:S(2)}) %collective-permute-start.5) | collective-permute-done | bytes 286752 | tf_op jit(solution)/shard_map/ppermute | solution.py:396
  38.7 0.0 collective-permute-done.3.xr
  38.7 3.3 %collective-permute-done.2.xl = f32[7,10,16,128]{3,2,1,0:T(8,128)S(1)} collective-permute-done((f32[7,10,16,128]{3,2,1,0:T(8,128)S(1)}, f32[7,10,16,128]{3,2,1,0:T(8,128)S(1)}, u32[]{:S(2)}, u32[]{:S(2)}) %collective-permute-start.2) | collective-permute-done | bytes 573472 | tf_op jit(solution)/shard_map/ppermute | solution.py:396
  42.0 1.1 shard_map.69
  43.1 4.5 %collective-permute-start.6 = (f32[7,20,8,128]{3,2,1,0:T(8,128)}, f32[7,20,8,128]{3,2,1,0:T(8,128)S(1)}, u32[]{:S(2)}, u32[]{:S(2)}) collective-permute-start(f32[7,20,8,128]{3,2,1,0:T(8,128)} %get-tuple-element.43), channel_id=1, source_target_pairs={{0,4},{4,8},{8,12},{12,16},{16,20},{20,24},{24,28},{28,32},{32,36}... | collective-permute-start | bytes 1720328 | tf_op jit(solution)/shard_map/ppermute | solution.py:396
  47.6 0.0 collective-permute-start.7
  47.6 0.1 stack.27
  47.7 6.9 %collective-permute-done.6.lower = f32[7,20,8,128]{3,2,1,0:T(8,128)S(1)} collective-permute-done((f32[7,20,8,128]{3,2,1,0:T(8,128)}, f32[7,20,8,128]{3,2,1,0:T(8,128)S(1)}, u32[]{:S(2)}, u32[]{:S(2)}) %collective-permute-start.6) | collective-permute-done | bytes 573472 | tf_op jit(solution)/shard_map/ppermute | solution.py:396
  54.5 2.4 %collective-permute-done.7.upper = f32[7,20,8,128]{3,2,1,0:T(8,128)S(1)} collective-permute-done((f32[7,20,8,128]{3,2,1,0:T(8,128)}, f32[7,20,8,128]{3,2,1,0:T(8,128)S(1)}, u32[]{:S(2)}, u32[]{:S(2)}) %collective-permute-start.7) | collective-permute-done | bytes 573472 | tf_op jit(solution)/shard_map/ppermute | solution.py:396
  56.9 7.8 %shard_map.70 = (f32[7,24,32,256]{3,2,1,0:T(8,128)S(1)}, f32[24,32,256]{2,1,0:T(8,128)S(1)}, f32[24,32,256]{2,1,0:T(8,128)S(1)}, f32[24,32,256]{2,1,0:T(8,128)S(...) custom-call(s32[6]{0:T(128)S(1)} %convert_element_type.3.ends, ...), custom_call_target="tpu_custom_call" | custom-call | tf_op jit(solution)/shard_map/pallas_call | solution.py:416
  64.7 0.0 copy-start.1
  64.7 0.0 copy-start.4
  64.7 2.1 %collective-permute-start.8 = (f32[2,3,8,256]{3,2,1,0:T(8,128)S(1)}, f32[2,3,8,256]{3,2,1,0:T(8,128)S(1)}, u32[]{:S(2)}, u32[]{:S(2)}) collective-permute-start(f32[2,3,8,256]{3,2,1,0:T(8,128)S(1)} %get-tuple-element.45), channel_id=1, source_target_pairs={{0,64},{64,128},{128,192},{192,256},{256,320},{320,384},{384,448},... | collective-permute-start | bytes 147464 | tf_op jit(solution)/shard_map/ppermute | solution.py:396
  66.8 4.6 %collective-permute-start.9 = (f32[2,3,8,256]{3,2,1,0:T(8,128)S(1)}, f32[2,3,8,256]{3,2,1,0:T(8,128)S(1)}, u32[]{:S(2)}, u32[]{:S(2)}) collective-permute-start(f32[2,3,8,256]{3,2,1,0:T(8,128)S(1)} %get-tuple-element.47), channel_id=1, source_target_pairs={{0,704},{64,0},{128,64},{192,128},{256,192},{320,256},{384,320},{4... | collective-permute-start | bytes 147464 | tf_op jit(solution)/shard_map/ppermute | solution.py:396
  71.4 0.0 collective-permute-done.8.xl
  71.4 1.1 collective-permute-done.9.xr
  72.6 1.2 collective-permute-start.10
  73.7 0.0 collective-permute-start.11
  73.8 1.1 collective-permute-done.10.yl
  74.9 2.6 %collective-permute-done.11.yr = f32[2,3,8,256]{3,2,1,0:T(8,128)S(1)} collective-permute-done((f32[2,3,8,256]{3,2,1,0:T(8,128)S(1)}, f32[2,3,8,256]{3,2,1,0:T(8,128)S(1)}, u32[]{:S(2)}, u32[]{:S(2)}) %collective-permute-start.11) | collective-permute-done | bytes 49184 | tf_op jit(solution)/shard_map/ppermute | solution.py:396
  77.5 3.6 %shard_map.72 = (f32[3,8,16,128]{3,2,1,0:T(8,128)}, f32[3,8,16,128]{3,2,1,0:T(8,128)S(1)}, f32[2,128]{1,0:T(2,128)S(1)}) custom-call(f32[2,3,8,256]{3,2,1,0:T(8,128)S(1)} %collective-permute-done.8.xl, f32[2,2,8,256]{3,2,1,0:T(8,128)S(1)} %get-tuple-element.46.own, f32[2,3,8,256]{3,2,1,0:T(8,128)S(1)} %collective-permute-done.9.xr, ...), custom_call_target="tpu_custom_call" | custom-call | tf_op jit(solution)/shard_map/pallas_call | solution.py:428
  81.2 19.2 %all_to_all.10 = f32[32,2,128]{2,1,0:T(2,128)S(1)} all-to-all(f32[32,2,128]{2,1,0:T(2,128)S(1)} %broadcast_in_dim.4), channel_id=1, replica_groups=mesh['gx'=12,'gc'=8,'co'=2,'gz'=4] {'gc','gz'}, dimensions={0} | all-to-all | bytes 65536 | tf_op jit(solution)/shard_map/all_to_all | solution.py:383
  100.5 16.8 %all_to_all.11 = f32[24,2,128]{2,1,0:T(2,128)S(1)} all-to-all(f32[24,2,128]{2,1,0:T(2,128)S(1)} %broadcast_in_dim.5), channel_id=1, replica_groups=mesh['gx'=12,'gc'=8,'co'=2,'gz'=4] {'gx','co'}, dimensions={0} | all-to-all | bytes 49152 | tf_op jit(solution)/shard_map/all_to_all | solution.py:383
  117.3 0.0 copy-done.1
  117.3 0.0 copy-done.4
  117.3 1.7 %multiply_subtract_fusion = (f32[3,8,16,128]{3,2,1,0:T(8,128)}, f32[3,8,16,128]{3,2,1,0:T(8,128)}) fusion(f32[3,8,16,128]{3,2,1,0:T(8,128)S(1)} %copy-done.1, f32[3,8,16,128]{3,2,1,0:T(8,128)S(1)} %get-tuple-element.62, f32[128]{0:T(128)S(1)} %fusion, f32[3,8,16,128]{3,2,1,0:T(8,128)S(1)} %copy-done.4, f32[3,8,16,128]{3,2,1,0:T(8,128)} %get-tuple-element.32), kind=kLoop, calls=%fused_computation | loop fusion | flops 196608 | bytes 1180160 | tf_op jit(solution)/shard_map/sub | solution.py:435
  (7 shorter events, 0.2 us)
Async XLA Ops:
  0.6 0.9 copy-start
  1.6 0.9 copy-start.2
  2.5 0.8 copy-start.3
  3.5 7.2 %collective-permute-start = (f32[7,16,128]{2,1,0:T(8,128)S(1)}, f32[7,16,128]{2,1,0:T(8,128)S(1)}, u32[]{:S(2)}, u32[]{:S(2)}) collective-permute-start(f32[7,16,128]{2,1,0:T(8,128)S(1)} %get-tuple-element.34), channel_id=1, source_target_pairs={{0,1},{1,2},{2,3},{3,0},{4,5},{5,6},{6,7},{7,4},{8,9},{9,10},{10,1... | collective-permute-start | bytes 172040 | tf_op jit(solution)/shard_map/ppermute | solution.py:396
  7.5 4.9 %collective-permute-start.1 = (f32[7,16,128]{2,1,0:T(8,128)S(1)}, f32[7,16,128]{2,1,0:T(8,128)S(1)}, u32[]{:S(2)}, u32[]{:S(2)}) collective-permute-start(f32[7,16,128]{2,1,0:T(8,128)S(1)} %get-tuple-element.35), channel_id=1, source_target_pairs={{0,3},{1,0},{2,1},{3,2},{4,7},{5,4},{6,5},{7,6},{8,11},{9,8},{10,9... | collective-permute-start | bytes 172040 | tf_op jit(solution)/shard_map/ppermute | solution.py:396
  12.5 26.2 %collective-permute-start.3 = (f32[7,10,16,128]{3,2,1,0:T(8,128)S(1)}, f32[7,10,16,128]{3,2,1,0:T(8,128)S(1)}, u32[]{:S(2)}, u32[]{:S(2)}) collective-permute-start(f32[7,10,16,128]{3,2,1,0:T(8,128)S(1)} %get-tuple-element.36.x0), channel_id=1, source_target_pairs={{0,704},{64,0},{128,64},{192,128},{256,192},{320,256},{384,320},{4... | collective-permute-start | bytes 1720328 | tf_op jit(solution)/shard_map/ppermute | solution.py:396
  26.8 15.2 %collective-permute-start.2 = (f32[7,10,16,128]{3,2,1,0:T(8,128)S(1)}, f32[7,10,16,128]{3,2,1,0:T(8,128)S(1)}, u32[]{:S(2)}, u32[]{:S(2)}) collective-permute-start(f32[7,10,16,128]{3,2,1,0:T(8,128)S(1)} %get-tuple-element.36.x0), channel_id=1, source_target_pairs={{0,64},{64,128},{128,192},{192,256},{256,320},{320,384},{384,448},... | collective-permute-start | bytes 1720328 | tf_op jit(solution)/shard_map/ppermute | solution.py:396
  28.7 7.2 %collective-permute-start.4 = (f32[7,10,8,128]{3,2,1,0:T(8,128)S(1)}, f32[7,10,8,128]{3,2,1,0:T(8,128)S(1)}, u32[]{:S(2)}, u32[]{:S(2)}) collective-permute-start(f32[7,10,8,128]{3,2,1,0:T(8,128)S(1)} %get-tuple-element.37), channel_id=1, source_target_pairs={{0,4},{4,8},{8,12},{12,16},{16,20},{20,24},{24,28},{28,32},{32,36}... | collective-permute-start | bytes 860168 | tf_op jit(solution)/shard_map/ppermute | solution.py:396
  32.3 6.4 %collective-permute-start.5 = (f32[7,10,8,128]{3,2,1,0:T(8,128)S(1)}, f32[7,10,8,128]{3,2,1,0:T(8,128)S(1)}, u32[]{:S(2)}, u32[]{:S(2)}) collective-permute-start(f32[7,10,8,128]{3,2,1,0:T(8,128)S(1)} %get-tuple-element.38), channel_id=1, source_target_pairs={{0,60},{4,0},{8,4},{12,8},{16,12},{20,16},{24,20},{28,24},{32,28},... | collective-permute-start | bytes 860168 | tf_op jit(solution)/shard_map/ppermute | solution.py:396
  43.1 11.5 %collective-permute-start.6 = (f32[7,20,8,128]{3,2,1,0:T(8,128)}, f32[7,20,8,128]{3,2,1,0:T(8,128)S(1)}, u32[]{:S(2)}, u32[]{:S(2)}) collective-permute-start(f32[7,20,8,128]{3,2,1,0:T(8,128)} %get-tuple-element.43), channel_id=1, source_target_pairs={{0,4},{4,8},{8,12},{12,16},{16,20},{20,24},{24,28},{28,32},{32,36}... | collective-permute-start | bytes 1720328 | tf_op jit(solution)/shard_map/ppermute | solution.py:396
  47.6 9.3 %collective-permute-start.7 = (f32[7,20,8,128]{3,2,1,0:T(8,128)}, f32[7,20,8,128]{3,2,1,0:T(8,128)S(1)}, u32[]{:S(2)}, u32[]{:S(2)}) collective-permute-start(f32[7,20,8,128]{3,2,1,0:T(8,128)} %get-tuple-element.44), channel_id=1, source_target_pairs={{0,60},{4,0},{8,4},{12,8},{16,12},{20,16},{24,20},{28,24},{32,28},... | collective-permute-start | bytes 1720328 | tf_op jit(solution)/shard_map/ppermute | solution.py:396
  64.7 52.6 %copy-start.1 = (f32[3,8,16,128]{3,2,1,0:T(8,128)S(1)}, f32[3,8,16,128]{3,2,1,0:T(8,128)}, u32[]{:S(2)}) copy-start(f32[3,8,16,128]{3,2,1,0:T(8,128)} %residual.1) | copy-start | bytes 589828
  64.7 52.6 %copy-start.4 = (f32[3,8,16,128]{3,2,1,0:T(8,128)S(1)}, f32[3,8,16,128]{3,2,1,0:T(8,128)}, u32[]{:S(2)}) copy-start(f32[3,8,16,128]{3,2,1,0:T(8,128)} %param.4) | copy-start | bytes 589828
  64.7 6.6 %collective-permute-start.8 = (f32[2,3,8,256]{3,2,1,0:T(8,128)S(1)}, f32[2,3,8,256]{3,2,1,0:T(8,128)S(1)}, u32[]{:S(2)}, u32[]{:S(2)}) collective-permute-start(f32[2,3,8,256]{3,2,1,0:T(8,128)S(1)} %get-tuple-element.45), channel_id=1, source_target_pairs={{0,64},{64,128},{128,192},{192,256},{256,320},{320,384},{384,448},... | collective-permute-start | bytes 147464 | tf_op jit(solution)/shard_map/ppermute | solution.py:396
  66.8 5.7 %collective-permute-start.9 = (f32[2,3,8,256]{3,2,1,0:T(8,128)S(1)}, f32[2,3,8,256]{3,2,1,0:T(8,128)S(1)}, u32[]{:S(2)}, u32[]{:S(2)}) collective-permute-start(f32[2,3,8,256]{3,2,1,0:T(8,128)S(1)} %get-tuple-element.47), channel_id=1, source_target_pairs={{0,704},{64,0},{128,64},{192,128},{256,192},{320,256},{384,320},{4... | collective-permute-start | bytes 147464 | tf_op jit(solution)/shard_map/ppermute | solution.py:396
  72.6 2.4 %collective-permute-start.10 = (f32[2,3,8,256]{3,2,1,0:T(8,128)S(1)}, f32[2,3,8,256]{3,2,1,0:T(8,128)S(1)}, u32[]{:S(2)}, u32[]{:S(2)}) collective-permute-start(f32[2,3,8,256]{3,2,1,0:T(8,128)S(1)} %get-tuple-element.48), channel_id=1, source_target_pairs={{0,4},{4,8},{8,12},{12,16},{16,20},{20,24},{24,28},{28,32},{32,36}... | collective-permute-start | bytes 147464 | tf_op jit(solution)/shard_map/ppermute | solution.py:396
  73.7 3.8 %collective-permute-start.11 = (f32[2,3,8,256]{3,2,1,0:T(8,128)S(1)}, f32[2,3,8,256]{3,2,1,0:T(8,128)S(1)}, u32[]{:S(2)}, u32[]{:S(2)}) collective-permute-start(f32[2,3,8,256]{3,2,1,0:T(8,128)S(1)} %get-tuple-element.49), channel_id=1, source_target_pairs={{0,60},{4,0},{8,4},{12,8},{16,12},{20,16},{24,20},{28,24},{32,28},... | collective-permute-start | bytes 147464 | tf_op jit(solution)/shard_map/ppermute | solution.py:396

commit v7 on v6

--- a/solution.py
+++ b/solution.py
@@ -20,21 +20,23 @@
 ROWS = CY + 16
 PLANES = CX + 16
 ZH = 16
-LIMIT = 20 * 1024 * 1024
+MIB = 1024 * 1024
 GYX = CX + 2
+SLAB = 8
 FIELDS = 7
 
 VMEM = pl.BlockSpec(memory_space=pltpu.VMEM)
 SMEM = pl.BlockSpec(memory_space=pltpu.SMEM)
 
 
-def call(kernel, outs, scratch=()):
+def call(kernel, outs, scratch=(), limit=4, flops=0):
     return pl.pallas_call(
         kernel,
         out_shape=[jax.ShapeDtypeStruct(s, F32) for s in outs],
         out_specs=[VMEM] * len(outs),
         scratch_shapes=[pltpu.VMEM(s, F32) for s in scratch],
-        compiler_params=pltpu.CompilerParams(vmem_limit_bytes=LIMIT),
+        compiler_params=pltpu.CompilerParams(vmem_limit_bytes=limit * MIB),
+        cost_estimate=pl.CostEstimate(flops=flops, bytes_accessed=0, transcendentals=0) if flops else None,
     )
 
 
@@ -71,7 +73,16 @@
     )
 
 
-def pack_kernel(density, residual, fixed, main, to_right, to_left):
+def modulus_of(bins):
+    f = (bins.astype(F32) + 1.0) / BINS
+    return 0.05 + 0.95 * f * f * f
+
+
+def pack_kernel(density_in, residual_in, fixed_in, to_right, to_left, density, residual, fixed, sems):
+    pairs = ((density_in, density), (residual_in, residual), (fixed_in, fixed))
+    copies = [pltpu.make_async_copy(a, b, sems.at[i]) for i, (a, b) in enumerate(pairs)]
+    for copy in copies:
+        copy.start()
     block = lane_of((CY, CZ)) // ZH
 
     def stage(f, planes):
@@ -82,35 +93,37 @@
             left = jnp.where(block == p, turned[p], left)
         to_right[f] = right
         to_left[f] = left
-        for p, v in enumerate(planes):
-            main[f, p] = v
-
-    def modulus(bins):
-        f = (bins.astype(F32) + 1.0) / BINS
-        return 0.05 + 0.95 * f * f * f
-
-    stage(0, [modulus(density[p]) for p in range(CX)])
+
+    for copy in copies:
+        copy.wait()
+    stage(0, [modulus_of(density[p]) for p in range(CX)])
     for c in range(3):
         stage(1 + c, [residual[c, p] for p in range(CX)])
         stage(4 + c, [1.0 - fixed[c, p].astype(F32) for p in range(CX)])
+
+
+def main_kernel(density, residual, fixed, main):
+    main[0] = modulus_of(density[...])
+    main[1:4] = residual[...]
+    main[4:7] = 1.0 - fixed[...].astype(F32)
 
 
 def join_kernel(main, zl, zr, brick, up, down):
     brick[:, 0:CX] = main[...]
     brick[:, CX] = zl[...]
     brick[:, CX + 1] = zr[...]
-    up[:, 0:CX] = main[:, :, 8:16]
-    up[:, CX] = zl[:, 8:16]
-    up[:, CX + 1] = zr[:, 8:16]
-    down[:, 0:CX] = main[:, :, 0:8]
-    down[:, CX] = zl[:, 0:8]
-    down[:, CX + 1] = zr[:, 0:8]
+    up[...] = brick[:, :, 8:16]
+    down[...] = brick[:, :, 0:8]
 
 
 def slab_kernel(xl, xr, up, down):
-    for first, brick in ((0, xl), (GYX, xr)):
-        up[:, first : first + GYX] = brick[:, :, 8:16]
-        down[:, first : first + GYX] = brick[:, :, 0:8]
+    for first, brick, near, far in ((0, xl, 4, 0), (SLAB, xr, 0, 4)):
+        for out, row, row4 in ((up, 8, 12), (down, 0, 0)):
+            out[:, first : first + 4] = brick[:, near : near + 4, row : row + 8]
+            out[:, first + 4 : first + 6] = brick[:, CX : CX + 2, row : row + 8]
+            for p in range(4):
+                at = slice(4 * (p % 2), 4 * (p % 2) + 4)
+                out[:, first + 6 + p // 2, at] = brick[:, far + p, row4 : row4 + 4]
 
 
 def steps(start, stop, each, body):
@@ -145,20 +158,29 @@
     block = lane_of((CY, CZ)) // ZH
     block8 = lane_of((8, CZ)) // ZH
 
+    def put(f, p, start, main, from_left, from_right, at):
+        halo = jnp.where(at == p % CX, from_right, from_left)
+        rows = slice(start, start + main.shape[0])
+        ext[f, p, rows, 0:CZ] = main
+        ext[f, p, rows, CZ:LANES] = pltpu.roll(halo, CZ - ZH * (p % CX), 1) if p % CX else halo
+
     def assemble(f, _):
-        for b, brick in enumerate((xl, x0, xr)):
-            below, above, first = (lower0, upper0, 0) if b == 1 else (lower, upper, 0 if b == 0 else GYX)
-            parts = (
-                (0, 8, below, first, block8),
-                (8, CY, brick, 0, block),
-                (8 + CY, 8, above, first, block8),
-            )
-            for start, rows, src, offset, at in parts:
-                from_left, from_right = src[f, offset + CX], src[f, offset + CX + 1]
-                for p in range(CX):
-                    halo = jnp.where(at == p, from_right, from_left)
-                    ext[f, CX * b + p, start : start + rows, 0:CZ] = src[f, offset + p]
-                    ext[f, CX * b + p, start : start + rows, CZ:LANES] = pltpu.roll(halo, CZ - ZH * p, 1) if p else halo
+        for p in range(PLANES):
+            b, q = p // CX, p % CX
+            brick = (xl, x0, xr)[b]
+            put(f, p, 8, brick[f, q], brick[f, CX], brick[f, CX + 1], block)
+            for start, own, side, turn in ((0, lower0, lower, 0), (8 + CY, upper0, upper, 1)):
+                if b == 1:
+                    v, zs = own[f, q], (own[f, CX], own[f, CX + 1])
+                else:
+                    first = 0 if b == 0 else SLAB
+                    zs = side[f, first + 4], side[f, first + 5]
+                    if (q >= 4) == (b == 0):
+                        v = side[f, first + q % 4]
+                    else:
+                        v = side[f, first + 6 + (q % 4) // 2]
+                        v = before(v, 4, 0) if q % 2 == turn else v
+                put(f, p, start, v, *zs, block8)
         return 0
 
     lax.fori_loop(0, FIELDS, assemble, 0)
@@ -395,11 +417,25 @@
         up, down = v if isinstance(v, tuple) else (v, v)
         return lax.ppermute(up, axes, ring(count, 1)), lax.ppermute(down, axes, ring(count, -1))
 
-    main, brick = (FIELDS, CX, CY, CZ), (FIELDS, GYX, CY, CZ)
-    pack, slab, slabs = (FIELDS, CY, CZ), (FIELDS, GYX, 8, CZ), (FIELDS, 2 * GYX, 8, CZ)
-    x0, to_right, to_left = call(pack_kernel, [main, pack, pack])(density_bins, residual, fixed_dofs)
+    brick, pack = (FIELDS, GYX, CY, CZ), (FIELDS, CY, CZ)
+    slab, slabs = (FIELDS, GYX, 8, CZ), (FIELDS, 2 * SLAB, 8, CZ)
+    to_right, to_left = pl.pallas_call(
+        pack_kernel,
+        out_shape=[jax.ShapeDtypeStruct(pack, F32)] * 2,
+        in_specs=[pl.BlockSpec(memory_space=pltpu.HBM)] * 3,
+        out_specs=[VMEM] * 2,
+        scratch_shapes=[
+            pltpu.VMEM((CX, CY, CZ), jnp.int32),
+            pltpu.VMEM((3, CX, CY, CZ), F32),
+            pltpu.VMEM((3, CX, CY, CZ), jnp.int32),
+            pltpu.SemaphoreType.DMA((3,)),
+        ],
+        compiler_params=pltpu.CompilerParams(vmem_limit_bytes=56 * MIB),
+    )(density_bins, residual, fixed_dofs)
     zl, zr = both((to_right, to_left), "gz", nz)
-    x0, up, down = lax.optimization_barrier(tuple(call(join_kernel, [brick, slab, slab])(x0, zl, zr)))
+    (main,) = call(main_kernel, [(FIELDS, CX, CY, CZ)], flops=10**9)(density_bins, residual, fixed_dofs)
+    join = call(join_kernel, [brick, slab, slab])(main, zl, zr)
+    x0, up, down, ends = lax.optimization_barrier((*join, ends))
     xl, xr = both(x0, "gx", nx)
     lower0, upper0 = both((up, down), y_axes, ny)
     xl, xr, lower0, upper0 = lax.optimization_barrier((xl, xr, lower0, upper0))
@@ -419,7 +455,7 @@
         in_specs=[SMEM] + [VMEM] * 7,
         out_specs=[VMEM] * len(outs),
         scratch_shapes=[pltpu.VMEM(s, F32) for s in scratch],
-        compiler_params=pltpu.CompilerParams(vmem_limit_bytes=LIMIT),
+        compiler_params=pltpu.CompilerParams(vmem_limit_bytes=8 * MIB),
     )(ends, xl, x0, xr, lower0, upper0, lower, upper)
     kept, (to_right, to_left, own) = fine[:-3], fine[-3:]
     cl, cr = both((to_right, to_left), "gx", nx)
@@ -429,6 +465,7 @@
         solve_kernel,
         [(3, CX, CY, CZ), (3, CX, CY, CZ), (2, CZ)],
         [(16, 16, LANES), (12, 2, ROWS // 2, CZ), (3,) + half, (9, 2, ROWS, CZ), (3,) + full, (3,) + full, (3,) + full, (12, 16, LANES)],
+        10,
     )(cl, own, cr, dl, dr, *kept)
     sums = all_sum(all_sum(sums, ("gc", "gz")), ("gx", "co"))
     alpha = (sums[0] / sums[1])[None, None, None]

time: 120 us -> 116 us (0.967)
  starting transfers between devices: 39.3 us -> 37.7 us
  waiting for transfers between devices: 25.6 us -> 24.2 us
    pallas_call x2 -> x3, Pallas kernels: 0.25 us -> 2.02 us  [the longest x1 1.91 us: shards(): pl.pallas_call(pack_kernel, out_shape=[jax.ShapeDtypeStruct(pack, F32)] *...]
    ppermute x6, starting transfers between devices: 17.2 us -> 15.4 us  [both(): lax.ppermute(up, axes, ring(count, 1))]
    ppermute x6, waiting for transfers between devices: 10.6 us -> 9.05 us  [both(): lax.ppermute(down, axes, ring(count, -1))]
  transfers between devices with their start and end apart: 12 -> 12, of which waited for: 9 -> 8; matrix products, arithmetic and copies ran while one was open for 0% -> 0% of each run, Pallas kernels for 0% -> 0%
where the time goes in v7:
time: 116 us
  starting transfers between devices  37.7 us (33%)
  blocking collectives  34.9 us (30%)
  waiting for transfers between devices  24.2 us (21%)
  Pallas kernels  13.5 us (12%)
  local copies, waits for them, and re-layouts  2.83 us (2%)
  other arithmetic  1.81 us (2%)
    all_to_all x2, blocking collectives, all_sum(): return lax.all_to_all(sent, axes, 0, 0).sum(axis=0)  34.9 us
    ppermute x6, starting transfers between devices, both(): lax.ppermute(down, axes, ring(count, -1))  22.3 us
    ppermute x6, starting transfers between devices, both(): lax.ppermute(up, axes, ring(count, 1))  15.4 us
    ppermute x6, waiting for transfers between devices, both(): lax.ppermute(up, axes, ring(count, 1))  15.2 us
    ppermute x6, waiting for transfers between devices, both(): lax.ppermute(down, axes, ring(count, -1))  9.05 us
    pallas_call x1, Pallas kernels, shards(): pl.pallas_call(fine_kernel, out_shape=[jax.ShapeDtypeStruct(s, F32) for s...  7.66 us
    pallas_call x1, Pallas kernels, shards(): call(solve_kernel, [(3, CX, CY, CZ), (3, CX, CY, CZ), (2, CZ)], [(16, 16,...  3.67 us
    unnamed x10, local copies, waits for them, and re-layouts  2.71 us
  transfers between devices with their start and end apart: 12, of which 8 were waited for; matrix products, arithmetic and copies ran while one was open for 0% of the time, Pallas kernels for 0%

profile of v7, /device:TPU:1, one launch (start us, length us, event | category | flops | bytes accessed | tf_op | source)
XLA Modules:
  0.0 115.8 jit_solution(10230195808463330627)
XLA Ops:
  0.6 1.9 %shard_map.68 = (f32[7,16,128]{2,1,0:T(8,128)}, f32[7,16,128]{2,1,0:T(8,128)}) custom-call(s32[8,16,128]{2,1,0:T(8,128)} %density_in.1, f32[3,8,16,128]{3,2,1,0:T(8,128)} %residual_in.1, s32[3,8,16,128]{3,2,1,0:T(8,128)} %fixed_in.1), custom_call_target="tpu_custom_call" | custom-call | tf_op jit(solution)/shard_map/pallas_call | solution.py:422
  2.5 3.9 %collective-permute-start = (f32[7,16,128]{2,1,0:T(8,128)}, f32[7,16,128]{2,1,0:T(8,128)S(1)}, u32[]{:S(2)}, u32[]{:S(2)}) collective-permute-start(f32[7,16,128]{2,1,0:T(8,128)} %get-tuple-element.36), channel_id=1, source_target_pairs={{0,1},{1,2},{2,3},{3,0},{4,5},{5,6},{6,7},{7,4},{8,9},{9,10},{10,1... | collective-permute-start | bytes 172040 | tf_op jit(solution)/shard_map/ppermute | solution.py:418
  6.5 3.2 %collective-permute-start.1 = (f32[7,16,128]{2,1,0:T(8,128)}, f32[7,16,128]{2,1,0:T(8,128)S(1)}, u32[]{:S(2)}, u32[]{:S(2)}) collective-permute-start(f32[7,16,128]{2,1,0:T(8,128)} %get-tuple-element.37), channel_id=1, source_target_pairs={{0,3},{1,0},{2,1},{3,2},{4,7},{5,4},{6,5},{7,6},{8,11},{9,8},{10,9... | collective-permute-start | bytes 172040 | tf_op jit(solution)/shard_map/ppermute | solution.py:418
  9.7 0.1 stack.27
  9.8 0.0 copy-start
  9.8 0.9 copy-done
  10.8 0.0 copy-start.2
  10.8 0.9 copy-done.2
  11.7 0.0 copy-start.3
  11.7 0.8 copy-done.3
  12.6 0.0 collective-permute-done.zl
  12.6 0.0 collective-permute-done.1.zr
  12.6 0.1 shard_map.69
  12.7 14.5 %collective-permute-start.3 = (f32[7,10,16,128]{3,2,1,0:T(8,128)S(1)}, f32[7,10,16,128]{3,2,1,0:T(8,128)S(1)}, u32[]{:S(2)}, u32[]{:S(2)}) collective-permute-start(f32[7,10,16,128]{3,2,1,0:T(8,128)S(1)} %get-tuple-element.42.x0), channel_id=1, source_target_pairs={{0,704},{64,0},{128,64},{192,128},{256,192},{320,256},{384,320},{4... | collective-permute-start | bytes 1720328 | tf_op jit(solution)/shard_map/ppermute | solution.py:418
  27.2 1.9 %collective-permute-start.2 = (f32[7,10,16,128]{3,2,1,0:T(8,128)S(1)}, f32[7,10,16,128]{3,2,1,0:T(8,128)S(1)}, u32[]{:S(2)}, u32[]{:S(2)}) collective-permute-start(f32[7,10,16,128]{3,2,1,0:T(8,128)S(1)} %get-tuple-element.42.x0), channel_id=1, source_target_pairs={{0,64},{64,128},{128,192},{192,256},{256,320},{320,384},{384,448},... | collective-permute-start | bytes 1720328 | tf_op jit(solution)/shard_map/ppermute | solution.py:418
  29.1 2.7 %collective-permute-start.4 = (f32[7,10,8,128]{3,2,1,0:T(8,128)S(1)}, f32[7,10,8,128]{3,2,1,0:T(8,128)S(1)}, u32[]{:S(2)}, u32[]{:S(2)}) collective-permute-start(f32[7,10,8,128]{3,2,1,0:T(8,128)S(1)} %get-tuple-element.43), channel_id=1, source_target_pairs={{0,4},{4,8},{8,12},{12,16},{16,20},{20,24},{24,28},{28,32},{32,36}... | collective-permute-start | bytes 860168 | tf_op jit(solution)/shard_map/ppermute | solution.py:418
  31.8 0.0 collective-permute-start.5
  31.8 3.6 %collective-permute-done.4.lower0 = f32[7,10,8,128]{3,2,1,0:T(8,128)S(1)} collective-permute-done((f32[7,10,8,128]{3,2,1,0:T(8,128)S(1)}, f32[7,10,8,128]{3,2,1,0:T(8,128)S(1)}, u32[]{:S(2)}, u32[]{:S(2)}) %collective-permute-start.4) | collective-permute-done | bytes 286752 | tf_op jit(solution)/shard_map/ppermute | solution.py:418
  35.4 2.8 %collective-permute-done.5.upper0 = f32[7,10,8,128]{3,2,1,0:T(8,128)S(1)} collective-permute-done((f32[7,10,8,128]{3,2,1,0:T(8,128)S(1)}, f32[7,10,8,128]{3,2,1,0:T(8,128)S(1)}, u32[]{:S(2)}, u32[]{:S(2)}) %collective-permute-start.5) | collective-permute-done | bytes 286752 | tf_op jit(solution)/shard_map/ppermute | solution.py:418
  38.2 0.0 collective-permute-done.3.xr
  38.2 5.0 %collective-permute-done.2.xl = f32[7,10,16,128]{3,2,1,0:T(8,128)S(1)} collective-permute-done((f32[7,10,16,128]{3,2,1,0:T(8,128)S(1)}, f32[7,10,16,128]{3,2,1,0:T(8,128)S(1)}, u32[]{:S(2)}, u32[]{:S(2)}) %collective-permute-start.2) | collective-permute-done | bytes 573472 | tf_op jit(solution)/shard_map/ppermute | solution.py:418
  43.2 0.1 shard_map.70
  43.3 3.6 %collective-permute-start.6 = (f32[7,16,8,128]{3,2,1,0:T(8,128)S(1)}, f32[7,16,8,128]{3,2,1,0:T(8,128)S(1)}, u32[]{:S(2)}, u32[]{:S(2)}) collective-permute-start(f32[7,16,8,128]{3,2,1,0:T(8,128)S(1)} %get-tuple-element.49), channel_id=1, source_target_pairs={{0,4},{4,8},{8,12},{12,16},{16,20},{20,24},{24,28},{28,32},{32,36}... | collective-permute-start | bytes 1376264 | tf_op jit(solution)/shard_map/ppermute | solution.py:418
  46.9 0.0 collective-permute-start.7
  47.0 5.4 %collective-permute-done.6.lower = f32[7,16,8,128]{3,2,1,0:T(8,128)S(1)} collective-permute-done((f32[7,16,8,128]{3,2,1,0:T(8,128)S(1)}, f32[7,16,8,128]{3,2,1,0:T(8,128)S(1)}, u32[]{:S(2)}, u32[]{:S(2)}) %collective-permute-start.6) | collective-permute-done | bytes 458784 | tf_op jit(solution)/shard_map/ppermute | solution.py:418
  52.4 2.5 %collective-permute-done.7.upper = f32[7,16,8,128]{3,2,1,0:T(8,128)S(1)} collective-permute-done((f32[7,16,8,128]{3,2,1,0:T(8,128)S(1)}, f32[7,16,8,128]{3,2,1,0:T(8,128)S(1)}, u32[]{:S(2)}, u32[]{:S(2)}) %collective-permute-start.7) | collective-permute-done | bytes 458784 | tf_op jit(solution)/shard_map/ppermute | solution.py:418
  54.9 7.7 %shard_map.71 = (f32[7,24,32,256]{3,2,1,0:T(8,128)S(1)}, f32[24,32,256]{2,1,0:T(8,128)S(1)}, f32[24,32,256]{2,1,0:T(8,128)S(1)}, f32[24,32,256]{2,1,0:T(8,128)S(...) custom-call(s32[6]{0:T(128)S(1)} %convert_element_type.3.ends, ...), custom_call_target="tpu_custom_call" | custom-call | tf_op jit(solution)/shard_map/pallas_call | solution.py:452
  62.5 0.0 copy-start.1
  62.5 0.0 copy-start.4
  62.5 2.1 %collective-permute-start.8 = (f32[2,3,8,256]{3,2,1,0:T(8,128)S(1)}, f32[2,3,8,256]{3,2,1,0:T(8,128)S(1)}, u32[]{:S(2)}, u32[]{:S(2)}) collective-permute-start(f32[2,3,8,256]{3,2,1,0:T(8,128)S(1)} %get-tuple-element.51), channel_id=1, source_target_pairs={{0,64},{64,128},{128,192},{192,256},{256,320},{320,384},{384,448},... | collective-permute-start | bytes 147464 | tf_op jit(solution)/shard_map/ppermute | solution.py:418
  64.6 4.6 %collective-permute-start.9 = (f32[2,3,8,256]{3,2,1,0:T(8,128)S(1)}, f32[2,3,8,256]{3,2,1,0:T(8,128)S(1)}, u32[]{:S(2)}, u32[]{:S(2)}) collective-permute-start(f32[2,3,8,256]{3,2,1,0:T(8,128)S(1)} %get-tuple-element.53), channel_id=1, source_target_pairs={{0,704},{64,0},{128,64},{192,128},{256,192},{320,256},{384,320},{4... | collective-permute-start | bytes 147464 | tf_op jit(solution)/shard_map/ppermute | solution.py:418
  69.2 0.0 collective-permute-done.8.xl
  69.2 1.1 collective-permute-done.9.xr
  70.4 1.2 %collective-permute-start.10 = (f32[2,3,8,256]{3,2,1,0:T(8,128)S(1)}, f32[2,3,8,256]{3,2,1,0:T(8,128)S(1)}, u32[]{:S(2)}, u32[]{:S(2)}) collective-permute-start(f32[2,3,8,256]{3,2,1,0:T(8,128)S(1)} %get-tuple-element.54), channel_id=1, source_target_pairs={{0,4},{4,8},{8,12},{12,16},{16,20},{20,24},{24,28},{28,32},{32,36}... | collective-permute-start | bytes 147464 | tf_op jit(solution)/shard_map/ppermute | solution.py:418
  71.6 0.0 collective-permute-start.11
  71.6 1.1 collective-permute-done.10.yl
  72.7 2.6 %collective-permute-done.11.yr = f32[2,3,8,256]{3,2,1,0:T(8,128)S(1)} collective-permute-done((f32[2,3,8,256]{3,2,1,0:T(8,128)S(1)}, f32[2,3,8,256]{3,2,1,0:T(8,128)S(1)}, u32[]{:S(2)}, u32[]{:S(2)}) %collective-permute-start.11) | collective-permute-done | bytes 49184 | tf_op jit(solution)/shard_map/ppermute | solution.py:418
  75.4 3.7 %shard_map.73 = (f32[3,8,16,128]{3,2,1,0:T(8,128)}, f32[3,8,16,128]{3,2,1,0:T(8,128)S(1)}, f32[2,128]{1,0:T(2,128)S(1)}) custom-call(f32[2,3,8,256]{3,2,1,0:T(8,128)S(1)} %collective-permute-done.8.xl, f32[2,2,8,256]{3,2,1,0:T(8,128)S(1)} %get-tuple-element.52.own, f32[2,3,8,256]{3,2,1,0:T(8,128)S(1)} %collective-permute-done.9.xr, ...), custom_call_target="tpu_custom_call" | custom-call | tf_op jit(solution)/shard_map/pallas_call | solution.py:464
  79.1 18.1 %all_to_all.10 = f32[32,2,128]{2,1,0:T(2,128)S(1)} all-to-all(f32[32,2,128]{2,1,0:T(2,128)S(1)} %broadcast_in_dim.4), channel_id=1, replica_groups=mesh['gx'=12,'gc'=8,'co'=2,'gz'=4] {'gc','gz'}, dimensions={0} | all-to-all | bytes 65536 | tf_op jit(solution)/shard_map/all_to_all | solution.py:405
  97.2 16.8 %all_to_all.11 = f32[24,2,128]{2,1,0:T(2,128)S(1)} all-to-all(f32[24,2,128]{2,1,0:T(2,128)S(1)} %broadcast_in_dim.5), channel_id=1, replica_groups=mesh['gx'=12,'gc'=8,'co'=2,'gz'=4] {'gx','co'}, dimensions={0} | all-to-all | bytes 49152 | tf_op jit(solution)/shard_map/all_to_all | solution.py:405
  114.0 0.0 copy-done.1
  114.0 0.0 copy-done.4
  114.0 1.7 %multiply_subtract_fusion = (f32[3,8,16,128]{3,2,1,0:T(8,128)}, f32[3,8,16,128]{3,2,1,0:T(8,128)}) fusion(f32[3,8,16,128]{3,2,1,0:T(8,128)S(1)} %copy-done.1, f32[3,8,16,128]{3,2,1,0:T(8,128)S(1)} %get-tuple-element.68, f32[128]{0:T(128)S(1)} %fusion, f32[3,8,16,128]{3,2,1,0:T(8,128)S(1)} %copy-done.4, f32[3,8,16,128]{3,2,1,0:T(8,128)} %get-tuple-element.35), kind=kLoop, calls=%fused_computation | loop fusion | flops 196608 | bytes 1180160 | tf_op jit(solution)/shard_map/sub | solution.py:472
  (8 shorter events, 0.2 us)
Async XLA Ops:
  2.5 10.0 %collective-permute-start = (f32[7,16,128]{2,1,0:T(8,128)}, f32[7,16,128]{2,1,0:T(8,128)S(1)}, u32[]{:S(2)}, u32[]{:S(2)}) collective-permute-start(f32[7,16,128]{2,1,0:T(8,128)} %get-tuple-element.36), channel_id=1, source_target_pairs={{0,1},{1,2},{2,3},{3,0},{4,5},{5,6},{6,7},{7,4},{8,9},{9,10},{10,1... | collective-permute-start | bytes 172040 | tf_op jit(solution)/shard_map/ppermute | solution.py:418
  6.5 6.1 %collective-permute-start.1 = (f32[7,16,128]{2,1,0:T(8,128)}, f32[7,16,128]{2,1,0:T(8,128)S(1)}, u32[]{:S(2)}, u32[]{:S(2)}) collective-permute-start(f32[7,16,128]{2,1,0:T(8,128)} %get-tuple-element.37), channel_id=1, source_target_pairs={{0,3},{1,0},{2,1},{3,2},{4,7},{5,4},{6,5},{7,6},{8,11},{9,8},{10,9... | collective-permute-start | bytes 172040 | tf_op jit(solution)/shard_map/ppermute | solution.py:418
  9.8 0.9 copy-start
  10.8 0.9 copy-start.2
  11.7 0.8 copy-start.3
  12.7 25.5 %collective-permute-start.3 = (f32[7,10,16,128]{3,2,1,0:T(8,128)S(1)}, f32[7,10,16,128]{3,2,1,0:T(8,128)S(1)}, u32[]{:S(2)}, u32[]{:S(2)}) collective-permute-start(f32[7,10,16,128]{3,2,1,0:T(8,128)S(1)} %get-tuple-element.42.x0), channel_id=1, source_target_pairs={{0,704},{64,0},{128,64},{192,128},{256,192},{320,256},{384,320},{4... | collective-permute-start | bytes 1720328 | tf_op jit(solution)/shard_map/ppermute | solution.py:418
  27.2 16.1 %collective-permute-start.2 = (f32[7,10,16,128]{3,2,1,0:T(8,128)S(1)}, f32[7,10,16,128]{3,2,1,0:T(8,128)S(1)}, u32[]{:S(2)}, u32[]{:S(2)}) collective-permute-start(f32[7,10,16,128]{3,2,1,0:T(8,128)S(1)} %get-tuple-element.42.x0), channel_id=1, source_target_pairs={{0,64},{64,128},{128,192},{192,256},{256,320},{320,384},{384,448},... | collective-permute-start | bytes 1720328 | tf_op jit(solution)/shard_map/ppermute | solution.py:418
  29.1 6.3 %collective-permute-start.4 = (f32[7,10,8,128]{3,2,1,0:T(8,128)S(1)}, f32[7,10,8,128]{3,2,1,0:T(8,128)S(1)}, u32[]{:S(2)}, u32[]{:S(2)}) collective-permute-start(f32[7,10,8,128]{3,2,1,0:T(8,128)S(1)} %get-tuple-element.43), channel_id=1, source_target_pairs={{0,4},{4,8},{8,12},{12,16},{16,20},{20,24},{24,28},{28,32},{32,36}... | collective-permute-start | bytes 860168 | tf_op jit(solution)/shard_map/ppermute | solution.py:418
  31.8 6.4 %collective-permute-start.5 = (f32[7,10,8,128]{3,2,1,0:T(8,128)S(1)}, f32[7,10,8,128]{3,2,1,0:T(8,128)S(1)}, u32[]{:S(2)}, u32[]{:S(2)}) collective-permute-start(f32[7,10,8,128]{3,2,1,0:T(8,128)S(1)} %get-tuple-element.44), channel_id=1, source_target_pairs={{0,60},{4,0},{8,4},{12,8},{16,12},{20,16},{24,20},{28,24},{32,28},... | collective-permute-start | bytes 860168 | tf_op jit(solution)/shard_map/ppermute | solution.py:418
  43.3 9.1 %collective-permute-start.6 = (f32[7,16,8,128]{3,2,1,0:T(8,128)S(1)}, f32[7,16,8,128]{3,2,1,0:T(8,128)S(1)}, u32[]{:S(2)}, u32[]{:S(2)}) collective-permute-start(f32[7,16,8,128]{3,2,1,0:T(8,128)S(1)} %get-tuple-element.49), channel_id=1, source_target_pairs={{0,4},{4,8},{8,12},{12,16},{16,20},{20,24},{24,28},{28,32},{32,36}... | collective-permute-start | bytes 1376264 | tf_op jit(solution)/shard_map/ppermute | solution.py:418
  46.9 7.9 %collective-permute-start.7 = (f32[7,16,8,128]{3,2,1,0:T(8,128)S(1)}, f32[7,16,8,128]{3,2,1,0:T(8,128)S(1)}, u32[]{:S(2)}, u32[]{:S(2)}) collective-permute-start(f32[7,16,8,128]{3,2,1,0:T(8,128)S(1)} %get-tuple-element.50), channel_id=1, source_target_pairs={{0,60},{4,0},{8,4},{12,8},{16,12},{20,16},{24,20},{28,24},{32,28},... | collective-permute-start | bytes 1376264 | tf_op jit(solution)/shard_map/ppermute | solution.py:418
  62.5 51.5 %copy-start.1 = (f32[3,8,16,128]{3,2,1,0:T(8,128)S(1)}, f32[3,8,16,128]{3,2,1,0:T(8,128)}, u32[]{:S(2)}) copy-start(f32[3,8,16,128]{3,2,1,0:T(8,128)} %residual_in.1) | copy-start | bytes 589828
  62.5 51.5 %copy-start.4 = (f32[3,8,16,128]{3,2,1,0:T(8,128)S(1)}, f32[3,8,16,128]{3,2,1,0:T(8,128)}, u32[]{:S(2)}) copy-start(f32[3,8,16,128]{3,2,1,0:T(8,128)} %param.4) | copy-start | bytes 589828
  62.5 6.6 %collective-permute-start.8 = (f32[2,3,8,256]{3,2,1,0:T(8,128)S(1)}, f32[2,3,8,256]{3,2,1,0:T(8,128)S(1)}, u32[]{:S(2)}, u32[]{:S(2)}) collective-permute-start(f32[2,3,8,256]{3,2,1,0:T(8,128)S(1)} %get-tuple-element.51), channel_id=1, source_target_pairs={{0,64},{64,128},{128,192},{192,256},{256,320},{320,384},{384,448},... | collective-permute-start | bytes 147464 | tf_op jit(solution)/shard_map/ppermute | solution.py:418
  64.6 5.7 %collective-permute-start.9 = (f32[2,3,8,256]{3,2,1,0:T(8,128)S(1)}, f32[2,3,8,256]{3,2,1,0:T(8,128)S(1)}, u32[]{:S(2)}, u32[]{:S(2)}) collective-permute-start(f32[2,3,8,256]{3,2,1,0:T(8,128)S(1)} %get-tuple-element.53), channel_id=1, source_target_pairs={{0,704},{64,0},{128,64},{192,128},{256,192},{320,256},{384,320},{4... | collective-permute-start | bytes 147464 | tf_op jit(solution)/shard_map/ppermute | solution.py:418
  70.4 2.4 %collective-permute-start.10 = (f32[2,3,8,256]{3,2,1,0:T(8,128)S(1)}, f32[2,3,8,256]{3,2,1,0:T(8,128)S(1)}, u32[]{:S(2)}, u32[]{:S(2)}) collective-permute-start(f32[2,3,8,256]{3,2,1,0:T(8,128)S(1)} %get-tuple-element.54), channel_id=1, source_target_pairs={{0,4},{4,8},{8,12},{12,16},{16,20},{20,24},{24,28},{28,32},{32,36}... | collective-permute-start | bytes 147464 | tf_op jit(solution)/shard_map/ppermute | solution.py:418
  71.6 3.8 %collective-permute-start.11 = (f32[2,3,8,256]{3,2,1,0:T(8,128)S(1)}, f32[2,3,8,256]{3,2,1,0:T(8,128)S(1)}, u32[]{:S(2)}, u32[]{:S(2)}) collective-permute-start(f32[2,3,8,256]{3,2,1,0:T(8,128)S(1)} %get-tuple-element.55), channel_id=1, source_target_pairs={{0,60},{4,0},{8,4},{12,8},{16,12},{20,16},{24,20},{28,24},{32,28},... | collective-permute-start | bytes 147464 | tf_op jit(solution)/shard_map/ppermute | solution.py:418

commit v8 on v7

--- a/solution.py
+++ b/solution.py
@@ -26,7 +26,6 @@
 FIELDS = 7
 
 VMEM = pl.BlockSpec(memory_space=pltpu.VMEM)
-SMEM = pl.BlockSpec(memory_space=pltpu.SMEM)
 
 
 def call(kernel, outs, scratch=(), limit=4, flops=0):
@@ -40,6 +39,17 @@
     )
 
 
+def kernel_call(kernel, outs, arrays, scratch=(), limit=4):
+    return pl.pallas_call(
+        kernel,
+        out_shape=[jax.ShapeDtypeStruct(s, F32) for s in outs],
+        in_specs=[VMEM] * arrays,
+        out_specs=[VMEM] * len(outs),
+        scratch_shapes=[pltpu.VMEM(s, F32) for s in scratch],
+        compiler_params=pltpu.CompilerParams(vmem_limit_bytes=limit * MIB),
+    )
+
+
 def before(v, k, axis):
     return pltpu.roll(v, k, axis)
 
@@ -116,14 +126,19 @@
     down[...] = brick[:, :, 0:8]
 
 
-def slab_kernel(xl, xr, up, down):
-    for first, brick, near, far in ((0, xl, 4, 0), (SLAB, xr, 0, 4)):
-        for out, row, row4 in ((up, 8, 12), (down, 0, 0)):
-            out[:, first : first + 4] = brick[:, near : near + 4, row : row + 8]
-            out[:, first + 4 : first + 6] = brick[:, CX : CX + 2, row : row + 8]
-            for p in range(4):
-                at = slice(4 * (p % 2), 4 * (p % 2) + 4)
-                out[:, first + 6 + p // 2, at] = brick[:, far + p, row4 : row4 + 4]
+def slab_kernel(xa, xb, up, down):
+    for core in range(2):
+        xl, xr = (xa, xb) if core else (xb, xa)
+
+        @pl.when(lax.axis_index("co") == core)
+        def _():
+            for first, brick, near, far in ((0, xl, 4, 0), (SLAB, xr, 0, 4)):
+                for out, row, row4 in ((up, 8, 12), (down, 0, 0)):
+                    out[:, first : first + 4] = brick[:, near : near + 4, row : row + 8]
+                    out[:, first + 4 : first + 6] = brick[:, CX : CX + 2, row : row + 8]
+                    for p in range(4):
+                        at = slice(4 * (p % 2), 4 * (p % 2) + 4)
+                        out[:, first + 6 + p // 2, at] = brick[:, far + p, row4 : row4 + 4]
 
 
 def steps(start, stop, each, body):
@@ -151,12 +166,14 @@
 
 
 def fine_kernel(
-    ends, xl, x0, xr, lower0, upper0, lower, upper,
-    ext, ux, uy, uz, inv, mux, muy, muz, mig, mc, o_right, o_left, o_own,
+    x0, xa, xb, lower0, upper0, lower, upper,
+    ext, ux, uy, uz, inv, mux, muy, muz, mig, mc, o_a, o_b, o_own,
     mm, spring, mrhs, cx_, cy_, cz_, cg, tmp32, tmp16,
 ):
     block = lane_of((CY, CZ)) // ZH
     block8 = lane_of((8, CZ)) // ZH
+
+    first_core = lax.axis_index("co") == 0
 
     def put(f, p, start, main, from_left, from_right, at):
         halo = jnp.where(at == p % CX, from_right, from_left)
@@ -167,8 +184,14 @@
     def assemble(f, _):
         for p in range(PLANES):
             b, q = p // CX, p % CX
-            brick = (xl, x0, xr)[b]
-            put(f, p, 8, brick[f, q], brick[f, CX], brick[f, CX + 1], block)
+
+            def mine(at):
+                if b == 1:
+                    return x0[f, at]
+                left, right = xb[f, at], xa[f, at]
+                return jnp.where(first_core, left, right) if b == 0 else jnp.where(first_core, right, left)
+
+            put(f, p, 8, mine(q), mine(CX), mine(CX + 1), block)
             for start, own, side, turn in ((0, lower0, lower, 0), (8 + CY, upper0, upper, 1)):
                 if b == 1:
                     v, zs = own[f, q], (own[f, CX], own[f, CX + 1])
@@ -185,16 +208,19 @@
 
     lax.fori_loop(0, FIELDS, assemble, 0)
 
-    lo_x, hi_x, lo_y, hi_y, lo_z, hi_z = (ends[i] for i in range(6))
+    ix, iz = lax.axis_index("gx"), lax.axis_index("gz")
+    iy = 2 * lax.axis_index("gc") + lax.axis_index("co")
+    lo_x, lo_y, lo_z = ix == 0, iy == 0, iz == 0
+    hi_x, hi_y, hi_z = ix == lax.axis_size("gx") - 1, iy == 2 * lax.axis_size("gc") - 1, iz == lax.axis_size("gz") - 1
     shape = (ROWS, LANES)
     row = lax.broadcasted_iota(jnp.int32, shape, 0)
     col = lane_of(shape)
-    half_y = jnp.where(((row == 7) & (lo_y == 1)) | ((row == 7 + CY) & (hi_y == 1)), 0.0, 0.5)
-    half_z = jnp.where(((col == LANES - 1) & (lo_z == 1)) | ((col == CZ - 1) & (hi_z == 1)), 0.0, 0.5)
+    half_y = jnp.where(((row == 7) & lo_y) | ((row == 7 + CY) & hi_y), 0.0, 0.5)
+    half_z = jnp.where(((col == LANES - 1) & lo_z) | ((col == CZ - 1) & hi_z), 0.0, 0.5)
 
     def links(p, _):
         here = ext[0, p]
-        cut = ((p == 7) & (lo_x == 1)) | ((p == 7 + CX) & (hi_x == 1))
+        cut = ((p == 7) & lo_x) | ((p == 7 + CX) & hi_x)
         ux[p] = jnp.where(cut, 0.0, 0.5) * (here + ext[0, jnp.minimum(p + 1, PLANES - 1)])
         uy[p] = half_y * (here + after(here, 1, 0))
         uz[p] = half_z * (here + after(here, 1, 1))
@@ -255,6 +281,7 @@
         cg[s] = pair_sum(a + b, 2)
 
     quad = lane_of((8, LANES)) % 4
+    sent = []
     for s in range(1, 5):
         g = cg[s] + cx_[s] + cx_[s - 1]
         g = g + cy_[s] + before(cy_[s], 1, 0) + cz_[s] + before(cz_[s], 4, 1)
@@ -268,13 +295,14 @@
             rhs.append(pair_sum(a + b, 2))
         first = jnp.where(quad == 0, rhs[0], jnp.where(quad == 1, rhs[1], jnp.where(quad == 2, rhs[2], g)))
         second = jnp.where(quad == 0, cx_[s], jnp.where(quad == 1, cy_[s], cz_[s]))
-        for i, v in enumerate((first, second)):
-            if s <= 3:
-                o_right[i, s - 1] = v
-            if s >= 2:
-                o_left[i, s - 2] = v
-            if s in (2, 3):
-                o_own[i, s - 2] = v
+        sent.append((first, second))
+    for i in range(2):
+        for k in range(3):
+            right, left = sent[k][i], sent[k + 1][i]
+            o_a[i, k] = jnp.where(first_core, left, right)
+            o_b[i, k] = jnp.where(first_core, right, left)
+        for k in range(2):
+            o_own[i, k] = sent[1 + k][i]
 
 
 def unpack(v, quad, count):
@@ -289,18 +317,25 @@
     ]
 
 
-def turn_kernel(xl, own, xr, up, down):
+def coarse_plane(xa, own, xb, i, s):
+    if 3 <= s < 5:
+        return own[i, s - 3]
+    k = s % 5
+    first = lax.axis_index("co") == 0
+    return jnp.where(first, xb[i, k], xa[i, k]) if s < 3 else jnp.where(first, xa[i, k], xb[i, k])
+
+
+def turn_kernel(xa, own, xb, up, down):
     for i in range(2):
         for s in range(8):
+            v = coarse_plane(xa, own, xb, i, s)
             for j in range(3):
-                for out, first in ((up, 3), (down, 2)):
-                    at = slice(first + j, first + j + 1)
-                    src = xl[i, s, at] if s < 3 else own[i, s - 3, at] if s < 5 else xr[i, s - 5, at]
-                    out[i, j, s : s + 1] = src
+                up[i, j, s : s + 1] = v[3 + j : 4 + j]
+                down[i, j, s : s + 1] = v[2 + j : 3 + j]
 
 
 def solve_kernel(
-    xl, own, xr, yl, yr, ext, ux_, uy_, uz_, ig_, mux_, muy_, muz_, mig_, mc_,
+    xa, own, xb, yl, yr, ext, ux_, uy_, uz_, ig_, mux_, muy_, muz_, mig_, mc_,
     direction, image, sums,
     packed, cc, pm, pf, m1, base, d, tmp16,
 ):
@@ -313,7 +348,7 @@
         for s in range(8):
             here = packed.at[8 * i + s]
             here[...] = jnp.zeros((16, LANES), F32)
-            here[4:8] = xl[i, s, 2:6] if s < 3 else own[i, s - 3, 2:6] if s < 5 else xr[i, s - 5, 2:6]
+            here[4:8] = coarse_plane(xa, own, xb, i, s)[2:6]
             for j in range(3):
                 here[1 + j : 2 + j] = yl[i, j, s : s + 1]
                 here[8 + j : 9 + j] = yr[i, j, s : s + 1]
@@ -409,10 +444,6 @@
     nx, nc, nz = lax.axis_size("gx"), lax.axis_size("gc"), lax.axis_size("gz")
     ny = 2 * nc
     y_axes = ("gc", "co")
-    ix, iz = lax.axis_index("gx"), lax.axis_index("gz")
-    iy = 2 * lax.axis_index("gc") + lax.axis_index("co")
-    ends = jnp.stack([ix == 0, ix == nx - 1, iy == 0, iy == ny - 1, iz == 0, iz == nz - 1]).astype(jnp.int32)
-
     def both(v, axes, count):
         up, down = v if isinstance(v, tuple) else (v, v)
         return lax.ppermute(up, axes, ring(count, 1)), lax.ppermute(down, axes, ring(count, -1))
@@ -435,11 +466,18 @@
     zl, zr = both((to_right, to_left), "gz", nz)
     (main,) = call(main_kernel, [(FIELDS, CX, CY, CZ)], flops=10**9)(density_bins, residual, fixed_dofs)
     join = call(join_kernel, [brick, slab, slab])(main, zl, zr)
-    x0, up, down, ends = lax.optimization_barrier((*join, ends))
-    xl, xr = both(x0, "gx", nx)
+    x0, up, down = lax.optimization_barrier(tuple(join))
+
+    def cross(a, b):
+        return tuple(
+            lax.ppermute(v, ("gx", "co"), [(2 * i + c, 2 * ((i + turn * (2 * c - 1)) % nx) + c) for i in range(nx) for c in range(2)])
+            for v, turn in ((a, 1), (b, -1))
+        )
+
+    xa, xb = cross(x0, x0)
     lower0, upper0 = both((up, down), y_axes, ny)
-    xl, xr, lower0, upper0 = lax.optimization_barrier((xl, xr, lower0, upper0))
-    lower, upper = both(tuple(call(slab_kernel, [slabs, slabs])(xl, xr)), y_axes, ny)
+    xa, xb, lower0, upper0 = lax.optimization_barrier((xa, xb, lower0, upper0))
+    lower, upper = both(tuple(kernel_call(slab_kernel, [slabs, slabs], 2)(xa, xb)), y_axes, ny)
 
     full = (12, ROWS, LANES)
     half = (8, ROWS // 2, LANES)
@@ -449,24 +487,18 @@
     outs += [(2, 3, 8, LANES), (2, 3, 8, LANES), (2, 2, 8, LANES)]
     scratch = [(3,) + all_f, all_m, (3,) + all_m]
     scratch += [(5, 8, LANES)] * 4 + [(24, 2, ROWS, CZ), (32, 2, ROWS // 2, CZ)]
-    fine = pl.pallas_call(
-        fine_kernel,
-        out_shape=[jax.ShapeDtypeStruct(s, F32) for s in outs],
-        in_specs=[SMEM] + [VMEM] * 7,
-        out_specs=[VMEM] * len(outs),
-        scratch_shapes=[pltpu.VMEM(s, F32) for s in scratch],
-        compiler_params=pltpu.CompilerParams(vmem_limit_bytes=8 * MIB),
-    )(ends, xl, x0, xr, lower0, upper0, lower, upper)
-    kept, (to_right, to_left, own) = fine[:-3], fine[-3:]
-    cl, cr = both((to_right, to_left), "gx", nx)
-    up, down = call(turn_kernel, [(2, 3, 8, LANES)] * 2)(cl, own, cr)
+    fine = kernel_call(fine_kernel, outs, 7, scratch, 8)(x0, xa, xb, lower0, upper0, lower, upper)
+    kept, (a, b, own) = fine[:-3], fine[-3:]
+    ca, cb = cross(a, b)
+    up, down = kernel_call(turn_kernel, [(2, 3, 8, LANES)] * 2, 3)(ca, own, cb)
     dl, dr = both((up, down), y_axes, ny)
-    direction, image, sums = call(
+    direction, image, sums = kernel_call(
         solve_kernel,
         [(3, CX, CY, CZ), (3, CX, CY, CZ), (2, CZ)],
+        5 + len(kept),
         [(16, 16, LANES), (12, 2, ROWS // 2, CZ), (3,) + half, (9, 2, ROWS, CZ), (3,) + full, (3,) + full, (3,) + full, (12, 16, LANES)],
         10,
-    )(cl, own, cr, dl, dr, *kept)
+    )(ca, own, cb, dl, dr, *kept)
     sums = all_sum(all_sum(sums, ("gc", "gz")), ("gx", "co"))
     alpha = (sums[0] / sums[1])[None, None, None]
     return (solution + alpha * direction, residual - alpha * image, direction)

time: 116 us -> 112 us (0.966)
  waiting for transfers between devices: 24.2 us -> 22 us
  blocking collectives: 34.9 us -> 33.5 us
    ppermute x0 -> x4, starting transfers between devices: none -> 23.2 us  [cross(): lax.ppermute(v, ('gx', 'co'), [(2 * i + c, 2 * ((i + turn * (2 * c - 1))...]
    ppermute x6 -> x4, starting transfers between devices: 22.3 us -> 4.1 us  [both(): lax.ppermute(down, axes, ring(count, -1))]
    ppermute x6 -> x4, waiting for transfers between devices: 15.2 us -> 9.26 us  [both(): lax.ppermute(up, axes, ring(count, 1))]
    ppermute x0 -> x4, waiting for transfers between devices: none -> 4.79 us  [cross(): lax.ppermute(v, ('gx', 'co'), [(2 * i + c, 2 * ((i + turn * (2 * c - 1))...]
    ppermute x6 -> x4, starting transfers between devices: 15.4 us -> 11.1 us  [both(): lax.ppermute(up, axes, ring(count, 1))]
    all_to_all x2, blocking collectives: 34.9 us -> 33.5 us  [all_sum(): return lax.all_to_all(sent, axes, 0, 0).sum(axis=0)]
    ppermute x6 -> x4, waiting for transfers between devices: 9.05 us -> 7.91 us  [both(): lax.ppermute(down, axes, ring(count, -1))]
where the time goes in v8:
time: 112 us
  starting transfers between devices  38.4 us (34%)
  blocking collectives  33.5 us (30%)
  waiting for transfers between devices  22 us (20%)
  Pallas kernels  12.5 us (11%)
  local copies, waits for them, and re-layouts  2.72 us (2%)
  other arithmetic  1.81 us (2%)
    all_to_all x2, blocking collectives, all_sum(): return lax.all_to_all(sent, axes, 0, 0).sum(axis=0)  33.5 us
    ppermute x4, starting transfers between devices, cross(): lax.ppermute(v, ('gx', 'co'), [(2 * i + c, 2 * ((i + turn * (2 * c - 1))...  23.2 us
    ppermute x4, starting transfers between devices, both(): lax.ppermute(up, axes, ring(count, 1))  11.1 us
    ppermute x4, waiting for transfers between devices, both(): lax.ppermute(up, axes, ring(count, 1))  9.26 us
    ppermute x4, waiting for transfers between devices, both(): lax.ppermute(down, axes, ring(count, -1))  7.91 us
    pallas_call x1, Pallas kernels, shards(): kernel_call(fine_kernel, outs, 7, scratch, 8)  6.86 us
    ppermute x4, waiting for transfers between devices, cross(): lax.ppermute(v, ('gx', 'co'), [(2 * i + c, 2 * ((i + turn * (2 * c - 1))...  4.79 us
    ppermute x4, starting transfers between devices, both(): lax.ppermute(down, axes, ring(count, -1))  4.1 us
  transfers between devices with their start and end apart: 12, of which 8 were waited for; matrix products, arithmetic and copies ran while one was open for 0% of the time, Pallas kernels for 0%

profile of v8, /device:TPU:1, one launch (start us, length us, event | category | flops | bytes accessed | tf_op | source)
XLA Modules:
  0.0 111.7 jit_solution(6120547860989991447)
XLA Ops:
  0.6 1.9 %shard_map.68 = (f32[7,16,128]{2,1,0:T(8,128)}, f32[7,16,128]{2,1,0:T(8,128)}) custom-call(s32[8,16,128]{2,1,0:T(8,128)} %density_in.1, f32[3,8,16,128]{3,2,1,0:T(8,128)} %residual_in.1, s32[3,8,16,128]{3,2,1,0:T(8,128)} %fixed_in.1), custom_call_target="tpu_custom_call" | custom-call | tf_op jit(solution)/shard_map/pallas_call | solution.py:453
  2.5 3.9 %collective-permute-start = (f32[7,16,128]{2,1,0:T(8,128)}, f32[7,16,128]{2,1,0:T(8,128)S(1)}, u32[]{:S(2)}, u32[]{:S(2)}) collective-permute-start(f32[7,16,128]{2,1,0:T(8,128)} %get-tuple-element.32), channel_id=1, source_target_pairs={{0,1},{1,2},{2,3},{3,0},{4,5},{5,6},{6,7},{7,4},{8,9},{9,10},{10,1... | collective-permute-start | bytes 172040 | tf_op jit(solution)/shard_map/ppermute | solution.py:449
  6.5 3.2 %collective-permute-start.1 = (f32[7,16,128]{2,1,0:T(8,128)}, f32[7,16,128]{2,1,0:T(8,128)S(1)}, u32[]{:S(2)}, u32[]{:S(2)}) collective-permute-start(f32[7,16,128]{2,1,0:T(8,128)} %get-tuple-element.33), channel_id=1, source_target_pairs={{0,3},{1,0},{2,1},{3,2},{4,7},{5,4},{6,5},{7,6},{8,11},{9,8},{10,9... | collective-permute-start | bytes 172040 | tf_op jit(solution)/shard_map/ppermute | solution.py:449
  9.7 0.0 copy-start
  9.7 0.9 copy-done
  10.6 0.0 copy-start.2
  10.6 0.9 copy-done.2
  11.6 0.0 copy-start.3
  11.6 0.8 copy-done.3
  12.4 0.0 collective-permute-done.zl
  12.4 0.0 collective-permute-done.1.zr
  12.5 0.1 shard_map.69
  12.5 14.5 %collective-permute-start.3 = (f32[7,10,16,128]{3,2,1,0:T(8,128)S(1)}, f32[7,10,16,128]{3,2,1,0:T(8,128)S(1)}, u32[]{:S(2)}, u32[]{:S(2)}) collective-permute-start(f32[7,10,16,128]{3,2,1,0:T(8,128)S(1)} %get-tuple-element.34.x0), channel_id=1, source_target_pairs={{0,64},{4,708},{64,128},{68,4},{128,192},{132,68},{192,256},{196,1... | collective-permute-start | bytes 1720328 | tf_op jit(solution)/shard_map/ppermute | solution.py:473
  27.0 1.9 %collective-permute-start.2 = (f32[7,10,16,128]{3,2,1,0:T(8,128)S(1)}, f32[7,10,16,128]{3,2,1,0:T(8,128)S(1)}, u32[]{:S(2)}, u32[]{:S(2)}) collective-permute-start(f32[7,10,16,128]{3,2,1,0:T(8,128)S(1)} %get-tuple-element.34.x0), channel_id=1, source_target_pairs={{0,704},{4,68},{64,0},{68,132},{128,64},{132,196},{192,128},{196,2... | collective-permute-start | bytes 1720328 | tf_op jit(solution)/shard_map/ppermute | solution.py:473
  29.0 2.7 %collective-permute-start.4 = (f32[7,10,8,128]{3,2,1,0:T(8,128)S(1)}, f32[7,10,8,128]{3,2,1,0:T(8,128)S(1)}, u32[]{:S(2)}, u32[]{:S(2)}) collective-permute-start(f32[7,10,8,128]{3,2,1,0:T(8,128)S(1)} %get-tuple-element.35), channel_id=1, source_target_pairs={{0,4},{4,8},{8,12},{12,16},{16,20},{20,24},{24,28},{28,32},{32,36}... | collective-permute-start | bytes 860168 | tf_op jit(solution)/shard_map/ppermute | solution.py:449
  31.7 0.0 collective-permute-start.5
  31.7 3.6 %collective-permute-done.4.lower0 = f32[7,10,8,128]{3,2,1,0:T(8,128)S(1)} collective-permute-done((f32[7,10,8,128]{3,2,1,0:T(8,128)S(1)}, f32[7,10,8,128]{3,2,1,0:T(8,128)S(1)}, u32[]{:S(2)}, u32[]{:S(2)}) %collective-permute-start.4) | collective-permute-done | bytes 286752 | tf_op jit(solution)/shard_map/ppermute | solution.py:449
  35.3 2.8 %collective-permute-done.5.upper0 = f32[7,10,8,128]{3,2,1,0:T(8,128)S(1)} collective-permute-done((f32[7,10,8,128]{3,2,1,0:T(8,128)S(1)}, f32[7,10,8,128]{3,2,1,0:T(8,128)S(1)}, u32[]{:S(2)}, u32[]{:S(2)}) %collective-permute-start.5) | collective-permute-done | bytes 286752 | tf_op jit(solution)/shard_map/ppermute | solution.py:449
  38.0 0.0 collective-permute-done.3.xb
  38.0 3.6 %collective-permute-done.2.xa = f32[7,10,16,128]{3,2,1,0:T(8,128)S(1)} collective-permute-done((f32[7,10,16,128]{3,2,1,0:T(8,128)S(1)}, f32[7,10,16,128]{3,2,1,0:T(8,128)S(1)}, u32[]{:S(2)}, u32[]{:S(2)}) %collective-permute-start.2) | collective-permute-done | bytes 573472 | tf_op jit(solution)/shard_map/ppermute | solution.py:473
  41.7 0.1 shard_map.70
  41.8 0.0 collective-permute-start.6
  41.8 0.5 collective-permute-start.7
  42.3 4.9 %collective-permute-done.6.lower = f32[7,16,8,128]{3,2,1,0:T(8,128)S(1)} collective-permute-done((f32[7,16,8,128]{3,2,1,0:T(8,128)S(1)}, f32[7,16,8,128]{3,2,1,0:T(8,128)S(1)}, u32[]{:S(2)}, u32[]{:S(2)}) %collective-permute-start.6) | collective-permute-done | bytes 458784 | tf_op jit(solution)/shard_map/ppermute | solution.py:449
  47.2 2.8 %collective-permute-done.7.upper = f32[7,16,8,128]{3,2,1,0:T(8,128)S(1)} collective-permute-done((f32[7,16,8,128]{3,2,1,0:T(8,128)S(1)}, f32[7,16,8,128]{3,2,1,0:T(8,128)S(1)}, u32[]{:S(2)}, u32[]{:S(2)}) %collective-permute-start.7) | collective-permute-done | bytes 458784 | tf_op jit(solution)/shard_map/ppermute | solution.py:449
  50.0 6.9 %shard_map.71 = (f32[7,24,32,256]{3,2,1,0:T(8,128)S(1)}, f32[24,32,256]{2,1,0:T(8,128)S(1)}, f32[24,32,256]{2,1,0:T(8,128)S(1)}, f32[24,32,256]{2,1,0:T(8,128)S(...) custom-call(f32[7,10,16,128]{3,2,1,0:T(8,128)S(1)} %get-tuple-elemen, ...), custom_call_target="tpu_custom_call" | custom-call | tf_op jit(solution)/shard_map/pallas_call | solution.py:490
  56.9 0.0 copy-start.1
  56.9 0.0 copy-start.4
  56.9 2.1 %collective-permute-start.8 = (f32[2,3,8,256]{3,2,1,0:T(8,128)S(1)}, f32[2,3,8,256]{3,2,1,0:T(8,128)S(1)}, u32[]{:S(2)}, u32[]{:S(2)}) collective-permute-start(f32[2,3,8,256]{3,2,1,0:T(8,128)S(1)} %get-tuple-element.43), channel_id=1, source_target_pairs={{0,704},{4,68},{64,0},{68,132},{128,64},{132,196},{192,128},{196,2... | collective-permute-start | bytes 147464 | tf_op jit(solution)/shard_map/ppermute | solution.py:473
  59.0 4.8 %collective-permute-start.9 = (f32[2,3,8,256]{3,2,1,0:T(8,128)S(1)}, f32[2,3,8,256]{3,2,1,0:T(8,128)S(1)}, u32[]{:S(2)}, u32[]{:S(2)}) collective-permute-start(f32[2,3,8,256]{3,2,1,0:T(8,128)S(1)} %get-tuple-element.45), channel_id=1, source_target_pairs={{0,64},{4,708},{64,128},{68,4},{128,192},{132,68},{192,256},{196,1... | collective-permute-start | bytes 147464 | tf_op jit(solution)/shard_map/ppermute | solution.py:473
  63.7 0.0 collective-permute-done.8.xa
  63.8 1.1 %collective-permute-done.9.xb = f32[2,3,8,256]{3,2,1,0:T(8,128)S(1)} collective-permute-done((f32[2,3,8,256]{3,2,1,0:T(8,128)S(1)}, f32[2,3,8,256]{3,2,1,0:T(8,128)S(1)}, u32[]{:S(2)}, u32[]{:S(2)}) %collective-permute-start.9) | collective-permute-done | bytes 49184 | tf_op jit(solution)/shard_map/ppermute | solution.py:473
  65.0 4.4 %collective-permute-start.10 = (f32[2,3,8,256]{3,2,1,0:T(8,128)S(1)}, f32[2,3,8,256]{3,2,1,0:T(8,128)S(1)}, u32[]{:S(2)}, u32[]{:S(2)}) collective-permute-start(f32[2,3,8,256]{3,2,1,0:T(8,128)S(1)} %get-tuple-element.46), channel_id=1, source_target_pairs={{0,4},{4,8},{8,12},{12,16},{16,20},{20,24},{24,28},{28,32},{32,36}... | collective-permute-start | bytes 147464 | tf_op jit(solution)/shard_map/ppermute | solution.py:449
  69.4 0.4 collective-permute-start.11
  69.8 0.8 collective-permute-done.10.yl
  70.5 2.3 %collective-permute-done.11.yr = f32[2,3,8,256]{3,2,1,0:T(8,128)S(1)} collective-permute-done((f32[2,3,8,256]{3,2,1,0:T(8,128)S(1)}, f32[2,3,8,256]{3,2,1,0:T(8,128)S(1)}, u32[]{:S(2)}, u32[]{:S(2)}) %collective-permute-start.11) | collective-permute-done | bytes 49184 | tf_op jit(solution)/shard_map/ppermute | solution.py:449
  72.9 3.4 %shard_map.73 = (f32[3,8,16,128]{3,2,1,0:T(8,128)}, f32[3,8,16,128]{3,2,1,0:T(8,128)S(1)}, f32[2,128]{1,0:T(2,128)S(1)}) custom-call(f32[2,3,8,256]{3,2,1,0:T(8,128)S(1)} %collective-permute-done.8.xa, f32[2,2,8,256]{3,2,1,0:T(8,128)S(1)} %get-tuple-element.44.own, f32[2,3,8,256]{3,2,1,0:T(8,128)S(1)} %collective-permute-done.9.xb, ...), custom_call_target="tpu_custom_call" | custom-call | tf_op jit(solution)/shard_map/pallas_call | solution.py:495
  76.3 19.4 %all_to_all.10 = f32[32,2,128]{2,1,0:T(2,128)S(1)} all-to-all(f32[32,2,128]{2,1,0:T(2,128)S(1)} %broadcast_in_dim.4), channel_id=1, replica_groups=mesh['gx'=12,'gc'=8,'co'=2,'gz'=4] {'gc','gz'}, dimensions={0} | all-to-all | bytes 65536 | tf_op jit(solution)/shard_map/all_to_all | solution.py:440
  95.8 14.1 %all_to_all.11 = f32[24,2,128]{2,1,0:T(2,128)S(1)} all-to-all(f32[24,2,128]{2,1,0:T(2,128)S(1)} %broadcast_in_dim.5), channel_id=1, replica_groups=mesh['gx'=12,'gc'=8,'co'=2,'gz'=4] {'gx','co'}, dimensions={0} | all-to-all | bytes 49152 | tf_op jit(solution)/shard_map/all_to_all | solution.py:440
  109.9 0.0 copy-done.1
  109.9 0.0 copy-done.4
  110.0 1.7 %multiply_subtract_fusion = (f32[3,8,16,128]{3,2,1,0:T(8,128)}, f32[3,8,16,128]{3,2,1,0:T(8,128)}) fusion(f32[3,8,16,128]{3,2,1,0:T(8,128)S(1)} %copy-done.1, f32[3,8,16,128]{3,2,1,0:T(8,128)S(1)} %get-tuple-element.60, f32[128]{0:T(128)S(1)} %fusion, f32[3,8,16,128]{3,2,1,0:T(8,128)S(1)} %copy-done.4, f32[3,8,16,128]{3,2,1,0:T(8,128)} %get-tuple-element.31), kind=kLoop, calls=%fused_computation | loop fusion | flops 196608 | bytes 1180160 | tf_op jit(solution)/shard_map/sub | solution.py:504
  (7 shorter events, 0.2 us)
Async XLA Ops:
  2.5 9.9 %collective-permute-start = (f32[7,16,128]{2,1,0:T(8,128)}, f32[7,16,128]{2,1,0:T(8,128)S(1)}, u32[]{:S(2)}, u32[]{:S(2)}) collective-permute-start(f32[7,16,128]{2,1,0:T(8,128)} %get-tuple-element.32), channel_id=1, source_target_pairs={{0,1},{1,2},{2,3},{3,0},{4,5},{5,6},{6,7},{7,4},{8,9},{9,10},{10,1... | collective-permute-start | bytes 172040 | tf_op jit(solution)/shard_map/ppermute | solution.py:449
  6.5 5.9 %collective-permute-start.1 = (f32[7,16,128]{2,1,0:T(8,128)}, f32[7,16,128]{2,1,0:T(8,128)S(1)}, u32[]{:S(2)}, u32[]{:S(2)}) collective-permute-start(f32[7,16,128]{2,1,0:T(8,128)} %get-tuple-element.33), channel_id=1, source_target_pairs={{0,3},{1,0},{2,1},{3,2},{4,7},{5,4},{6,5},{7,6},{8,11},{9,8},{10,9... | collective-permute-start | bytes 172040 | tf_op jit(solution)/shard_map/ppermute | solution.py:449
  9.7 0.9 copy-start
  10.6 0.9 copy-start.2
  11.6 0.8 copy-start.3
  12.5 25.5 %collective-permute-start.3 = (f32[7,10,16,128]{3,2,1,0:T(8,128)S(1)}, f32[7,10,16,128]{3,2,1,0:T(8,128)S(1)}, u32[]{:S(2)}, u32[]{:S(2)}) collective-permute-start(f32[7,10,16,128]{3,2,1,0:T(8,128)S(1)} %get-tuple-element.34.x0), channel_id=1, source_target_pairs={{0,64},{4,708},{64,128},{68,4},{128,192},{132,68},{192,256},{196,1... | collective-permute-start | bytes 1720328 | tf_op jit(solution)/shard_map/ppermute | solution.py:473
  27.0 14.6 %collective-permute-start.2 = (f32[7,10,16,128]{3,2,1,0:T(8,128)S(1)}, f32[7,10,16,128]{3,2,1,0:T(8,128)S(1)}, u32[]{:S(2)}, u32[]{:S(2)}) collective-permute-start(f32[7,10,16,128]{3,2,1,0:T(8,128)S(1)} %get-tuple-element.34.x0), channel_id=1, source_target_pairs={{0,704},{4,68},{64,0},{68,132},{128,64},{132,196},{192,128},{196,2... | collective-permute-start | bytes 1720328 | tf_op jit(solution)/shard_map/ppermute | solution.py:473
  29.0 6.3 %collective-permute-start.4 = (f32[7,10,8,128]{3,2,1,0:T(8,128)S(1)}, f32[7,10,8,128]{3,2,1,0:T(8,128)S(1)}, u32[]{:S(2)}, u32[]{:S(2)}) collective-permute-start(f32[7,10,8,128]{3,2,1,0:T(8,128)S(1)} %get-tuple-element.35), channel_id=1, source_target_pairs={{0,4},{4,8},{8,12},{12,16},{16,20},{20,24},{24,28},{28,32},{32,36}... | collective-permute-start | bytes 860168 | tf_op jit(solution)/shard_map/ppermute | solution.py:449
  31.7 6.4 %collective-permute-start.5 = (f32[7,10,8,128]{3,2,1,0:T(8,128)S(1)}, f32[7,10,8,128]{3,2,1,0:T(8,128)S(1)}, u32[]{:S(2)}, u32[]{:S(2)}) collective-permute-start(f32[7,10,8,128]{3,2,1,0:T(8,128)S(1)} %get-tuple-element.36), channel_id=1, source_target_pairs={{0,60},{4,0},{8,4},{12,8},{16,12},{20,16},{24,20},{28,24},{32,28},... | collective-permute-start | bytes 860168 | tf_op jit(solution)/shard_map/ppermute | solution.py:449
  41.8 5.4 %collective-permute-start.6 = (f32[7,16,8,128]{3,2,1,0:T(8,128)S(1)}, f32[7,16,8,128]{3,2,1,0:T(8,128)S(1)}, u32[]{:S(2)}, u32[]{:S(2)}) collective-permute-start(f32[7,16,8,128]{3,2,1,0:T(8,128)S(1)} %get-tuple-element.41), channel_id=1, source_target_pairs={{0,4},{4,8},{8,12},{12,16},{16,20},{20,24},{24,28},{28,32},{32,36}... | collective-permute-start | bytes 1376264 | tf_op jit(solution)/shard_map/ppermute | solution.py:449
  41.8 8.2 %collective-permute-start.7 = (f32[7,16,8,128]{3,2,1,0:T(8,128)S(1)}, f32[7,16,8,128]{3,2,1,0:T(8,128)S(1)}, u32[]{:S(2)}, u32[]{:S(2)}) collective-permute-start(f32[7,16,8,128]{3,2,1,0:T(8,128)S(1)} %get-tuple-element.42), channel_id=1, source_target_pairs={{0,60},{4,0},{8,4},{12,8},{16,12},{20,16},{24,20},{28,24},{32,28},... | collective-permute-start | bytes 1376264 | tf_op jit(solution)/shard_map/ppermute | solution.py:449
  56.9 53.1 %copy-start.1 = (f32[3,8,16,128]{3,2,1,0:T(8,128)S(1)}, f32[3,8,16,128]{3,2,1,0:T(8,128)}, u32[]{:S(2)}) copy-start(f32[3,8,16,128]{3,2,1,0:T(8,128)} %residual_in.1) | copy-start | bytes 589828
  56.9 53.1 %copy-start.4 = (f32[3,8,16,128]{3,2,1,0:T(8,128)S(1)}, f32[3,8,16,128]{3,2,1,0:T(8,128)}, u32[]{:S(2)}) copy-start(f32[3,8,16,128]{3,2,1,0:T(8,128)} %param.4) | copy-start | bytes 589828
  56.9 6.8 %collective-permute-start.8 = (f32[2,3,8,256]{3,2,1,0:T(8,128)S(1)}, f32[2,3,8,256]{3,2,1,0:T(8,128)S(1)}, u32[]{:S(2)}, u32[]{:S(2)}) collective-permute-start(f32[2,3,8,256]{3,2,1,0:T(8,128)S(1)} %get-tuple-element.43), channel_id=1, source_target_pairs={{0,704},{4,68},{64,0},{68,132},{128,64},{132,196},{192,128},{196,2... | collective-permute-start | bytes 147464 | tf_op jit(solution)/shard_map/ppermute | solution.py:473
  59.0 5.9 %collective-permute-start.9 = (f32[2,3,8,256]{3,2,1,0:T(8,128)S(1)}, f32[2,3,8,256]{3,2,1,0:T(8,128)S(1)}, u32[]{:S(2)}, u32[]{:S(2)}) collective-permute-start(f32[2,3,8,256]{3,2,1,0:T(8,128)S(1)} %get-tuple-element.45), channel_id=1, source_target_pairs={{0,64},{4,708},{64,128},{68,4},{128,192},{132,68},{192,256},{196,1... | collective-permute-start | bytes 147464 | tf_op jit(solution)/shard_map/ppermute | solution.py:473
  65.0 5.6 %collective-permute-start.10 = (f32[2,3,8,256]{3,2,1,0:T(8,128)S(1)}, f32[2,3,8,256]{3,2,1,0:T(8,128)S(1)}, u32[]{:S(2)}, u32[]{:S(2)}) collective-permute-start(f32[2,3,8,256]{3,2,1,0:T(8,128)S(1)} %get-tuple-element.46), channel_id=1, source_target_pairs={{0,4},{4,8},{8,12},{12,16},{16,20},{20,24},{24,28},{28,32},{32,36}... | collective-permute-start | bytes 147464 | tf_op jit(solution)/shard_map/ppermute | solution.py:449
  69.4 3.5 %collective-permute-start.11 = (f32[2,3,8,256]{3,2,1,0:T(8,128)S(1)}, f32[2,3,8,256]{3,2,1,0:T(8,128)S(1)}, u32[]{:S(2)}, u32[]{:S(2)}) collective-permute-start(f32[2,3,8,256]{3,2,1,0:T(8,128)S(1)} %get-tuple-element.47), channel_id=1, source_target_pairs={{0,60},{4,0},{8,4},{12,8},{16,12},{20,16},{24,20},{28,24},{32,28},... | collective-permute-start | bytes 147464 | tf_op jit(solution)/shard_map/ppermute | solution.py:449

commit v9 on v8

--- a/solution.py
+++ b/solution.py
@@ -181,9 +181,11 @@
         ext[f, p, rows, 0:CZ] = main
         ext[f, p, rows, CZ:LANES] = pltpu.roll(halo, CZ - ZH * (p % CX), 1) if p % CX else halo
 
-    def assemble(f, _):
+    def assemble(f):
         for p in range(PLANES):
             b, q = p // CX, p % CX
+            if f and p in (0, PLANES - 1):
+                continue
 
             def mine(at):
                 if b == 1:
@@ -204,9 +206,9 @@
                         v = side[f, first + 6 + (q % 4) // 2]
                         v = before(v, 4, 0) if q % 2 == turn else v
                 put(f, p, start, v, *zs, block8)
-        return 0
-
-    lax.fori_loop(0, FIELDS, assemble, 0)
+
+    for f in range(FIELDS):
+        assemble(f)
 
     ix, iz = lax.axis_index("gx"), lax.axis_index("gz")
     iy = 2 * lax.axis_index("gc") + lax.axis_index("co")
@@ -461,7 +463,7 @@
             pltpu.VMEM((3, CX, CY, CZ), jnp.int32),
             pltpu.SemaphoreType.DMA((3,)),
         ],
-        compiler_params=pltpu.CompilerParams(vmem_limit_bytes=56 * MIB),
+        compiler_params=pltpu.CompilerParams(vmem_limit_bytes=56_410_000),
     )(density_bins, residual, fixed_dofs)
     zl, zr = both((to_right, to_left), "gz", nz)
     (main,) = call(main_kernel, [(FIELDS, CX, CY, CZ)], flops=10**9)(density_bins, residual, fixed_dofs)

time: 112 us -> 111 us (level)
  no operation moved by 1% of the time
where the time goes in v9:
time: 111 us; the launch traced here: 110 us
  starting transfers between devices  38.4 us (35%)
  blocking collectives  33.3 us (30%)
  waiting for transfers between devices  22 us (20%)
  Pallas kernels  11.5 us (10%)
  local copies, waits for them, and re-layouts  2.72 us (2%)
  other arithmetic  1.81 us (2%)
    all_to_all x2, blocking collectives, all_sum(): return lax.all_to_all(sent, axes, 0, 0).sum(axis=0)  33.3 us
    ppermute x4, starting transfers between devices, cross(): lax.ppermute(v, ('gx', 'co'), [(2 * i + c, 2 * ((i + turn * (2 * c - 1))...  23.2 us
    ppermute x4, starting transfers between devices, both(): lax.ppermute(up, axes, ring(count, 1))  11.1 us
    ppermute x4, waiting for transfers between devices, both(): lax.ppermute(up, axes, ring(count, 1))  9.26 us
    ppermute x4, waiting for transfers between devices, both(): lax.ppermute(down, axes, ring(count, -1))  7.91 us
    pallas_call x1, Pallas kernels, shards(): kernel_call(fine_kernel, outs, 7, scratch, 8)  6.52 us
    ppermute x4, waiting for transfers between devices, cross(): lax.ppermute(v, ('gx', 'co'), [(2 * i + c, 2 * ((i + turn * (2 * c - 1))...  4.79 us
    ppermute x4, starting transfers between devices, both(): lax.ppermute(down, axes, ring(count, -1))  4.1 us
  transfers between devices with their start and end apart: 12, of which 8 were waited for; matrix products, arithmetic and copies ran while one was open for 0% of the time, Pallas kernels for 0%

profile of v9, /device:TPU:1, one launch (start us, length us, event | category | flops | bytes accessed | tf_op | source)
XLA Modules:
  0.0 110.5 jit_solution(12550154051050391158)
XLA Ops:
  0.6 1.3 %shard_map.68 = (f32[7,16,128]{2,1,0:T(8,128)S(1)}, f32[7,16,128]{2,1,0:T(8,128)S(1)}) custom-call(s32[8,16,128]{2,1,0:T(8,128)} %density_in.1, f32[3,8,16,128]{3,2,1,0:T(8,128)} %residual_in.1, s32[3,8,16,128]{3,2,1,0:T(8,128)} %fixed_in.1), custom_call_target="tpu_custom_call" | custom-call | tf_op jit(solution)/shard_map/pallas_call | solution.py:455
  1.9 3.9 %collective-permute-start = (f32[7,16,128]{2,1,0:T(8,128)S(1)}, f32[7,16,128]{2,1,0:T(8,128)S(1)}, u32[]{:S(2)}, u32[]{:S(2)}) collective-permute-start(f32[7,16,128]{2,1,0:T(8,128)S(1)} %get-tuple-element.32), channel_id=1, source_target_pairs={{0,1},{1,2},{2,3},{3,0},{4,5},{5,6},{6,7},{7,4},{8,9},{9,10},{10,1... | collective-permute-start | bytes 172040 | tf_op jit(solution)/shard_map/ppermute | solution.py:451
  5.9 3.2 %collective-permute-start.1 = (f32[7,16,128]{2,1,0:T(8,128)S(1)}, f32[7,16,128]{2,1,0:T(8,128)S(1)}, u32[]{:S(2)}, u32[]{:S(2)}) collective-permute-start(f32[7,16,128]{2,1,0:T(8,128)S(1)} %get-tuple-element.33), channel_id=1, source_target_pairs={{0,3},{1,0},{2,1},{3,2},{4,7},{5,4},{6,5},{7,6},{8,11},{9,8},{10,9... | collective-permute-start | bytes 172040 | tf_op jit(solution)/shard_map/ppermute | solution.py:451
  9.1 0.0 copy-start
  9.1 0.9 copy-done
  10.0 0.0 copy-start.2
  10.0 0.9 copy-done.2
  10.9 0.0 copy-start.3
  10.9 0.8 copy-done.3
  11.8 0.0 collective-permute-done.zl
  11.8 0.0 collective-permute-done.1.zr
  11.8 0.1 shard_map.69
  11.9 14.5 %collective-permute-start.3 = (f32[7,10,16,128]{3,2,1,0:T(8,128)S(1)}, f32[7,10,16,128]{3,2,1,0:T(8,128)S(1)}, u32[]{:S(2)}, u32[]{:S(2)}) collective-permute-start(f32[7,10,16,128]{3,2,1,0:T(8,128)S(1)} %get-tuple-element.34.x0), channel_id=1, source_target_pairs={{0,64},{4,708},{64,128},{68,4},{128,192},{132,68},{192,256},{196,1... | collective-permute-start | bytes 1720328 | tf_op jit(solution)/shard_map/ppermute | solution.py:475
  26.4 1.9 %collective-permute-start.2 = (f32[7,10,16,128]{3,2,1,0:T(8,128)S(1)}, f32[7,10,16,128]{3,2,1,0:T(8,128)S(1)}, u32[]{:S(2)}, u32[]{:S(2)}) collective-permute-start(f32[7,10,16,128]{3,2,1,0:T(8,128)S(1)} %get-tuple-element.34.x0), channel_id=1, source_target_pairs={{0,704},{4,68},{64,0},{68,132},{128,64},{132,196},{192,128},{196,2... | collective-permute-start | bytes 1720328 | tf_op jit(solution)/shard_map/ppermute | solution.py:475
  28.3 2.7 %collective-permute-start.4 = (f32[7,10,8,128]{3,2,1,0:T(8,128)S(1)}, f32[7,10,8,128]{3,2,1,0:T(8,128)S(1)}, u32[]{:S(2)}, u32[]{:S(2)}) collective-permute-start(f32[7,10,8,128]{3,2,1,0:T(8,128)S(1)} %get-tuple-element.35), channel_id=1, source_target_pairs={{0,4},{4,8},{8,12},{12,16},{16,20},{20,24},{24,28},{28,32},{32,36}... | collective-permute-start | bytes 860168 | tf_op jit(solution)/shard_map/ppermute | solution.py:451
  31.0 0.0 collective-permute-start.5
  31.0 3.6 %collective-permute-done.4.lower0 = f32[7,10,8,128]{3,2,1,0:T(8,128)S(1)} collective-permute-done((f32[7,10,8,128]{3,2,1,0:T(8,128)S(1)}, f32[7,10,8,128]{3,2,1,0:T(8,128)S(1)}, u32[]{:S(2)}, u32[]{:S(2)}) %collective-permute-start.4) | collective-permute-done | bytes 286752 | tf_op jit(solution)/shard_map/ppermute | solution.py:451
  34.6 2.8 %collective-permute-done.5.upper0 = f32[7,10,8,128]{3,2,1,0:T(8,128)S(1)} collective-permute-done((f32[7,10,8,128]{3,2,1,0:T(8,128)S(1)}, f32[7,10,8,128]{3,2,1,0:T(8,128)S(1)}, u32[]{:S(2)}, u32[]{:S(2)}) %collective-permute-start.5) | collective-permute-done | bytes 286752 | tf_op jit(solution)/shard_map/ppermute | solution.py:451
  37.4 0.0 collective-permute-done.3.xb
  37.4 3.6 %collective-permute-done.2.xa = f32[7,10,16,128]{3,2,1,0:T(8,128)S(1)} collective-permute-done((f32[7,10,16,128]{3,2,1,0:T(8,128)S(1)}, f32[7,10,16,128]{3,2,1,0:T(8,128)S(1)}, u32[]{:S(2)}, u32[]{:S(2)}) %collective-permute-start.2) | collective-permute-done | bytes 573472 | tf_op jit(solution)/shard_map/ppermute | solution.py:475
  41.0 0.1 shard_map.70
  41.1 0.0 collective-permute-start.6
  41.2 0.5 collective-permute-start.7
  41.7 4.9 %collective-permute-done.6.lower = f32[7,16,8,128]{3,2,1,0:T(8,128)S(1)} collective-permute-done((f32[7,16,8,128]{3,2,1,0:T(8,128)S(1)}, f32[7,16,8,128]{3,2,1,0:T(8,128)S(1)}, u32[]{:S(2)}, u32[]{:S(2)}) %collective-permute-start.6) | collective-permute-done | bytes 458784 | tf_op jit(solution)/shard_map/ppermute | solution.py:451
  46.6 2.8 %collective-permute-done.7.upper = f32[7,16,8,128]{3,2,1,0:T(8,128)S(1)} collective-permute-done((f32[7,16,8,128]{3,2,1,0:T(8,128)S(1)}, f32[7,16,8,128]{3,2,1,0:T(8,128)S(1)}, u32[]{:S(2)}, u32[]{:S(2)}) %collective-permute-start.7) | collective-permute-done | bytes 458784 | tf_op jit(solution)/shard_map/ppermute | solution.py:451
  49.4 6.5 %shard_map.71 = (f32[7,24,32,256]{3,2,1,0:T(8,128)S(1)}, f32[24,32,256]{2,1,0:T(8,128)S(1)}, f32[24,32,256]{2,1,0:T(8,128)S(1)}, f32[24,32,256]{2,1,0:T(8,128)S(...) custom-call(f32[7,10,16,128]{3,2,1,0:T(8,128)S(1)} %get-tuple-elemen, ...), custom_call_target="tpu_custom_call" | custom-call | tf_op jit(solution)/shard_map/pallas_call | solution.py:492
  55.9 0.0 copy-start.1
  55.9 0.0 copy-start.4
  55.9 2.1 %collective-permute-start.8 = (f32[2,3,8,256]{3,2,1,0:T(8,128)S(1)}, f32[2,3,8,256]{3,2,1,0:T(8,128)S(1)}, u32[]{:S(2)}, u32[]{:S(2)}) collective-permute-start(f32[2,3,8,256]{3,2,1,0:T(8,128)S(1)} %get-tuple-element.43), channel_id=1, source_target_pairs={{0,704},{4,68},{64,0},{68,132},{128,64},{132,196},{192,128},{196,2... | collective-permute-start | bytes 147464 | tf_op jit(solution)/shard_map/ppermute | solution.py:475
  58.0 4.8 %collective-permute-start.9 = (f32[2,3,8,256]{3,2,1,0:T(8,128)S(1)}, f32[2,3,8,256]{3,2,1,0:T(8,128)S(1)}, u32[]{:S(2)}, u32[]{:S(2)}) collective-permute-start(f32[2,3,8,256]{3,2,1,0:T(8,128)S(1)} %get-tuple-element.45), channel_id=1, source_target_pairs={{0,64},{4,708},{64,128},{68,4},{128,192},{132,68},{192,256},{196,1... | collective-permute-start | bytes 147464 | tf_op jit(solution)/shard_map/ppermute | solution.py:475
  62.8 0.0 collective-permute-done.8.xa
  62.8 1.1 %collective-permute-done.9.xb = f32[2,3,8,256]{3,2,1,0:T(8,128)S(1)} collective-permute-done((f32[2,3,8,256]{3,2,1,0:T(8,128)S(1)}, f32[2,3,8,256]{3,2,1,0:T(8,128)S(1)}, u32[]{:S(2)}, u32[]{:S(2)}) %collective-permute-start.9) | collective-permute-done | bytes 49184 | tf_op jit(solution)/shard_map/ppermute | solution.py:475
  64.0 4.4 %collective-permute-start.10 = (f32[2,3,8,256]{3,2,1,0:T(8,128)S(1)}, f32[2,3,8,256]{3,2,1,0:T(8,128)S(1)}, u32[]{:S(2)}, u32[]{:S(2)}) collective-permute-start(f32[2,3,8,256]{3,2,1,0:T(8,128)S(1)} %get-tuple-element.46), channel_id=1, source_target_pairs={{0,4},{4,8},{8,12},{12,16},{16,20},{20,24},{24,28},{28,32},{32,36}... | collective-permute-start | bytes 147464 | tf_op jit(solution)/shard_map/ppermute | solution.py:451
  68.4 0.4 collective-permute-start.11
  68.8 0.8 collective-permute-done.10.yl
  69.6 2.3 %collective-permute-done.11.yr = f32[2,3,8,256]{3,2,1,0:T(8,128)S(1)} collective-permute-done((f32[2,3,8,256]{3,2,1,0:T(8,128)S(1)}, f32[2,3,8,256]{3,2,1,0:T(8,128)S(1)}, u32[]{:S(2)}, u32[]{:S(2)}) %collective-permute-start.11) | collective-permute-done | bytes 49184 | tf_op jit(solution)/shard_map/ppermute | solution.py:451
  71.9 3.4 %shard_map.73 = (f32[3,8,16,128]{3,2,1,0:T(8,128)}, f32[3,8,16,128]{3,2,1,0:T(8,128)S(1)}, f32[2,128]{1,0:T(2,128)S(1)}) custom-call(f32[2,3,8,256]{3,2,1,0:T(8,128)S(1)} %collective-permute-done.8.xa, f32[2,2,8,256]{3,2,1,0:T(8,128)S(1)} %get-tuple-element.44.own, f32[2,3,8,256]{3,2,1,0:T(8,128)S(1)} %collective-permute-done.9.xb, ...), custom_call_target="tpu_custom_call" | custom-call | tf_op jit(solution)/shard_map/pallas_call | solution.py:497
  75.4 19.3 %all_to_all.10 = f32[32,2,128]{2,1,0:T(2,128)S(1)} all-to-all(f32[32,2,128]{2,1,0:T(2,128)S(1)} %broadcast_in_dim.4), channel_id=1, replica_groups=mesh['gx'=12,'gc'=8,'co'=2,'gz'=4] {'gc','gz'}, dimensions={0} | all-to-all | bytes 65536 | tf_op jit(solution)/shard_map/all_to_all | solution.py:442
  94.7 14.0 %all_to_all.11 = f32[24,2,128]{2,1,0:T(2,128)S(1)} all-to-all(f32[24,2,128]{2,1,0:T(2,128)S(1)} %broadcast_in_dim.5), channel_id=1, replica_groups=mesh['gx'=12,'gc'=8,'co'=2,'gz'=4] {'gx','co'}, dimensions={0} | all-to-all | bytes 49152 | tf_op jit(solution)/shard_map/all_to_all | solution.py:442
  108.7 0.0 copy-done.1
  108.8 0.0 copy-done.4
  108.8 1.7 %multiply_subtract_fusion = (f32[3,8,16,128]{3,2,1,0:T(8,128)}, f32[3,8,16,128]{3,2,1,0:T(8,128)}) fusion(f32[3,8,16,128]{3,2,1,0:T(8,128)S(1)} %copy-done.1, f32[3,8,16,128]{3,2,1,0:T(8,128)S(1)} %get-tuple-element.60, f32[128]{0:T(128)S(1)} %fusion, f32[3,8,16,128]{3,2,1,0:T(8,128)S(1)} %copy-done.4, f32[3,8,16,128]{3,2,1,0:T(8,128)} %get-tuple-element.31), kind=kLoop, calls=%fused_computation | loop fusion | flops 196608 | bytes 1180160 | tf_op jit(solution)/shard_map/sub | solution.py:506
  (7 shorter events, 0.2 us)
Async XLA Ops:
  1.9 9.9 %collective-permute-start = (f32[7,16,128]{2,1,0:T(8,128)S(1)}, f32[7,16,128]{2,1,0:T(8,128)S(1)}, u32[]{:S(2)}, u32[]{:S(2)}) collective-permute-start(f32[7,16,128]{2,1,0:T(8,128)S(1)} %get-tuple-element.32), channel_id=1, source_target_pairs={{0,1},{1,2},{2,3},{3,0},{4,5},{5,6},{6,7},{7,4},{8,9},{9,10},{10,1... | collective-permute-start | bytes 172040 | tf_op jit(solution)/shard_map/ppermute | solution.py:451
  5.9 5.9 %collective-permute-start.1 = (f32[7,16,128]{2,1,0:T(8,128)S(1)}, f32[7,16,128]{2,1,0:T(8,128)S(1)}, u32[]{:S(2)}, u32[]{:S(2)}) collective-permute-start(f32[7,16,128]{2,1,0:T(8,128)S(1)} %get-tuple-element.33), channel_id=1, source_target_pairs={{0,3},{1,0},{2,1},{3,2},{4,7},{5,4},{6,5},{7,6},{8,11},{9,8},{10,9... | collective-permute-start | bytes 172040 | tf_op jit(solution)/shard_map/ppermute | solution.py:451
  9.1 0.9 copy-start
  10.0 0.9 copy-start.2
  10.9 0.8 copy-start.3
  11.9 25.5 %collective-permute-start.3 = (f32[7,10,16,128]{3,2,1,0:T(8,128)S(1)}, f32[7,10,16,128]{3,2,1,0:T(8,128)S(1)}, u32[]{:S(2)}, u32[]{:S(2)}) collective-permute-start(f32[7,10,16,128]{3,2,1,0:T(8,128)S(1)} %get-tuple-element.34.x0), channel_id=1, source_target_pairs={{0,64},{4,708},{64,128},{68,4},{128,192},{132,68},{192,256},{196,1... | collective-permute-start | bytes 1720328 | tf_op jit(solution)/shard_map/ppermute | solution.py:475
  26.4 14.6 %collective-permute-start.2 = (f32[7,10,16,128]{3,2,1,0:T(8,128)S(1)}, f32[7,10,16,128]{3,2,1,0:T(8,128)S(1)}, u32[]{:S(2)}, u32[]{:S(2)}) collective-permute-start(f32[7,10,16,128]{3,2,1,0:T(8,128)S(1)} %get-tuple-element.34.x0), channel_id=1, source_target_pairs={{0,704},{4,68},{64,0},{68,132},{128,64},{132,196},{192,128},{196,2... | collective-permute-start | bytes 1720328 | tf_op jit(solution)/shard_map/ppermute | solution.py:475
  28.3 6.3 %collective-permute-start.4 = (f32[7,10,8,128]{3,2,1,0:T(8,128)S(1)}, f32[7,10,8,128]{3,2,1,0:T(8,128)S(1)}, u32[]{:S(2)}, u32[]{:S(2)}) collective-permute-start(f32[7,10,8,128]{3,2,1,0:T(8,128)S(1)} %get-tuple-element.35), channel_id=1, source_target_pairs={{0,4},{4,8},{8,12},{12,16},{16,20},{20,24},{24,28},{28,32},{32,36}... | collective-permute-start | bytes 860168 | tf_op jit(solution)/shard_map/ppermute | solution.py:451
  31.0 6.4 %collective-permute-start.5 = (f32[7,10,8,128]{3,2,1,0:T(8,128)S(1)}, f32[7,10,8,128]{3,2,1,0:T(8,128)S(1)}, u32[]{:S(2)}, u32[]{:S(2)}) collective-permute-start(f32[7,10,8,128]{3,2,1,0:T(8,128)S(1)} %get-tuple-element.36), channel_id=1, source_target_pairs={{0,60},{4,0},{8,4},{12,8},{16,12},{20,16},{24,20},{28,24},{32,28},... | collective-permute-start | bytes 860168 | tf_op jit(solution)/shard_map/ppermute | solution.py:451
  41.1 5.4 %collective-permute-start.6 = (f32[7,16,8,128]{3,2,1,0:T(8,128)S(1)}, f32[7,16,8,128]{3,2,1,0:T(8,128)S(1)}, u32[]{:S(2)}, u32[]{:S(2)}) collective-permute-start(f32[7,16,8,128]{3,2,1,0:T(8,128)S(1)} %get-tuple-element.41), channel_id=1, source_target_pairs={{0,4},{4,8},{8,12},{12,16},{16,20},{20,24},{24,28},{28,32},{32,36}... | collective-permute-start | bytes 1376264 | tf_op jit(solution)/shard_map/ppermute | solution.py:451
  41.2 8.2 %collective-permute-start.7 = (f32[7,16,8,128]{3,2,1,0:T(8,128)S(1)}, f32[7,16,8,128]{3,2,1,0:T(8,128)S(1)}, u32[]{:S(2)}, u32[]{:S(2)}) collective-permute-start(f32[7,16,8,128]{3,2,1,0:T(8,128)S(1)} %get-tuple-element.42), channel_id=1, source_target_pairs={{0,60},{4,0},{8,4},{12,8},{16,12},{20,16},{24,20},{28,24},{32,28},... | collective-permute-start | bytes 1376264 | tf_op jit(solution)/shard_map/ppermute | solution.py:451
  55.9 52.9 %copy-start.1 = (f32[3,8,16,128]{3,2,1,0:T(8,128)S(1)}, f32[3,8,16,128]{3,2,1,0:T(8,128)}, u32[]{:S(2)}) copy-start(f32[3,8,16,128]{3,2,1,0:T(8,128)} %residual_in.1) | copy-start | bytes 589828
  55.9 52.8 %copy-start.4 = (f32[3,8,16,128]{3,2,1,0:T(8,128)S(1)}, f32[3,8,16,128]{3,2,1,0:T(8,128)}, u32[]{:S(2)}) copy-start(f32[3,8,16,128]{3,2,1,0:T(8,128)} %param.4) | copy-start | bytes 589828
  55.9 6.8 %collective-permute-start.8 = (f32[2,3,8,256]{3,2,1,0:T(8,128)S(1)}, f32[2,3,8,256]{3,2,1,0:T(8,128)S(1)}, u32[]{:S(2)}, u32[]{:S(2)}) collective-permute-start(f32[2,3,8,256]{3,2,1,0:T(8,128)S(1)} %get-tuple-element.43), channel_id=1, source_target_pairs={{0,704},{4,68},{64,0},{68,132},{128,64},{132,196},{192,128},{196,2... | collective-permute-start | bytes 147464 | tf_op jit(solution)/shard_map/ppermute | solution.py:475
  58.0 5.9 %collective-permute-start.9 = (f32[2,3,8,256]{3,2,1,0:T(8,128)S(1)}, f32[2,3,8,256]{3,2,1,0:T(8,128)S(1)}, u32[]{:S(2)}, u32[]{:S(2)}) collective-permute-start(f32[2,3,8,256]{3,2,1,0:T(8,128)S(1)} %get-tuple-element.45), channel_id=1, source_target_pairs={{0,64},{4,708},{64,128},{68,4},{128,192},{132,68},{192,256},{196,1... | collective-permute-start | bytes 147464 | tf_op jit(solution)/shard_map/ppermute | solution.py:475
  64.0 5.6 %collective-permute-start.10 = (f32[2,3,8,256]{3,2,1,0:T(8,128)S(1)}, f32[2,3,8,256]{3,2,1,0:T(8,128)S(1)}, u32[]{:S(2)}, u32[]{:S(2)}) collective-permute-start(f32[2,3,8,256]{3,2,1,0:T(8,128)S(1)} %get-tuple-element.46), channel_id=1, source_target_pairs={{0,4},{4,8},{8,12},{12,16},{16,20},{20,24},{24,28},{28,32},{32,36}... | collective-permute-start | bytes 147464 | tf_op jit(solution)/shard_map/ppermute | solution.py:451
  68.4 3.5 %collective-permute-start.11 = (f32[2,3,8,256]{3,2,1,0:T(8,128)S(1)}, f32[2,3,8,256]{3,2,1,0:T(8,128)S(1)}, u32[]{:S(2)}, u32[]{:S(2)}) collective-permute-start(f32[2,3,8,256]{3,2,1,0:T(8,128)S(1)} %get-tuple-element.47), channel_id=1, source_target_pairs={{0,60},{4,0},{8,4},{12,8},{16,12},{20,16},{24,20},{28,24},{32,28},... | collective-permute-start | bytes 147464 | tf_op jit(solution)/shard_map/ppermute | solution.py:451

commit v10 on v9

--- a/solution.py
+++ b/solution.py
@@ -22,6 +22,7 @@
 ZH = 16
 MIB = 1024 * 1024
 GYX = CX + 2
+CROSS = CX + 6 * (CX - 1) + 14
 SLAB = 8
 FIELDS = 7
 
@@ -118,12 +119,28 @@
     main[4:7] = 1.0 - fixed[...].astype(F32)
 
 
-def join_kernel(main, zl, zr, brick, up, down):
+def join_kernel(main, zl, zr, brick, up, down, a, b):
     brick[:, 0:CX] = main[...]
     brick[:, CX] = zl[...]
     brick[:, CX + 1] = zr[...]
     up[...] = brick[:, :, 8:16]
     down[...] = brick[:, :, 0:8]
+    for core in range(2):
+        left, right = (b, a) if core else (a, b)
+
+        @pl.when(lax.axis_index("co") == core)
+        def _():
+            for out, near in ((left, 0), (right, 1)):
+                out[0:CX] = main[0]
+                for f in range(1, FIELDS):
+                    out[7 * f + 1 : 7 * f + 8] = main[f, near : near + 7]
+                for f in range(FIELDS):
+                    out[50 + 2 * f] = zl[f]
+                    out[51 + 2 * f] = zr[f]
+
+
+def crossed(f, p, left):
+    return p if f == 0 else 7 * f + 1 + p - left
 
 
 def slab_kernel(xa, xb, up, down):
@@ -132,13 +149,17 @@
 
         @pl.when(lax.axis_index("co") == core)
         def _():
-            for first, brick, near, far in ((0, xl, 4, 0), (SLAB, xr, 0, 4)):
-                for out, row, row4 in ((up, 8, 12), (down, 0, 0)):
-                    out[:, first : first + 4] = brick[:, near : near + 4, row : row + 8]
-                    out[:, first + 4 : first + 6] = brick[:, CX : CX + 2, row : row + 8]
-                    for p in range(4):
-                        at = slice(4 * (p % 2), 4 * (p % 2) + 4)
-                        out[:, first + 6 + p // 2, at] = brick[:, far + p, row4 : row4 + 4]
+            for first, brick, near, far, left in ((0, xl, 4, 0, 1), (SLAB, xr, 0, 4, 0)):
+                for f in range(FIELDS):
+                    k = crossed(f, near, left)
+                    for out, row, row4 in ((up, 8, 12), (down, 0, 0)):
+                        out[f, first : first + 4] = brick[k : k + 4, row : row + 8]
+                        out[f, first + 4 : first + 6] = brick[50 + 2 * f : 52 + 2 * f, row : row + 8]
+                        for p in range(4):
+                            if f and far + p == (0 if left else 7):
+                                continue
+                            at = slice(4 * (p % 2), 4 * (p % 2) + 4)
+                            out[f, first + 6 + p // 2, at] = brick[crossed(f, far + p, left), row4 : row4 + 4]
 
 
 def steps(start, stop, each, body):
@@ -184,13 +205,15 @@
     def assemble(f):
         for p in range(PLANES):
             b, q = p // CX, p % CX
+
             if f and p in (0, PLANES - 1):
                 continue
 
             def mine(at):
                 if b == 1:
                     return x0[f, at]
-                left, right = xb[f, at], xa[f, at]
+                k = 50 + 2 * f + at - CX if at >= CX else crossed(f, at, b == 0)
+                left, right = xb[k], xa[k]
                 return jnp.where(first_core, left, right) if b == 0 else jnp.where(first_core, right, left)
 
             put(f, p, 8, mine(q), mine(CX), mine(CX + 1), block)
@@ -467,8 +490,8 @@
     )(density_bins, residual, fixed_dofs)
     zl, zr = both((to_right, to_left), "gz", nz)
     (main,) = call(main_kernel, [(FIELDS, CX, CY, CZ)], flops=10**9)(density_bins, residual, fixed_dofs)
-    join = call(join_kernel, [brick, slab, slab])(main, zl, zr)
-    x0, up, down = lax.optimization_barrier(tuple(join))
+    join = kernel_call(join_kernel, [brick, slab, slab, (CROSS, CY, CZ), (CROSS, CY, CZ)], 3, limit=8)(main, zl, zr)
+    x0, up, down, a, b = lax.optimization_barrier(tuple(join))
 
     def cross(a, b):
         return tuple(
@@ -476,7 +499,7 @@
             for v, turn in ((a, 1), (b, -1))
         )
 
-    xa, xb = cross(x0, x0)
+    xa, xb = cross(a, b)
     lower0, upper0 = both((up, down), y_axes, ny)
     xa, xb, lower0, upper0 = lax.optimization_barrier((xa, xb, lower0, upper0))
     lower, upper = both(tuple(kernel_call(slab_kernel, [slabs, slabs], 2)(xa, xb)), y_axes, ny)

time: 111 us -> 111 us (level)
  starting transfers between devices: 38.4 us -> 39.7 us
    ppermute x4, starting transfers between devices: 11.1 us -> 12.7 us  [both(): lax.ppermute(up, axes, ring(count, 1))]
    ppermute x4, waiting for transfers between devices: 4.79 us -> 3.57 us  [cross(): lax.ppermute(v, ('gx', 'co'), [(2 * i + c, 2 * ((i + turn * (2 * c - 1))...]
where the time goes in v10:
time: 111 us; the launch traced here: 110 us
  starting transfers between devices  39.7 us (36%)
  blocking collectives  32.7 us (29%)
  waiting for transfers between devices  21.1 us (19%)
  Pallas kernels  11.5 us (10%)
  local copies, waits for them, and re-layouts  2.72 us (2%)
  other arithmetic  1.81 us (2%)
    all_to_all x2, blocking collectives, all_sum(): return lax.all_to_all(sent, axes, 0, 0).sum(axis=0)  32.7 us
    ppermute x4, starting transfers between devices, cross(): lax.ppermute(v, ('gx', 'co'), [(2 * i + c, 2 * ((i + turn * (2 * c - 1))...  23.6 us
    ppermute x4, starting transfers between devices, both(): lax.ppermute(up, axes, ring(count, 1))  12.7 us
    ppermute x4, waiting for transfers between devices, both(): lax.ppermute(up, axes, ring(count, 1))  9.89 us
    ppermute x4, waiting for transfers between devices, both(): lax.ppermute(down, axes, ring(count, -1))  7.59 us
    pallas_call x1, Pallas kernels, shards(): kernel_call(fine_kernel, outs, 7, scratch, 8)  6.53 us
    ppermute x4, waiting for transfers between devices, cross(): lax.ppermute(v, ('gx', 'co'), [(2 * i + c, 2 * ((i + turn * (2 * c - 1))...  3.57 us
    ppermute x4, starting transfers between devices, both(): lax.ppermute(down, axes, ring(count, -1))  3.48 us
  transfers between devices with their start and end apart: 12, of which 8 were waited for; matrix products, arithmetic and copies ran while one was open for 0% of the time, Pallas kernels for 0%

profile of v10, /device:TPU:1, one launch (start us, length us, event | category | flops | bytes accessed | tf_op | source)
XLA Modules:
  0.0 110.3 jit_solution(1984220542177282116)
XLA Ops:
  0.6 1.3 %shard_map.68 = (f32[7,16,128]{2,1,0:T(8,128)S(1)}, f32[7,16,128]{2,1,0:T(8,128)S(1)}) custom-call(s32[8,16,128]{2,1,0:T(8,128)} %density_in.1, f32[3,8,16,128]{3,2,1,0:T(8,128)} %residual_in.1, s32[3,8,16,128]{3,2,1,0:T(8,128)} %fixed_in.1), custom_call_target="tpu_custom_call" | custom-call | tf_op jit(solution)/shard_map/pallas_call | solution.py:478
  1.9 3.9 %collective-permute-start = (f32[7,16,128]{2,1,0:T(8,128)S(1)}, f32[7,16,128]{2,1,0:T(8,128)S(1)}, u32[]{:S(2)}, u32[]{:S(2)}) collective-permute-start(f32[7,16,128]{2,1,0:T(8,128)S(1)} %get-tuple-element.34), channel_id=1, source_target_pairs={{0,1},{1,2},{2,3},{3,0},{4,5},{5,6},{6,7},{7,4},{8,9},{9,10},{10,1... | collective-permute-start | bytes 172040 | tf_op jit(solution)/shard_map/ppermute | solution.py:474
  5.9 3.2 %collective-permute-start.1 = (f32[7,16,128]{2,1,0:T(8,128)S(1)}, f32[7,16,128]{2,1,0:T(8,128)S(1)}, u32[]{:S(2)}, u32[]{:S(2)}) collective-permute-start(f32[7,16,128]{2,1,0:T(8,128)S(1)} %get-tuple-element.35), channel_id=1, source_target_pairs={{0,3},{1,0},{2,1},{3,2},{4,7},{5,4},{6,5},{7,6},{8,11},{9,8},{10,9... | collective-permute-start | bytes 172040 | tf_op jit(solution)/shard_map/ppermute | solution.py:474
  9.1 0.0 copy-start
  9.1 0.9 copy-done
  10.0 0.0 copy-start.2
  10.0 0.9 copy-done.2
  10.9 0.0 copy-start.3
  10.9 0.8 copy-done.3
  11.8 0.0 collective-permute-done.zl
  11.8 0.0 collective-permute-done.1.zr
  11.8 0.1 shard_map.69
  12.0 4.2 %collective-permute-start.2 = (f32[64,16,128]{2,1,0:T(8,128)S(1)}, f32[64,16,128]{2,1,0:T(8,128)S(1)}, u32[]{:S(2)}, u32[]{:S(2)}) collective-permute-start(f32[64,16,128]{2,1,0:T(8,128)S(1)} %get-tuple-element.37), channel_id=1, source_target_pairs={{0,704},{4,68},{64,0},{68,132},{128,64},{132,196},{192,128},{196,2... | collective-permute-start | bytes 1572872 | tf_op jit(solution)/shard_map/ppermute | solution.py:498
  16.2 12.2 %collective-permute-start.3 = (f32[64,16,128]{2,1,0:T(8,128)S(1)}, f32[64,16,128]{2,1,0:T(8,128)S(1)}, u32[]{:S(2)}, u32[]{:S(2)}) collective-permute-start(f32[64,16,128]{2,1,0:T(8,128)S(1)} %get-tuple-element.38), channel_id=1, source_target_pairs={{0,64},{4,708},{64,128},{68,4},{128,192},{132,68},{192,256},{196,1... | collective-permute-start | bytes 1572872 | tf_op jit(solution)/shard_map/ppermute | solution.py:498
  28.4 2.7 %collective-permute-start.4 = (f32[7,10,8,128]{3,2,1,0:T(8,128)S(1)}, f32[7,10,8,128]{3,2,1,0:T(8,128)S(1)}, u32[]{:S(2)}, u32[]{:S(2)}) collective-permute-start(f32[7,10,8,128]{3,2,1,0:T(8,128)S(1)} %get-tuple-element.39), channel_id=1, source_target_pairs={{0,4},{4,8},{8,12},{12,16},{16,20},{20,24},{24,28},{28,32},{32,36}... | collective-permute-start | bytes 860168 | tf_op jit(solution)/shard_map/ppermute | solution.py:474
  31.1 0.0 collective-permute-start.5
  31.1 3.6 %collective-permute-done.4.lower0 = f32[7,10,8,128]{3,2,1,0:T(8,128)S(1)} collective-permute-done((f32[7,10,8,128]{3,2,1,0:T(8,128)S(1)}, f32[7,10,8,128]{3,2,1,0:T(8,128)S(1)}, u32[]{:S(2)}, u32[]{:S(2)}) %collective-permute-start.4) | collective-permute-done | bytes 286752 | tf_op jit(solution)/shard_map/ppermute | solution.py:474
  34.7 2.8 %collective-permute-done.5.upper0 = f32[7,10,8,128]{3,2,1,0:T(8,128)S(1)} collective-permute-done((f32[7,10,8,128]{3,2,1,0:T(8,128)S(1)}, f32[7,10,8,128]{3,2,1,0:T(8,128)S(1)}, u32[]{:S(2)}, u32[]{:S(2)}) %collective-permute-start.5) | collective-permute-done | bytes 286752 | tf_op jit(solution)/shard_map/ppermute | solution.py:474
  37.5 0.0 collective-permute-done.2.xa
  37.5 2.4 %collective-permute-done.3.xb = f32[64,16,128]{2,1,0:T(8,128)S(1)} collective-permute-done((f32[64,16,128]{2,1,0:T(8,128)S(1)}, f32[64,16,128]{2,1,0:T(8,128)S(1)}, u32[]{:S(2)}, u32[]{:S(2)}) %collective-permute-start.3) | collective-permute-done | bytes 524320 | tf_op jit(solution)/shard_map/ppermute | solution.py:498
  39.9 0.1 shard_map.70
  40.0 1.6 %collective-permute-start.6 = (f32[7,16,8,128]{3,2,1,0:T(8,128)S(1)}, f32[7,16,8,128]{3,2,1,0:T(8,128)S(1)}, u32[]{:S(2)}, u32[]{:S(2)}) collective-permute-start(f32[7,16,8,128]{3,2,1,0:T(8,128)S(1)} %get-tuple-element.45), channel_id=1, source_target_pairs={{0,4},{4,8},{8,12},{12,16},{16,20},{20,24},{24,28},{28,32},{32,36}... | collective-permute-start | bytes 1376264 | tf_op jit(solution)/shard_map/ppermute | solution.py:474
  41.5 0.0 collective-permute-start.7
  41.5 5.4 %collective-permute-done.6.lower = f32[7,16,8,128]{3,2,1,0:T(8,128)S(1)} collective-permute-done((f32[7,16,8,128]{3,2,1,0:T(8,128)S(1)}, f32[7,16,8,128]{3,2,1,0:T(8,128)S(1)}, u32[]{:S(2)}, u32[]{:S(2)}) %collective-permute-start.6) | collective-permute-done | bytes 458784 | tf_op jit(solution)/shard_map/ppermute | solution.py:474
  47.0 2.5 %collective-permute-done.7.upper = f32[7,16,8,128]{3,2,1,0:T(8,128)S(1)} collective-permute-done((f32[7,16,8,128]{3,2,1,0:T(8,128)S(1)}, f32[7,16,8,128]{3,2,1,0:T(8,128)S(1)}, u32[]{:S(2)}, u32[]{:S(2)}) %collective-permute-start.7) | collective-permute-done | bytes 458784 | tf_op jit(solution)/shard_map/ppermute | solution.py:474
  49.5 6.5 %shard_map.71 = (f32[7,24,32,256]{3,2,1,0:T(8,128)S(1)}, f32[24,32,256]{2,1,0:T(8,128)S(1)}, f32[24,32,256]{2,1,0:T(8,128)S(1)}, f32[24,32,256]{2,1,0:T(8,128)S(...) custom-call(f32[7,10,16,128]{3,2,1,0:T(8,128)S(1)} %get-tuple-elemen, ...), custom_call_target="tpu_custom_call" | custom-call | tf_op jit(solution)/shard_map/pallas_call | solution.py:515
  56.0 0.0 copy-start.1
  56.0 0.0 copy-start.4
  56.0 2.1 %collective-permute-start.8 = (f32[2,3,8,256]{3,2,1,0:T(8,128)S(1)}, f32[2,3,8,256]{3,2,1,0:T(8,128)S(1)}, u32[]{:S(2)}, u32[]{:S(2)}) collective-permute-start(f32[2,3,8,256]{3,2,1,0:T(8,128)S(1)} %get-tuple-element.47), channel_id=1, source_target_pairs={{0,704},{4,68},{64,0},{68,132},{128,64},{132,196},{192,128},{196,2... | collective-permute-start | bytes 147464 | tf_op jit(solution)/shard_map/ppermute | solution.py:498
  58.1 5.1 %collective-permute-start.9 = (f32[2,3,8,256]{3,2,1,0:T(8,128)S(1)}, f32[2,3,8,256]{3,2,1,0:T(8,128)S(1)}, u32[]{:S(2)}, u32[]{:S(2)}) collective-permute-start(f32[2,3,8,256]{3,2,1,0:T(8,128)S(1)} %get-tuple-element.49), channel_id=1, source_target_pairs={{0,64},{4,708},{64,128},{68,4},{128,192},{132,68},{192,256},{196,1... | collective-permute-start | bytes 147464 | tf_op jit(solution)/shard_map/ppermute | solution.py:498
  63.2 0.0 collective-permute-done.8.xa
  63.2 1.1 %collective-permute-done.9.xb = f32[2,3,8,256]{3,2,1,0:T(8,128)S(1)} collective-permute-done((f32[2,3,8,256]{3,2,1,0:T(8,128)S(1)}, f32[2,3,8,256]{3,2,1,0:T(8,128)S(1)}, u32[]{:S(2)}, u32[]{:S(2)}) %collective-permute-start.9) | collective-permute-done | bytes 49184 | tf_op jit(solution)/shard_map/ppermute | solution.py:498
  64.4 4.4 %collective-permute-start.10 = (f32[2,3,8,256]{3,2,1,0:T(8,128)S(1)}, f32[2,3,8,256]{3,2,1,0:T(8,128)S(1)}, u32[]{:S(2)}, u32[]{:S(2)}) collective-permute-start(f32[2,3,8,256]{3,2,1,0:T(8,128)S(1)} %get-tuple-element.50), channel_id=1, source_target_pairs={{0,4},{4,8},{8,12},{12,16},{16,20},{20,24},{24,28},{28,32},{32,36}... | collective-permute-start | bytes 147464 | tf_op jit(solution)/shard_map/ppermute | solution.py:474
  68.8 0.3 collective-permute-start.11
  69.1 0.9 collective-permute-done.10.yl
  70.0 2.3 %collective-permute-done.11.yr = f32[2,3,8,256]{3,2,1,0:T(8,128)S(1)} collective-permute-done((f32[2,3,8,256]{3,2,1,0:T(8,128)S(1)}, f32[2,3,8,256]{3,2,1,0:T(8,128)S(1)}, u32[]{:S(2)}, u32[]{:S(2)}) %collective-permute-start.11) | collective-permute-done | bytes 49184 | tf_op jit(solution)/shard_map/ppermute | solution.py:474
  72.3 3.4 %shard_map.73 = (f32[3,8,16,128]{3,2,1,0:T(8,128)}, f32[3,8,16,128]{3,2,1,0:T(8,128)S(1)}, f32[2,128]{1,0:T(2,128)S(1)}) custom-call(f32[2,3,8,256]{3,2,1,0:T(8,128)S(1)} %collective-permute-done.8.xa, f32[2,2,8,256]{3,2,1,0:T(8,128)S(1)} %get-tuple-element.48.own, f32[2,3,8,256]{3,2,1,0:T(8,128)S(1)} %collective-permute-done.9.xb, ...), custom_call_target="tpu_custom_call" | custom-call | tf_op jit(solution)/shard_map/pallas_call | solution.py:520
  75.8 18.9 %all_to_all.10 = f32[32,2,128]{2,1,0:T(2,128)S(1)} all-to-all(f32[32,2,128]{2,1,0:T(2,128)S(1)} %broadcast_in_dim.4), channel_id=1, replica_groups=mesh['gx'=12,'gc'=8,'co'=2,'gz'=4] {'gc','gz'}, dimensions={0} | all-to-all | bytes 65536 | tf_op jit(solution)/shard_map/all_to_all | solution.py:465
  94.7 13.9 %all_to_all.11 = f32[24,2,128]{2,1,0:T(2,128)S(1)} all-to-all(f32[24,2,128]{2,1,0:T(2,128)S(1)} %broadcast_in_dim.5), channel_id=1, replica_groups=mesh['gx'=12,'gc'=8,'co'=2,'gz'=4] {'gx','co'}, dimensions={0} | all-to-all | bytes 49152 | tf_op jit(solution)/shard_map/all_to_all | solution.py:465
  108.6 0.0 copy-done.1
  108.6 0.0 copy-done.4
  108.6 1.7 %multiply_subtract_fusion = (f32[3,8,16,128]{3,2,1,0:T(8,128)}, f32[3,8,16,128]{3,2,1,0:T(8,128)}) fusion(f32[3,8,16,128]{3,2,1,0:T(8,128)S(1)} %copy-done.1, f32[3,8,16,128]{3,2,1,0:T(8,128)S(1)} %get-tuple-element.64, f32[128]{0:T(128)S(1)} %fusion, f32[3,8,16,128]{3,2,1,0:T(8,128)S(1)} %copy-done.4, f32[3,8,16,128]{3,2,1,0:T(8,128)} %get-tuple-element.33), kind=kLoop, calls=%fused_computation | loop fusion | flops 196608 | bytes 1180160 | tf_op jit(solution)/shard_map/sub | solution.py:529
  (7 shorter events, 0.2 us)
Async XLA Ops:
  1.9 9.9 %collective-permute-start = (f32[7,16,128]{2,1,0:T(8,128)S(1)}, f32[7,16,128]{2,1,0:T(8,128)S(1)}, u32[]{:S(2)}, u32[]{:S(2)}) collective-permute-start(f32[7,16,128]{2,1,0:T(8,128)S(1)} %get-tuple-element.34), channel_id=1, source_target_pairs={{0,1},{1,2},{2,3},{3,0},{4,5},{5,6},{6,7},{7,4},{8,9},{9,10},{10,1... | collective-permute-start | bytes 172040 | tf_op jit(solution)/shard_map/ppermute | solution.py:474
  5.9 5.9 %collective-permute-start.1 = (f32[7,16,128]{2,1,0:T(8,128)S(1)}, f32[7,16,128]{2,1,0:T(8,128)S(1)}, u32[]{:S(2)}, u32[]{:S(2)}) collective-permute-start(f32[7,16,128]{2,1,0:T(8,128)S(1)} %get-tuple-element.35), channel_id=1, source_target_pairs={{0,3},{1,0},{2,1},{3,2},{4,7},{5,4},{6,5},{7,6},{8,11},{9,8},{10,9... | collective-permute-start | bytes 172040 | tf_op jit(solution)/shard_map/ppermute | solution.py:474
  9.1 0.9 copy-start
  10.0 0.9 copy-start.2
  10.9 0.8 copy-start.3
  12.0 25.5 %collective-permute-start.2 = (f32[64,16,128]{2,1,0:T(8,128)S(1)}, f32[64,16,128]{2,1,0:T(8,128)S(1)}, u32[]{:S(2)}, u32[]{:S(2)}) collective-permute-start(f32[64,16,128]{2,1,0:T(8,128)S(1)} %get-tuple-element.37), channel_id=1, source_target_pairs={{0,704},{4,68},{64,0},{68,132},{128,64},{132,196},{192,128},{196,2... | collective-permute-start | bytes 1572872 | tf_op jit(solution)/shard_map/ppermute | solution.py:498
  16.2 23.7 %collective-permute-start.3 = (f32[64,16,128]{2,1,0:T(8,128)S(1)}, f32[64,16,128]{2,1,0:T(8,128)S(1)}, u32[]{:S(2)}, u32[]{:S(2)}) collective-permute-start(f32[64,16,128]{2,1,0:T(8,128)S(1)} %get-tuple-element.38), channel_id=1, source_target_pairs={{0,64},{4,708},{64,128},{68,4},{128,192},{132,68},{192,256},{196,1... | collective-permute-start | bytes 1572872 | tf_op jit(solution)/shard_map/ppermute | solution.py:498
  28.4 6.3 %collective-permute-start.4 = (f32[7,10,8,128]{3,2,1,0:T(8,128)S(1)}, f32[7,10,8,128]{3,2,1,0:T(8,128)S(1)}, u32[]{:S(2)}, u32[]{:S(2)}) collective-permute-start(f32[7,10,8,128]{3,2,1,0:T(8,128)S(1)} %get-tuple-element.39), channel_id=1, source_target_pairs={{0,4},{4,8},{8,12},{12,16},{16,20},{20,24},{24,28},{28,32},{32,36}... | collective-permute-start | bytes 860168 | tf_op jit(solution)/shard_map/ppermute | solution.py:474
  31.1 6.4 %collective-permute-start.5 = (f32[7,10,8,128]{3,2,1,0:T(8,128)S(1)}, f32[7,10,8,128]{3,2,1,0:T(8,128)S(1)}, u32[]{:S(2)}, u32[]{:S(2)}) collective-permute-start(f32[7,10,8,128]{3,2,1,0:T(8,128)S(1)} %get-tuple-element.40), channel_id=1, source_target_pairs={{0,60},{4,0},{8,4},{12,8},{16,12},{20,16},{24,20},{28,24},{32,28},... | collective-permute-start | bytes 860168 | tf_op jit(solution)/shard_map/ppermute | solution.py:474
  40.0 7.0 %collective-permute-start.6 = (f32[7,16,8,128]{3,2,1,0:T(8,128)S(1)}, f32[7,16,8,128]{3,2,1,0:T(8,128)S(1)}, u32[]{:S(2)}, u32[]{:S(2)}) collective-permute-start(f32[7,16,8,128]{3,2,1,0:T(8,128)S(1)} %get-tuple-element.45), channel_id=1, source_target_pairs={{0,4},{4,8},{8,12},{12,16},{16,20},{20,24},{24,28},{28,32},{32,36}... | collective-permute-start | bytes 1376264 | tf_op jit(solution)/shard_map/ppermute | solution.py:474
  41.5 7.9 %collective-permute-start.7 = (f32[7,16,8,128]{3,2,1,0:T(8,128)S(1)}, f32[7,16,8,128]{3,2,1,0:T(8,128)S(1)}, u32[]{:S(2)}, u32[]{:S(2)}) collective-permute-start(f32[7,16,8,128]{3,2,1,0:T(8,128)S(1)} %get-tuple-element.46), channel_id=1, source_target_pairs={{0,60},{4,0},{8,4},{12,8},{16,12},{20,16},{24,20},{28,24},{32,28},... | collective-permute-start | bytes 1376264 | tf_op jit(solution)/shard_map/ppermute | solution.py:474
  56.0 52.6 %copy-start.1 = (f32[3,8,16,128]{3,2,1,0:T(8,128)S(1)}, f32[3,8,16,128]{3,2,1,0:T(8,128)}, u32[]{:S(2)}) copy-start(f32[3,8,16,128]{3,2,1,0:T(8,128)} %residual_in.1) | copy-start | bytes 589828
  56.0 52.6 %copy-start.4 = (f32[3,8,16,128]{3,2,1,0:T(8,128)S(1)}, f32[3,8,16,128]{3,2,1,0:T(8,128)}, u32[]{:S(2)}) copy-start(f32[3,8,16,128]{3,2,1,0:T(8,128)} %param.4) | copy-start | bytes 589828
  56.0 7.2 %collective-permute-start.8 = (f32[2,3,8,256]{3,2,1,0:T(8,128)S(1)}, f32[2,3,8,256]{3,2,1,0:T(8,128)S(1)}, u32[]{:S(2)}, u32[]{:S(2)}) collective-permute-start(f32[2,3,8,256]{3,2,1,0:T(8,128)S(1)} %get-tuple-element.47), channel_id=1, source_target_pairs={{0,704},{4,68},{64,0},{68,132},{128,64},{132,196},{192,128},{196,2... | collective-permute-start | bytes 147464 | tf_op jit(solution)/shard_map/ppermute | solution.py:498
  58.1 6.3 %collective-permute-start.9 = (f32[2,3,8,256]{3,2,1,0:T(8,128)S(1)}, f32[2,3,8,256]{3,2,1,0:T(8,128)S(1)}, u32[]{:S(2)}, u32[]{:S(2)}) collective-permute-start(f32[2,3,8,256]{3,2,1,0:T(8,128)S(1)} %get-tuple-element.49), channel_id=1, source_target_pairs={{0,64},{4,708},{64,128},{68,4},{128,192},{132,68},{192,256},{196,1... | collective-permute-start | bytes 147464 | tf_op jit(solution)/shard_map/ppermute | solution.py:498
  64.4 5.6 %collective-permute-start.10 = (f32[2,3,8,256]{3,2,1,0:T(8,128)S(1)}, f32[2,3,8,256]{3,2,1,0:T(8,128)S(1)}, u32[]{:S(2)}, u32[]{:S(2)}) collective-permute-start(f32[2,3,8,256]{3,2,1,0:T(8,128)S(1)} %get-tuple-element.50), channel_id=1, source_target_pairs={{0,4},{4,8},{8,12},{12,16},{16,20},{20,24},{24,28},{28,32},{32,36}... | collective-permute-start | bytes 147464 | tf_op jit(solution)/shard_map/ppermute | solution.py:474
  68.8 3.5 %collective-permute-start.11 = (f32[2,3,8,256]{3,2,1,0:T(8,128)S(1)}, f32[2,3,8,256]{3,2,1,0:T(8,128)S(1)}, u32[]{:S(2)}, u32[]{:S(2)}) collective-permute-start(f32[2,3,8,256]{3,2,1,0:T(8,128)S(1)} %get-tuple-element.51), channel_id=1, source_target_pairs={{0,60},{4,0},{8,4},{12,8},{16,12},{20,16},{24,20},{28,24},{32,28},... | collective-permute-start | bytes 147464 | tf_op jit(solution)/shard_map/ppermute | solution.py:474
